TPU v7x, 32 devices: a whole 2x2x4 slice. The times are simulated.
32 devices in a mesh: tm: 4 (over y, core), patch: 8 (over z, x).
Axes of the slice: x: 2, y: 2, z: 4, core: 2. Of those that a mesh axis runs over, the one named last changes fastest.
Arguments:
- query_vectors: bfloat16 [16, 4, 64, 2048], P(None, 'tm', 'patch'), may hold values from -32 to 32
- key_vectors: bfloat16 [16, 4, 64, 2048], P(None, 'tm', 'patch'), may hold values from -32 to 32
- value_vectors: bfloat16 [16, 4, 64, 2048], P(None, 'tm', 'patch'), may hold values from -6 to 6
- grad_output: bfloat16 [16, 4, 64, 2048], P(None, 'tm', 'patch'), may hold values from -6 to 6
- time_bias: float32 [16, 4], replicated, may hold values from -26 to 2
Outputs:
- grad_queries: bfloat16 [16, 4, 64, 2048], P(None, 'tm', 'patch')
- grad_keys: bfloat16 [16, 4, 64, 2048], P(None, 'tm', 'patch')
- grad_values: bfloat16 [16, 4, 64, 2048], P(None, 'tm', 'patch')
- grad_bias: float32 [16, 4], replicated
All inputs are finite; a program needn't handle non-finite values.
Results may differ from a plain program's by a relative error of at most 0.0069.
Values may be sent and summed in bfloat16 or wider, within the bound.
No kernel may reach another device: no remote copies, remote signals or barrier semaphores. Data moves between devices by JAX's collectives and lax.ppermute only.
A program may use at most 64 MiB of HBM per device.

v0:
```python
import math

import jax
import jax.numpy as jnp
from jax import lax
from jax.sharding import PartitionSpec as P


def score_table(bias_rows, frames):
    steps = jnp.arange(frames, dtype=jnp.int32)
    offsets = steps[:, None] - steps[None, :]
    onehot = (offsets[:, :, None] == steps[None, None, :]).astype(jnp.float32)
    table = jnp.einsum("hd,tud->htu", bias_rows, onehot, precision=lax.Precision.HIGHEST)
    return (table, offsets >= 0, onehot)


def attend_back(query_heads, key_heads, value_heads, grad_heads, bias_rows):
    frames = query_heads.shape[1]
    score_scale = 1.0 / math.sqrt(query_heads.shape[4])
    table, causal, onehot = score_table(bias_rows, frames)
    scores = (
        jnp.einsum("atxhd,auxhd->axhtu", query_heads, key_heads, preferred_element_type=jnp.float32)
        * score_scale
        + table[None, None]
    )
    scores = jnp.where(causal, scores, -jnp.inf)
    row_max = jnp.max(scores, axis=-1, keepdims=True)
    expon = jnp.exp(scores - row_max)
    weights = expon / jnp.sum(expon, axis=-1, keepdims=True)
    weights_low = weights.astype(jnp.bfloat16)
    attended = jnp.einsum(
        "axhtu,auxhd->atxhd", weights_low, value_heads, preferred_element_type=jnp.float32
    )
    rowdot = jnp.einsum(
        "atxhd,atxhd->axht", grad_heads, attended, preferred_element_type=jnp.float32
    )
    grad_weights = jnp.einsum(
        "atxhd,auxhd->axhtu", grad_heads, value_heads, preferred_element_type=jnp.float32
    )
    grad_scores = weights * (grad_weights - rowdot[..., None])
    bias_terms = jnp.einsum("axhtu,tud->axhd", grad_scores, onehot, precision=lax.Precision.HIGHEST)
    grad_low = grad_scores.astype(jnp.bfloat16)
    grad_query = (
        jnp.einsum("axhtu,auxhd->atxhd", grad_low, key_heads, preferred_element_type=jnp.float32)
        * score_scale
    ).astype(jnp.bfloat16)
    grad_key = (
        jnp.einsum("axhtu,atxhd->auxhd", grad_low, query_heads, preferred_element_type=jnp.float32)
        * score_scale
    ).astype(jnp.bfloat16)
    grad_value = jnp.einsum(
        "axhtu,atxhd->auxhd", weights_low, grad_heads, preferred_element_type=jnp.float32
    ).astype(jnp.bfloat16)
    return (grad_query, grad_key, grad_value, bias_terms)


def per_device(query_vectors, key_vectors, value_vectors, grad_output, time_bias):
    head_count = time_bias.shape[0]
    frames = time_bias.shape[1]
    head_dim = query_vectors.shape[3] // head_count
    split_shape = query_vectors.shape[:3] + (head_count, head_dim)
    query_heads = query_vectors.reshape(split_shape)
    key_heads = key_vectors.reshape(split_shape)
    value_heads = value_vectors.reshape(split_shape)
    grad_heads = grad_output.reshape(split_shape)
    local_heads = head_count // lax.axis_size("tm")
    first_head = lax.axis_index("tm") * local_heads
    bias_rows = lax.dynamic_slice_in_dim(time_bias, first_head, local_heads, 0)
    grad_query, grad_key, grad_value, bias_terms = attend_back(
        lax.all_to_all(query_heads, "tm", split_axis=3, concat_axis=1, tiled=True),
        lax.all_to_all(key_heads, "tm", split_axis=3, concat_axis=1, tiled=True),
        lax.all_to_all(value_heads, "tm", split_axis=3, concat_axis=1, tiled=True),
        lax.all_to_all(grad_heads, "tm", split_axis=3, concat_axis=1, tiled=True),
        bias_rows,
    )
    grad_query, grad_key, grad_value, bias_terms = (
        lax.all_to_all(grad_query, "tm", split_axis=1, concat_axis=3, tiled=True),
        lax.all_to_all(grad_key, "tm", split_axis=1, concat_axis=3, tiled=True),
        lax.all_to_all(grad_value, "tm", split_axis=1, concat_axis=3, tiled=True),
        jnp.sum(bias_terms, axis=1),
    )
    partial_value = jnp.sum(bias_terms, axis=0)
    partial_full = lax.dynamic_update_slice_in_dim(
        jnp.zeros((head_count, frames), jnp.float32), partial_value, first_head, 0
    )
    bias_total = lax.psum(partial_full, ("tm", "patch"))
    return (
        grad_query.reshape(query_vectors.shape),
        grad_key.reshape(query_vectors.shape),
        grad_value.reshape(query_vectors.shape),
        bias_total,
    )


def solution(mesh):
    placed = (
        P(None, "tm", "patch", None),
        P(None, "tm", "patch", None),
        P(None, "tm", "patch", None),
        P(None, "tm", "patch", None),
        P(),
    )
    return jax.shard_map(
        per_device,
        mesh=mesh,
        in_specs=placed,
        out_specs=(
            P(None, "tm", "patch", None),
            P(None, "tm", "patch", None),
            P(None, "tm", "patch", None),
            P(),
        ),
        check_vma=False,
    )
```

profile of v0, /device:TPU:0, one launch (start us, length us, event | category | flops | bytes accessed | tf_op | source)
XLA Modules:
  0.0 138.2 jit_solution(17004518652829236400)
XLA Ops:
  0.6 0.0 copy-start
  0.6 1.2 copy.184
  1.8 0.9 copy.102
  2.7 0.0 copy-start.1
  2.7 4.4 %all-to-all-start.3 = ((bf16[16,1,8,16,128]{4,2,0,1,3:T(8,128)(2,1)}), bf16[16,1,8,16,128]{4,2,0,1,3:T(8,128)(2,1)S(1)}, u32[]{:S(2)}, u32[]{:S(2)}) async-start(bf16[16,1,8,16,128]{4,2,0,1,3:T(8,128)(2,1)} %copy.102), calls=%async_computation.3 | async-start | bytes 1048576 | tf_op jit(solution)/shard_map/all_to_all | solution.py:72
  7.1 0.0 copy-done.1
  7.1 0.1 copy.185
  7.2 0.9 copy.99
  8.2 0.0 copy-start.2
  8.2 7.8 %all-to-all-done.3 = bf16[16,1,8,16,128]{4,2,0,1,3:T(8,128)(2,1)S(1)} async-done(((bf16[16,1,8,16,128]{4,2,0,1,3:T(8,128)(2,1)}), bf16[16,1,8,16,128]{4,2,0,1,3:T(8,128)(2,1)S(1)}, u32[]{:S(2)}, u32[]{:S(2)}) %all-to-all-start.3) | async-done | bytes 524320 | tf_op jit(solution)/shard_map/all_to_all | solution.py:72
  16.0 3.5 %all-to-all-start.2 = ((bf16[16,1,8,16,128]{4,2,0,1,3:T(8,128)(2,1)}), bf16[16,1,8,16,128]{4,2,0,1,3:T(8,128)(2,1)S(1)}, u32[]{:S(2)}, u32[]{:S(2)}) async-start(bf16[16,1,8,16,128]{4,2,0,1,3:T(8,128)(2,1)} %copy.99), calls=%async_computation.2 | async-start | bytes 1048576 | tf_op jit(solution)/shard_map/all_to_all | solution.py:73
  19.4 0.0 copy-done.2
  19.4 0.1 copy.186
  19.6 0.9 copy.92
  20.5 0.0 copy-start.3
  20.5 7.7 %all-to-all-done.2 = bf16[16,1,8,16,128]{4,2,0,1,3:T(8,128)(2,1)S(1)} async-done(((bf16[16,1,8,16,128]{4,2,0,1,3:T(8,128)(2,1)}), bf16[16,1,8,16,128]{4,2,0,1,3:T(8,128)(2,1)S(1)}, u32[]{:S(2)}, u32[]{:S(2)}) %all-to-all-start.2) | async-done | bytes 524320 | tf_op jit(solution)/shard_map/all_to_all | solution.py:73
  28.2 3.5 %all-to-all-start.1 = ((bf16[16,1,8,16,128]{4,2,0,1,3:T(8,128)(2,1)}), bf16[16,1,8,16,128]{4,2,0,1,3:T(8,128)(2,1)S(1)}, u32[]{:S(2)}, u32[]{:S(2)}) async-start(bf16[16,1,8,16,128]{4,2,0,1,3:T(8,128)(2,1)} %copy.92), calls=%async_computation.1 | async-start | bytes 1048576 | tf_op jit(solution)/shard_map/all_to_all | solution.py:71
  31.7 0.0 copy-done.3
  31.7 0.1 copy.187
  31.9 0.9 copy.89
  32.8 7.7 %all-to-all-done.1 = bf16[16,1,8,16,128]{4,2,0,1,3:T(8,128)(2,1)S(1)} async-done(((bf16[16,1,8,16,128]{4,2,0,1,3:T(8,128)(2,1)}), bf16[16,1,8,16,128]{4,2,0,1,3:T(8,128)(2,1)S(1)}, u32[]{:S(2)}, u32[]{:S(2)}) %all-to-all-start.1) | async-done | bytes 524320 | tf_op jit(solution)/shard_map/all_to_all | solution.py:71
  40.5 0.0 copy-start.4
  40.5 4.1 %all-to-all-start = ((bf16[16,1,8,16,128]{4,2,0,1,3:T(8,128)(2,1)}), bf16[16,1,8,16,128]{4,2,0,1,3:T(8,128)(2,1)}, u32[]{:S(2)}, u32[]{:S(2)}) async-start(bf16[16,1,8,16,128]{4,2,0,1,3:T(8,128)(2,1)} %copy.89), calls=%async_computation | async-start | bytes 1048576 | tf_op jit(solution)/shard_map/all_to_all | solution.py:70
  44.7 0.0 copy-done
  44.7 0.3 fusion.30
  45.0 0.8 fusion.13
  45.8 1.0 copy.106
  46.9 6.7 %all-to-all-done = bf16[16,1,8,16,128]{4,2,0,1,3:T(8,128)(2,1)} async-done(((bf16[16,1,8,16,128]{4,2,0,1,3:T(8,128)(2,1)}), bf16[16,1,8,16,128]{4,2,0,1,3:T(8,128)(2,1)}, u32[]{:S(2)}, u32[]{:S(2)}) %all-to-all-start) | async-done | bytes 524320 | tf_op jit(solution)/shard_map/all_to_all | solution.py:70
  53.6 0.0 copy-done.4
  53.6 1.9 %fusion.8 = f32[16,8,4,4,4]{3,4,2,1,0:T(4,128)S(1)} fusion(bf16[16,1,8,4,4,128]{5,2,0,4,3,1:T(8,128)(2,1)S(1)} %bitcast.129, bf16[16,1,8,4,4,128]{5,2,0,4,3,1:T(8,128)(2,1)} %bitcast.2), kind=kOutput, calls=%fused_computation.17 | convolution fusion | flops 2097152 | bytes 1081344 | tf_op jit(solution)/shard_map/atxhd,auxhd->axhtu/dot_general | solution.py:22
  55.5 1.1 copy.95
  56.6 0.2 fusion.28
  56.8 0.2 fusion.27
  56.9 0.2 fusion.37
  57.1 1.2 copy.113
  58.3 1.5 %fusion.2 = f32[16,8,4,4]{3,2,1,0:T(4,128)S(1)} fusion(bf16[16,8,4,4,4]{3,4,2,1,0:T(4,128)(2,1)S(1)} %copy.113, bf16[16,1,8,4,4,128]{5,2,0,4,3,1:T(8,128)(2,1)S(1)} %bitcast.128, bf16[16,1,8,4,4,128]{5,2,0,4,3,1:T(8,128)(2,1)S(1)} %bitcast.125), kind=kOutput, calls=%fused_computation.6 | convolution fusion | flops 2881536 | bytes 1073152 | tf_op jit(solution)/shard_map/axhtu,auxhd->atxhd/dot_general | solution.py:31
  59.8 0.3 copy.128
  60.1 0.2 fusion.38
  60.3 0.0 copy-start.5
  60.3 1.2 copy.110
  61.5 0.0 copy-done.5
  61.5 0.9 fusion.4
  62.5 1.0 copy.108
  63.5 3.5 %all-to-all-start.4 = ((bf16[16,4,8,4,128]{4,3,2,0,1:T(4,128)(2,1)}), bf16[16,4,8,4,128]{4,3,2,0,1:T(4,128)(2,1)S(1)}, u32[]{:S(2)}, u32[]{:S(2)}) async-start(bf16[16,4,8,4,128]{4,3,2,0,1:T(4,128)(2,1)} %copy.108), calls=%async_computation.4 | async-start | bytes 1048576 | tf_op jit(solution)/shard_map/all_to_all | solution.py:77
  66.9 1.8 %fusion.3 = bf16[16,4,8,4,128]{4,1,3,2,0:T(4,128)(2,1)S(1)} fusion(bf16[16,8,4,4,4]{3,4,2,1,0:T(4,128)(2,1)S(1)} %copy.110, bf16[16,1,8,4,4,128]{5,2,0,4,3,1:T(8,128)(2,1)} %bitcast.2), kind=kOutput, calls=%fused_computation.7 | convolution fusion | flops 2621440 | bytes 1064960 | tf_op jit(solution)/shard_map/axhtu,atxhd->auxhd/dot_general | solution.py:48
  68.7 1.0 copy.111
  69.7 6.0 %all-to-all-done.4 = bf16[16,4,8,4,128]{4,3,2,0,1:T(4,128)(2,1)S(1)} async-done(((bf16[16,4,8,4,128]{4,3,2,0,1:T(4,128)(2,1)}), bf16[16,4,8,4,128]{4,3,2,0,1:T(4,128)(2,1)S(1)}, u32[]{:S(2)}, u32[]{:S(2)}) %all-to-all-start.4) | async-done | bytes 524320 | tf_op jit(solution)/shard_map/all_to_all | solution.py:77
  75.7 3.5 %all-to-all-start.5 = ((bf16[16,4,8,4,128]{4,3,2,0,1:T(4,128)(2,1)}), bf16[16,4,8,4,128]{4,3,2,0,1:T(4,128)(2,1)S(1)}, u32[]{:S(2)}, u32[]{:S(2)}) async-start(bf16[16,4,8,4,128]{4,3,2,0,1:T(4,128)(2,1)} %copy.111), calls=%async_computation.5 | async-start | bytes 1048576 | tf_op jit(solution)/shard_map/all_to_all | solution.py:78
  79.2 0.7 fusion.5
  79.9 1.0 copy.114
  80.9 7.1 %all-to-all-done.5 = bf16[16,4,8,4,128]{4,3,2,0,1:T(4,128)(2,1)S(1)} async-done(((bf16[16,4,8,4,128]{4,3,2,0,1:T(4,128)(2,1)}), bf16[16,4,8,4,128]{4,3,2,0,1:T(4,128)(2,1)S(1)}, u32[]{:S(2)}, u32[]{:S(2)}) %all-to-all-start.5) | async-done | bytes 524320 | tf_op jit(solution)/shard_map/all_to_all | solution.py:78
  88.0 3.5 %all-to-all-start.6 = ((bf16[16,4,8,4,128]{4,3,2,0,1:T(4,128)(2,1)}), bf16[16,4,8,4,128]{4,3,2,0,1:T(4,128)(2,1)S(1)}, u32[]{:S(2)}, u32[]{:S(2)}) async-start(bf16[16,4,8,4,128]{4,3,2,0,1:T(4,128)(2,1)} %copy.114), calls=%async_computation.6 | async-start | bytes 1048576 | tf_op jit(solution)/shard_map/all_to_all | solution.py:79
  91.5 0.4 fusion.6
  91.9 0.1 copy.117
  92.0 0.1 dynamic_update_slice.3
  92.1 43.3 %psum.7 = f32[16,4]{0,1:T(4,128)} all-reduce(f32[16,4]{0,1:T(4,128)S(1)} %dynamic_update_slice.3), channel_id=1, replica_groups=mesh['tm'=4,'patch'=8] {'tm','patch'}, use_global_device_ids=true, to_apply=%region_3.4 | all-reduce | flops 64 | bytes 512 | tf_op jit(solution)/shard_map/psum | solution.py:86
  135.4 0.9 copy.109
  136.3 0.9 copy.112
  137.3 0.0 all-to-all-done.6
  137.3 0.9 copy.115
  (4 shorter events, 0.0 us)
Async XLA Ops:
  0.6 44.1 %copy-start = (f32[16,4]{0,1:T(4,128)S(1)}, f32[16,4]{0,1:T(4,128)}, u32[]{:S(2)}) copy-start(f32[16,4]{0,1:T(4,128)} %param.9) | copy-start | bytes 772
  2.7 4.4 %copy-start.1 = (bf16[16,1,8,2048]{3,2,1,0:T(8,128)(2,1)S(1)}, bf16[16,1,8,2048]{3,2,1,0:T(8,128)(2,1)}, u32[]{:S(2)}) copy-start(bf16[16,1,8,2048]{3,2,1,0:T(8,128)(2,1)} %param.8) | copy-start | bytes 1572868
  2.7 13.2 %all-to-all-start.3 = ((bf16[16,1,8,16,128]{4,2,0,1,3:T(8,128)(2,1)}), bf16[16,1,8,16,128]{4,2,0,1,3:T(8,128)(2,1)S(1)}, u32[]{:S(2)}, u32[]{:S(2)}) async-start(bf16[16,1,8,16,128]{4,2,0,1,3:T(8,128)(2,1)} %copy.102), calls=%async_computation.3 | async-start | bytes 1048576 | tf_op jit(solution)/shard_map/all_to_all | solution.py:72
  8.2 11.3 %copy-start.2 = (bf16[16,1,8,2048]{3,2,1,0:T(8,128)(2,1)S(1)}, bf16[16,1,8,2048]{3,2,1,0:T(8,128)(2,1)}, u32[]{:S(2)}) copy-start(bf16[16,1,8,2048]{3,2,1,0:T(8,128)(2,1)} %param.6) | copy-start | bytes 1572868
  16.0 12.3 %all-to-all-start.2 = ((bf16[16,1,8,16,128]{4,2,0,1,3:T(8,128)(2,1)}), bf16[16,1,8,16,128]{4,2,0,1,3:T(8,128)(2,1)S(1)}, u32[]{:S(2)}, u32[]{:S(2)}) async-start(bf16[16,1,8,16,128]{4,2,0,1,3:T(8,128)(2,1)} %copy.99), calls=%async_computation.2 | async-start | bytes 1048576 | tf_op jit(solution)/shard_map/all_to_all | solution.py:73
  20.5 11.2 %copy-start.3 = (bf16[16,1,8,2048]{3,2,1,0:T(8,128)(2,1)S(1)}, bf16[16,1,8,2048]{3,2,1,0:T(8,128)(2,1)}, u32[]{:S(2)}) copy-start(bf16[16,1,8,2048]{3,2,1,0:T(8,128)(2,1)} %param.5) | copy-start | bytes 1572868
  28.2 12.3 %all-to-all-start.1 = ((bf16[16,1,8,16,128]{4,2,0,1,3:T(8,128)(2,1)}), bf16[16,1,8,16,128]{4,2,0,1,3:T(8,128)(2,1)S(1)}, u32[]{:S(2)}, u32[]{:S(2)}) async-start(bf16[16,1,8,16,128]{4,2,0,1,3:T(8,128)(2,1)} %copy.92), calls=%async_computation.1 | async-start | bytes 1048576 | tf_op jit(solution)/shard_map/all_to_all | solution.py:71
  40.5 13.1 %copy-start.4 = (bf16[16,1,8,16,128]{4,2,0,1,3:T(8,128)(2,1)}, bf16[16,1,8,16,128]{4,2,0,1,3:T(8,128)(2,1)S(1)}, u32[]{:S(2)}) copy-start(bf16[16,1,8,16,128]{4,2,0,1,3:T(8,128)(2,1)S(1)} %all-to-all-done.1) | copy-start | bytes 1572868
  40.5 13.1 %all-to-all-start = ((bf16[16,1,8,16,128]{4,2,0,1,3:T(8,128)(2,1)}), bf16[16,1,8,16,128]{4,2,0,1,3:T(8,128)(2,1)}, u32[]{:S(2)}, u32[]{:S(2)}) async-start(bf16[16,1,8,16,128]{4,2,0,1,3:T(8,128)(2,1)} %copy.89), calls=%async_computation | async-start | bytes 1048576 | tf_op jit(solution)/shard_map/all_to_all | solution.py:70
  60.3 1.2 copy-start.5
  63.5 12.3 %all-to-all-start.4 = ((bf16[16,4,8,4,128]{4,3,2,0,1:T(4,128)(2,1)}), bf16[16,4,8,4,128]{4,3,2,0,1:T(4,128)(2,1)S(1)}, u32[]{:S(2)}, u32[]{:S(2)}) async-start(bf16[16,4,8,4,128]{4,3,2,0,1:T(4,128)(2,1)} %copy.108), calls=%async_computation.4 | async-start | bytes 1048576 | tf_op jit(solution)/shard_map/all_to_all | solution.py:77
  75.7 12.3 %all-to-all-start.5 = ((bf16[16,4,8,4,128]{4,3,2,0,1:T(4,128)(2,1)}), bf16[16,4,8,4,128]{4,3,2,0,1:T(4,128)(2,1)S(1)}, u32[]{:S(2)}, u32[]{:S(2)}) async-start(bf16[16,4,8,4,128]{4,3,2,0,1:T(4,128)(2,1)} %copy.111), calls=%async_computation.5 | async-start | bytes 1048576 | tf_op jit(solution)/shard_map/all_to_all | solution.py:78
  88.0 49.2 %all-to-all-start.6 = ((bf16[16,4,8,4,128]{4,3,2,0,1:T(4,128)(2,1)}), bf16[16,4,8,4,128]{4,3,2,0,1:T(4,128)(2,1)S(1)}, u32[]{:S(2)}, u32[]{:S(2)}) async-start(bf16[16,4,8,4,128]{4,3,2,0,1:T(4,128)(2,1)} %copy.114), calls=%async_computation.6 | async-start | bytes 1048576 | tf_op jit(solution)/shard_map/all_to_all | solution.py:79
where the time goes:
time: 139 us; the launch traced here: 138 us
  blocking collectives  43.3 us (31%)
  waiting for transfers between devices  43.1 us (31%)
  starting transfers between devices  25.9 us (19%)
  local copies, waits for them, and re-layouts  16 us (12%)
  matrix products  8.27 us (6%)
    psum x1, blocking collectives, per_device(): bias_total = lax.psum(partial_full, ('tm', 'patch'))  43.3 us
    all_to_all x1, waiting for transfers between devices, per_device(): lax.all_to_all(value_heads, 'tm', split_axis=3, concat_axis=1, tiled=True)  7.79 us
    all_to_all x1, waiting for transfers between devices, per_device(): lax.all_to_all(grad_heads, 'tm', split_axis=3, concat_axis=1, tiled=True)  7.74 us
    all_to_all x1, waiting for transfers between devices, per_device(): lax.all_to_all(key_heads, 'tm', split_axis=3, concat_axis=1, tiled=True)  7.74 us
    all_to_all x1, waiting for transfers between devices, per_device(): lax.all_to_all(grad_key, 'tm', split_axis=1, concat_axis=3, tiled=True)  7.12 us
    all_to_all x1, waiting for transfers between devices, per_device(): lax.all_to_all(query_heads, 'tm', split_axis=3, concat_axis=1, tiled=True)  6.72 us
    all_to_all x1, waiting for transfers between devices, per_device(): lax.all_to_all(grad_query, 'tm', split_axis=1, concat_axis=3, tiled=True)  6.01 us
    all_to_all x1, starting transfers between devices, per_device(): lax.all_to_all(value_heads, 'tm', split_axis=3, concat_axis=1, tiled=True)  4.37 us
  transfers between devices with their start and end apart: 7, of which 6 were waited for; matrix products, arithmetic and copies ran while one was open for 9% of the time, Pallas kernels for 0%

commit v1 on v0

v1 whole, which is shorter than its diff:
```python
import functools
import math

import jax
import jax.numpy as jnp
from jax import lax
from jax.experimental import pallas as pl
from jax.experimental.pallas import tpu as pltpu
from jax.sharding import PartitionSpec as P

LANES = 128
TILE = 16
COPY_ROWS = 16
LITTLE = pl.CostEstimate(flops=1, bytes_accessed=1, transcendentals=0)
CHUNKS = 2


def score_table(bias_rows, frames):
    steps = jnp.arange(frames, dtype=jnp.int32)
    offsets = steps[:, None] - steps[None, :]
    onehot = (offsets[:, :, None] == steps[None, None, :]).astype(jnp.float32)
    table = jnp.einsum("hd,tud->htu", bias_rows, onehot, precision=lax.Precision.HIGHEST)
    return (table, offsets >= 0, onehot)


def attend_back(query_heads, key_heads, value_heads, grad_heads, bias_rows):
    frames = query_heads.shape[1]
    score_scale = 1.0 / math.sqrt(query_heads.shape[4])
    table, causal, onehot = score_table(bias_rows, frames)
    wide = jnp.float32
    scores = (
        jnp.einsum("atxhd,auxhd->axhtu", query_heads, key_heads, preferred_element_type=wide)
        * score_scale
        + table[None, None]
    )
    scores = jnp.where(causal, scores, -jnp.inf)
    row_max = jnp.max(scores, axis=-1, keepdims=True)
    expon = jnp.exp(scores - row_max)
    weights = expon / jnp.sum(expon, axis=-1, keepdims=True)
    weights_low = weights.astype(jnp.bfloat16)
    attended = jnp.einsum(
        "axhtu,auxhd->atxhd", weights_low, value_heads, preferred_element_type=wide
    )
    rowdot = jnp.einsum("atxhd,atxhd->axht", grad_heads, attended, preferred_element_type=wide)
    grad_weights = jnp.einsum(
        "atxhd,auxhd->axhtu", grad_heads, value_heads, preferred_element_type=wide
    )
    grad_scores = weights * (grad_weights - rowdot[..., None])
    bias_terms = jnp.einsum("axhtu,tud->axhd", grad_scores, onehot, precision=lax.Precision.HIGHEST)
    grad_low = grad_scores.astype(jnp.bfloat16)
    grad_query = (
        jnp.einsum("axhtu,auxhd->atxhd", grad_low, key_heads, preferred_element_type=wide)
        * score_scale
    ).astype(jnp.bfloat16)
    grad_key = (
        jnp.einsum("axhtu,atxhd->auxhd", grad_low, query_heads, preferred_element_type=wide)
        * score_scale
    ).astype(jnp.bfloat16)
    grad_value = jnp.einsum(
        "axhtu,atxhd->auxhd", weights_low, grad_heads, preferred_element_type=wide
    ).astype(jnp.bfloat16)
    return (grad_query, grad_key, grad_value, bias_terms)


def sum_everywhere(value, sizes):
    for axis, size in sizes:
        if size & (size - 1):
            value = lax.psum(value, axis)
            continue
        step = 1
        while step < size:
            other = lax.ppermute(value, axis, [(i, i ^ step) for i in range(size)])
            value = value + other
            step *= 2
    return value


def by_heads(query_vectors, key_vectors, value_vectors, grad_output, time_bias, sizes):
    head_count = time_bias.shape[0]
    frames = time_bias.shape[1]
    head_dim = query_vectors.shape[3] // head_count
    split_shape = query_vectors.shape[:3] + (head_count, head_dim)
    local_heads = head_count // lax.axis_size("tm")
    first_head = lax.axis_index("tm") * local_heads
    bias_rows = lax.dynamic_slice_in_dim(time_bias, first_head, local_heads, 0)
    spread = [
        lax.all_to_all(item.reshape(split_shape), "tm", split_axis=3, concat_axis=1, tiled=True)
        for item in (query_vectors, key_vectors, value_vectors, grad_output)
    ]
    *grads, bias_terms = attend_back(*spread, bias_rows)
    grads = [
        lax.all_to_all(item, "tm", split_axis=1, concat_axis=3, tiled=True).reshape(
            query_vectors.shape
        )
        for item in grads
    ]
    partial = lax.dynamic_update_slice_in_dim(
        jnp.zeros((head_count, frames), jnp.float32),
        jnp.sum(bias_terms, axis=(0, 1)),
        first_head,
        0,
    )
    return (*grads, sum_everywhere(partial, sizes))


def pair_dots(queries, keys, grads, values, pairs, heads):
    place = lax.broadcasted_iota(jnp.int32, (TILE, LANES), 1)
    held = [jnp.zeros((TILE, LANES), jnp.float32)] * (2 * len(pairs))
    for head in range(heads):
        at = slice(head * LANES, (head + 1) * LANES)
        here = place == head
        load = lambda refs: [ref[at].astype(jnp.float32) for ref in refs]
        q, k, o, v = load(queries), load(keys), load(grads), load(values)
        for j, (t, u) in enumerate(pairs):
            score = jnp.sum(q[t] * k[u], axis=1, keepdims=True)
            held[j] = jnp.where(here, score, held[j])
            gain = jnp.sum(o[t] * v[u], axis=1, keepdims=True)
            held[len(pairs) + j] = jnp.where(here, gain, held[len(pairs) + j])
    return held


def over_tiles(rows, body):
    pl.loop(0, rows // TILE)(lambda i: body(i * TILE))


def tile_at(start):
    return pl.ds(pl.multiple_of(start, TILE), TILE)


class Shifted:
    def __init__(self, ref, start):
        self.ref, self.start = ref, start

    def at_rows(self, row):
        return View(self.ref, tile_at(self.start + row))


class View:
    def __init__(self, ref, rows):
        self.ref, self.rows = ref, rows

    def __getitem__(self, lanes):
        return self.ref[self.rows, lanes]

    def __setitem__(self, lanes, value):
        self.ref[self.rows, lanes] = value


def tiles_of(refs, row):
    return tuple(ref.at_rows(row) for ref in refs)


def shifted(refs, start):
    return tuple(Shifted(ref, start) for ref in refs)


def soft_row(scores, gains):
    top = functools.reduce(jnp.maximum, scores)
    expon = [jnp.exp(item - top) for item in scores]
    total = functools.reduce(jnp.add, expon)
    weights = [item / total for item in expon]
    low = [item.astype(jnp.bfloat16) for item in weights]
    rowdot = functools.reduce(
        jnp.add, [a.astype(jnp.float32) * g for a, g in zip(low, gains)]
    )
    grads = [w * (g - rowdot) for w, g in zip(weights, gains)]
    return low, grads


LOCAL = ((0, 0), (1, 0), (1, 1))
CROSS = ((0, 0), (0, 1), (1, 0), (1, 1))


def unpack(packed, heads):
    return [packed if j == 0 else pltpu.roll(packed, LANES - heads * j, axis=1) for j in range(6)]


def bias_lines(terms):
    lines = []
    for items in terms:
        lines.append(
            jnp.sum(functools.reduce(jnp.add, items), axis=0, keepdims=True)
            if items
            else jnp.zeros((1, LANES), jnp.float32)
        )
    return jnp.concatenate(lines + [jnp.zeros((4, LANES), jnp.float32)], axis=0)


def early_rows(diag, scale, offset):
    score = lambda j, d: diag[j] * scale + offset[d]
    row0 = soft_row([score(0, 0)], [diag[3]])
    row1 = soft_row([score(1, 1), score(2, 0)], [diag[4], diag[5]])
    return row0, row1


def my_place():
    me = lax.axis_index("tm")
    return lax.rem(me, 2), lax.div(me, 2)


def with_frames(own, other, work):
    core, chip = my_place()
    for at_chip in range(2):
        pl.when((chip == at_chip) & (core == 0))(functools.partial(work, at_chip, own, other))
        pl.when((chip == at_chip) & (core == 1))(functools.partial(work, at_chip, other, own))


def chunk_start(chunk, size):
    return jnp.where(my_place()[1] == 0, chunk, CHUNKS - 1 - chunk) * size


def sent_start(chunk, size):
    return jnp.where(my_place()[1] == 1, chunk, CHUNKS - 1 - chunk) * size


def copy_rows(sources, start, out, sems, rows):
    copies = []
    for j, ref in enumerate(sources):
        for row in range(0, out.shape[1], rows):
            copies.append(
                pltpu.make_async_copy(
                    ref.at[pl.ds(pl.multiple_of(start + row, rows), rows)],
                    out.at[j, pl.ds(row, rows)],
                    sems.at[len(copies)],
                )
            )
    for copy in copies:
        copy.start()
    for copy in copies:
        copy.wait()


def take_far(refs, row, outs):
    chip = my_place()[1]

    def take(places):
        for out, place in zip(outs, places):
            for step in range(0, out.shape[0], TILE):
                out[step : step + TILE, : refs[place].shape[1]] = refs[place][
                    tile_at(row + step), :
                ]

    pl.when(chip == 0)(lambda: take((1, 2)))
    pl.when(chip == 1)(lambda: take((0, 3)))


def fetch_theirs_kernel(q, k, v, o, near, other, sems):
    half, size = near.shape[1], other.shape[1]
    copy_rows((q, k, v, o), (1 - my_place()[0]) * half, near, sems, COPY_ROWS)
    take_far(planes(near), sent_start(0, size), planes(other))


def fetch_mine_kernel(q, k, v, o, after, mine, sems):
    copy_rows((q, k, v, o), my_place()[0] * mine.shape[1], mine, sems, COPY_ROWS)


def split_wide(value):
    parts = []
    for _ in range(3):
        part = value.astype(jnp.bfloat16)
        value = value - part.astype(jnp.float32)
        parts.append(part)
    return parts


def local_kernel(heads, scale, table, mine, near, theirs, small, out_bias, *outs):
    others = outs[: CHUNKS - 1]
    sames = [outs[CHUNKS - 1 : CHUNKS + 1]] + [planes(out) for out in outs[CHUNKS + 1 :]]
    core, chip = my_place()
    half, size, width = mine.shape[1], sames[0][0].shape[0], mine.shape[2]
    own, other = shifted(planes(mine), 0), shifted(planes(near), 0)
    offset = [table[d : d + 1, :] for d in range(4)]
    out_bias[...] = jnp.zeros_like(out_bias)

    def run(a, b):
        def tile(row):
            at, bt = tiles_of(a, row), tiles_of(b, row)
            held = pair_dots(
                (at[0], bt[0]), (at[1], bt[1]), (at[3], bt[3]), (at[2], bt[2]), LOCAL, heads
            )
            total = held[0]
            for j in range(1, 6):
                total = total + pltpu.roll(held[j], heads * j, axis=1)
            small[tile_at(row), :] = total
            (_, d0), (_, d1) = early_rows(held, scale, offset)
            lines = bias_lines([[d0[0], d1[1]], [d1[0]], [], []])
            out_bias[...] += jnp.where(chip == 0, lines, jnp.zeros_like(lines))

        over_tiles(half, tile)

    pl.when(core == 0)(lambda: run(own, other))
    pl.when(core == 1)(lambda: run(other, own))

    for c, out in enumerate(others):
        take_far(planes(theirs), sent_start(c + 1, size), planes(out))
    for c, out in enumerate(sames):
        start = sent_start(c, size)
        take_far(planes(mine), start, out)
        for step in range(0, size, TILE):
            parts = split_wide(small[tile_at(start + step), :])
            rows = slice(step, step + TILE)
            out[0][rows, width : width + LANES] = parts[0]
            out[0][rows, width + LANES :] = parts[1]
            out[1][rows, width : width + LANES] = parts[2]
            out[1][rows, width + LANES :] = jnp.zeros((TILE, LANES), jnp.bfloat16)


EARLY, LATE = 14, 10


def score_tile(heads, scale, chip, a, b, table, small_own, small_far):
    offset = [table[d : d + 1, :] for d in range(4)]
    if chip == 0:
        queries, keys = ((a[4], a[5]), (b[4], b[5])), ((a[1], a[2]), (b[1], b[2]))
    else:
        queries, keys = ((a[0], a[3]), (b[0], b[3])), ((a[4], a[5]), (b[4], b[5]))
    held = pair_dots(
        [x[0] for x in queries], [x[0] for x in keys],
        [x[1] for x in queries], [x[1] for x in keys], CROSS, heads,
    )
    diag = unpack(small_far if chip == 0 else small_own, heads)
    score = lambda j, d: held[j] * scale + offset[d]
    p2, d2 = soft_row(
        [score(0, 2), score(1, 1), diag[0] * scale + offset[0]], [held[4], held[5], diag[3]]
    )
    p3, d3 = soft_row(
        [score(2, 3), score(3, 2), diag[1] * scale + offset[1], diag[2] * scale + offset[0]],
        [held[6], held[7], diag[4], diag[5]],
    )
    lines = bias_lines([[d2[2], d3[3]], [d2[1], d3[2]], [d2[0], d3[1]], [d3[0]]])
    if chip == 1:
        items = [d2[2], d3[2], d3[3], d2[0], d2[1], d3[0], d3[1], p2[2], p3[2], p3[3]]
    else:
        (p0, d0), (p1, d1) = early_rows(unpack(small_own, heads), scale, offset)
        items = [d0[0], d1[0], d1[1], d2[0], d2[1], d3[0], d3[1]]
        items += [p0[0], p1[0], p1[1], p2[0], p2[1], p3[0], p3[1]]
    return [item.astype(jnp.bfloat16) for item in items], lines


def gradient_tile(heads, scale, chip, a, b, items, out_a, out_b):
    width = 2 * LANES
    lines = -(-heads // TILE) * TILE
    line = lax.broadcasted_iota(jnp.int32, (lines, width), 0)
    head = lax.broadcasted_iota(jnp.int32, (lines, width), 1) // LANES
    zeros = jnp.zeros((LANES - lines, width), jnp.bfloat16)
    spread = jnp.concatenate(items, axis=0)

    for pair in range(heads // 2):
        at = slice(pair * width, (pair + 1) * width)
        pick = jnp.where(line == 2 * pair + head, 1.0, 0.0).astype(jnp.bfloat16)
        flat = jnp.dot(
            spread, jnp.concatenate([pick, zeros], axis=0), preferred_element_type=jnp.float32
        )
        w = [flat[j * TILE : (j + 1) * TILE, :] for j in range(len(items))]

        def put(ref, value):
            ref[at] = value.astype(jnp.bfloat16)

        def wide(*refs):
            return [ref[at].astype(jnp.float32) for ref in refs]

        if chip == 0:
            ka, kb = wide(a[1], b[1])
            put(out_a[0], w[0] * ka * scale)
            put(out_b[0], (w[1] * ka + w[2] * kb) * scale)
            for to, x, g, rate in ((1, 0, 0, scale), (2, 3, 7, 1.0)):
                xa, xb, x2, x3 = wide(a[x], b[x], a[3 + to], b[3 + to])
                for_a = w[g] * xa + w[g + 1] * xb + w[g + 3] * x2 + w[g + 5] * x3
                for_b = w[g + 2] * xb + w[g + 4] * x2 + w[g + 6] * x3
                put(out_a[to], for_a * rate)
                put(out_b[to], for_b * rate)
        else:
            k2, k3, k0, k1 = wide(a[1], b[1], a[4], b[4])
            put(out_a[0], (w[0] * k2 + w[3] * k0 + w[4] * k1) * scale)
            put(out_b[0], (w[1] * k2 + w[2] * k3 + w[5] * k0 + w[6] * k1) * scale)
            q2, q3, o2, o3 = wide(a[0], b[0], a[3], b[3])
            put(out_a[1], (w[0] * q2 + w[1] * q3) * scale)
            put(out_b[1], w[2] * q3 * scale)
            put(out_a[2], w[7] * o2 + w[8] * o3)
            put(out_b[2], w[9] * o3)


def planes(ref):
    return tuple(ref.at[j] for j in range(ref.shape[0]))


def frames_of(mine, near, far, start):
    *same, other = far
    return (
        shifted(planes(mine), start) + shifted(pair_of(same), 0),
        shifted(planes(near), start) + shifted(planes(other), 0),
    )


def pair_of(same):
    return tuple(same) if len(same) == 2 else planes(same[0])


def far_small(far, rows, width):
    first, second = pair_of(far[:-1])
    parts = [first[rows, width : width + LANES], first[rows, width + LANES :]]
    parts += [second[rows, width : width + LANES]]
    return functools.reduce(jnp.add, [part.astype(jnp.float32) for part in parts])


def score_kernel(heads, scale, chunk, table, small, bias, mine, near, *refs):
    *far, out_items, out_bias, lines_ref = refs
    size, width = out_items.shape[1], mine.shape[2]
    start = chunk_start(chunk, size)
    lines_ref[...] = bias[...]

    def work(chip, a, b):
        def tile(row):
            items, lines = score_tile(
                heads, scale, chip, tiles_of(a, row), tiles_of(b, row), table,
                small[tile_at(start + row), :], far_small(far, tile_at(row), width),
            )
            for j, item in enumerate(items):
                out_items[j, tile_at(row), :] = item
            lines_ref[...] += lines

        over_tiles(size, tile)

    with_frames(*frames_of(mine, near, far, start), work)
    out_bias[...] = lines_ref[: out_bias.shape[0], : out_bias.shape[1]]


def gradient_kernel(heads, scale, chunk, items_ref, mine, near, *refs):
    *far, out_own, out_other = refs
    size = out_own.shape[1]
    own, neighbour = frames_of(mine, near, far, chunk_start(chunk, size))
    own_out, other_out = shifted(planes(out_own), 0), shifted(planes(out_other), 0)

    def work(chip, a, b):
        out_a, out_b = (own_out, other_out) if a is own else (other_out, own_out)

        def tile(row):
            items = [items_ref[j, tile_at(row), :] for j in range(LATE if chip else EARLY)]
            gradient_tile(
                heads, scale, chip, tiles_of(a, row), tiles_of(b, row), items,
                tiles_of(out_a, row), tiles_of(out_b, row),
            )

        over_tiles(size, tile)

    with_frames(own, neighbour, work)


def whole_kernel(heads, scale, chunk, table, small, mine, near, *refs):
    *far, out_own = refs[:-3]
    out_others = refs[-3:]
    size, width = out_own.shape[1], mine.shape[2]
    start = chunk_start(chunk, size)
    own, neighbour = frames_of(mine, near, far, start)
    own_out, other_out = shifted(planes(out_own), 0), shifted(out_others, 0)

    def work(chip, a, b):
        out_a, out_b = (own_out, other_out) if a is own else (other_out, own_out)

        def tile(row):
            at, bt = tiles_of(a, row), tiles_of(b, row)
            items, _ = score_tile(
                heads, scale, chip, at, bt, table,
                small[tile_at(start + row), :], far_small(far, tile_at(row), width),
            )
            gradient_tile(
                heads, scale, chip, at, bt, items, tiles_of(out_a, row), tiles_of(out_b, row)
            )

        over_tiles(size, tile)

    with_frames(own, neighbour, work)


def output_kernel(*refs):
    kept, refs = refs[:CHUNKS], refs[CHUNKS:]
    *backs, left, right = refs[:-6]
    outs, (out_bias, total, sems) = refs[-6:-3], refs[-3:]
    backs = [planes(backs[0])] + [backs[j : j + 3] for j in range(1, len(backs), 3)]
    size = kept[0].shape[1]
    half = CHUNKS * size
    core = my_place()[0]
    total[...] = left[...] + right[...]
    copies = [pltpu.make_async_copy(total, out_bias, sems.at[0])]
    for c in range(CHUNKS):
        for which, piece in ((core, planes(kept[c])), (1 - core, backs[c])):
            start = pl.multiple_of(which * half + chunk_start(c, size), TILE)
            for part, out in zip(piece, outs):
                copies.append(
                    pltpu.make_async_copy(part, out.at[pl.ds(start, size)], sems.at[len(copies)])
                )
    for copy in copies:
        copy.start()
    for copy in copies:
        copy.wait()


def four_way(value, axes, masks, count):
    first, second = masks
    got = [
        lax.ppermute(value, axes, [(i, i ^ mask) for i in range(count)])
        for mask in (first, second, first ^ second)
    ]
    return (value + got[0]) + (got[1] + got[2])


def sum_group(value, sizes):
    axes = tuple(axis for axis, _ in sizes)
    (_, tm), (_, patch) = sizes
    count = tm * patch
    masks = [patch] + [1 << j for j in range(patch.bit_length() - 1)] + [2 * patch]
    while len(masks) > 2:
        value = four_way(value, axes, masks[:2], count)
        masks = masks[2:]
    if len(masks) == 2:
        value = value + lax.ppermute(value, axes, [(i, i ^ masks[0]) for i in range(count)])
    return value, lax.ppermute(value, axes, [(i, i ^ masks[-1]) for i in range(count)])


def by_chips(query_vectors, key_vectors, value_vectors, grad_output, time_bias, sizes):
    heads, frames = time_bias.shape
    clips, _, patches, width = query_vectors.shape
    rows = clips * patches
    half = rows // 2
    size = half // CHUNKS
    scale = 1.0 / math.sqrt(width // heads)
    own = [
        pltpu.with_memory_space_constraint(x.reshape(rows, width), pltpu.HBM)
        for x in (query_vectors, key_vectors, value_vectors, grad_output)
    ]
    vmem_spec = pl.BlockSpec(memory_space=pltpu.VMEM)
    any_spec = pl.BlockSpec(memory_space=pl.ANY)

    def swap(x, bits):
        return lax.ppermute(x, "tm", [(i, i ^ bits) for i in range(4)])

    def shape(*dims, dtype=jnp.bfloat16):
        return jax.ShapeDtypeStruct(dims, dtype)

    def call(kernel, name, out_shape, *args, scratch=(), hbm=0, out_spec=vmem_spec):
        return pl.pallas_call(
            kernel,
            in_specs=[any_spec] * hbm + [vmem_spec] * (len(args) - hbm),
            out_specs=[out_spec] * len(out_shape),
            out_shape=out_shape,
            scratch_shapes=scratch,
            compiler_params=pltpu.CompilerParams(vmem_limit_bytes=16 * 2**20),
            cost_estimate=LITTLE,
            name=name,
        )(*args)

    wide = jnp.float32
    copies = [pltpu.SemaphoreType.DMA((4 * half // COPY_ROWS,))]
    far_shape, same_shape = shape(2, size, width), shape(2, size, width + 2 * LANES)
    table = jnp.pad(time_bias.T, ((0, 8 - frames), (0, LANES - heads)))
    theirs, other = call(
        fetch_theirs_kernel, "fetch_theirs", [shape(4, half, width), far_shape], *own,
        scratch=copies, hbm=4,
    )
    near = swap(theirs, 1)
    others = [swap(other, 3)]
    (mine,) = call(
        fetch_mine_kernel, "fetch_mine", [shape(4, half, width)], *own, other, scratch=copies, hbm=5
    )
    small, bias, *sent = call(
        functools.partial(local_kernel, heads, scale),
        "local_scores",
        [shape(half, LANES, dtype=wide), shape(8, LANES, dtype=wide)]
        + [far_shape] * (CHUNKS - 1)
        + [shape(size, width + 2 * LANES)] * 2
        + [same_shape] * (CHUNKS - 1),
        table, mine, near, theirs,
    )
    sames = [[swap(x, 2) for x in sent[CHUNKS - 1 : CHUNKS + 1]]]
    sames += [[swap(x, 2)] for x in sent[CHUNKS + 1 :]]
    others += [swap(x, 3) for x in sent[: CHUNKS - 1]]

    kept, backs = [], []
    pieces = [shape(3, size, width)] * 2
    for c in range(CHUNKS):
        arrays = (mine, near, *sames[c], others[c])
        if c == 0:
            items, bias = call(
                functools.partial(score_kernel, heads, scale, c),
                "scores",
                [shape(EARLY, size, LANES), shape(frames, heads, dtype=wide)],
                table, small, bias, *arrays,
                scratch=[pltpu.VMEM((8, LANES), wide)],
            )
            bias = sum_group(bias, sizes)
            piece, *back = call(
                functools.partial(gradient_kernel, heads, scale, c), "gradients", pieces,
                items, *arrays,
            )
        else:
            piece, *back = call(
                functools.partial(whole_kernel, heads, scale, c), "scores_and_gradients",
                pieces[:1] + [shape(size, width)] * 3, table, small, *arrays,
            )
        kept.append(piece)
        backs.append([swap(x, 1) for x in back])
    *grads, bias = call(
        output_kernel,
        "outputs",
        [shape(rows, width)] * 3 + [shape(frames, heads, dtype=wide)],
        *kept, *(x for back in backs for x in back), *bias,
        scratch=[
            pltpu.VMEM((frames, heads), wide),
            pltpu.SemaphoreType.DMA((1 + 6 * CHUNKS,)),
        ],
        out_spec=any_spec,
    )
    return (*[x.reshape(query_vectors.shape) for x in grads], bias.T)


def solution(mesh):
    sizes = tuple((axis, mesh.shape[axis]) for axis in ("tm", "patch"))

    def per_device(*args):
        heads, frames = args[4].shape
        fits = (
            mesh.shape["tm"] == 4
            and frames == 4
            and args[0].shape[1] == 1
            and heads * LANES == args[0].shape[3]
            and heads * 6 <= LANES
            and heads % 2 == 0
            and args[0].shape[0] * args[0].shape[2] % (2 * TILE * CHUNKS) == 0
            and mesh.shape["patch"].bit_count() == 1
        )
        return (by_chips if fits else by_heads)(*args, sizes)

    vectors = P(None, "tm", "patch", None)
    return jax.shard_map(
        per_device,
        mesh=mesh,
        in_specs=(vectors,) * 4 + (P(),),
        out_specs=(vectors,) * 3 + (P(),),
        check_vma=False,
    )
```

time: 139 us -> 39.1 us (0.28)
  blocking collectives: 43.3 us -> 0 us
  waiting for transfers between devices: 43.1 us -> 13.1 us
  local copies, waits for them, and re-layouts: 16 us -> 0.01 us
  starting transfers between devices: 25.9 us -> 16.2 us
  Pallas kernels: 0 us -> 8.85 us
  matrix products: 8.27 us -> 0 us
    psum x1 -> x0, blocking collectives: 43.3 us -> none  [per_device(): bias_total = lax.psum(partial_full, ('tm', 'patch'))]
    all_to_all x7 -> x0, waiting for transfers between devices: 43.1 us -> none  [the longest x1 7.79 us: per_device(): lax.all_to_all(value_heads, 'tm', split_axis=3, concat_axis=1, tiled=True)]
    all_to_all x7 -> x0, starting transfers between devices: 25.9 us -> none  [the longest x1 4.37 us: per_device(): lax.all_to_all(value_heads, 'tm', split_axis=3, concat_axis=1, tiled=True)]
    ppermute x0 -> x17, starting transfers between devices: none -> 16.2 us  [the longest x10 7.66 us: swap(): return lax.ppermute(x, 'tm', [(i, i ^ bits) for i in range(4)])]
    ppermute x0 -> x17, waiting for transfers between devices: none -> 13.1 us  [the longest x10 10 us: swap(): return lax.ppermute(x, 'tm', [(i, i ^ bits) for i in range(4)])]
    pallas_call x0 -> x7, Pallas kernels: none -> 8.85 us  [call(): pl.pallas_call(kernel, in_specs=[any_spec] * hbm + [vmem_spec] * (len(arg...]
    dot_general x8 -> x0, matrix products: 8.27 us -> none  [the longest x1 1.87 us: attend_back(): jnp.einsum('atxhd,auxhd->axhtu', query_heads, key_heads, preferred_elemen...]
    convert_element_type x5 -> x0, local copies, waits for them, and re-layouts: 5.36 us -> none  [the longest x1 1.19 us: attend_back(): grad_low = grad_scores.astype(jnp.bfloat16)]
  transfers between devices with their start and end apart: 7 -> 17, of which waited for: 6 -> 7; matrix products, arithmetic and copies ran while one was open for 9% -> 0% of each run, Pallas kernels for 0% -> 16%
where the time goes in v1:
time: 39.1 us; the launch traced here: 38.9 us
  starting transfers between devices  16.2 us (41%)
  waiting for transfers between devices  13.1 us (34%)
  Pallas kernels  8.85 us (23%)
  between operations  0.73 us (2%)
    ppermute x10, waiting for transfers between devices, swap(): return lax.ppermute(x, 'tm', [(i, i ^ bits) for i in range(4)])  10 us
    pallas_call x7, Pallas kernels, call(): pl.pallas_call(kernel, in_specs=[any_spec] * hbm + [vmem_spec] * (len(arg...  8.85 us
    ppermute x10, starting transfers between devices, swap(): return lax.ppermute(x, 'tm', [(i, i ^ bits) for i in range(4)])  7.66 us
    ppermute x6, starting transfers between devices, four_way(): lax.ppermute(value, axes, [(i, i ^ mask) for i in range(count)])  7.33 us
    ppermute x1, waiting for transfers between devices, sum_group(): lax.ppermute(value, axes, [(i, i ^ masks[-1]) for i in range(count)])  2.42 us
    ppermute x1, starting transfers between devices, sum_group(): lax.ppermute(value, axes, [(i, i ^ masks[-1]) for i in range(count)])  1.22 us
  transfers between devices with their start and end apart: 17, of which 7 were waited for; matrix products, arithmetic and copies ran while one was open for 0% of the time, Pallas kernels for 16%

profile of v1, /device:TPU:0, one launch (start us, length us, event | category | flops | bytes accessed | tf_op | source)
XLA Modules:
  0.0 38.9 jit_solution(12809450418895339401)
XLA Ops:
  0.6 1.4 %fetch_theirs.1 = (bf16[4,64,2048]{2,1,0:T(8,128)(2,1)S(1)}, bf16[2,32,2048]{2,1,0:T(8,128)(2,1)S(1)}) custom-call(bf16[128,2048]{1,0:T(8,128)(2,1)} %bitcast.15, bf16[128,2048]{1,0:T(8,128)(2,1)} %bitcast.17, bf16[128,2048]{1,0:T(8,128)(2,1)} %bitcast.19, bf16[128,2048]{1,0:T(8,128)(2,1)} %bitcast.21), custom_call_target="tpu_custom_call" | custom-call | flops 1 | bytes 1 | tf_op jit(solution)/shard_map/fetch_theirs/pallas_call | solution.py:541
  2.0 0.5 %collective-permute-start = (bf16[4,64,2048]{2,1,0:T(8,128)(2,1)S(1)}, bf16[4,64,2048]{2,1,0:T(8,128)(2,1)S(1)}, u32[]{:S(2)}, u32[]{:S(2)}) collective-permute-start(bf16[4,64,2048]{2,1,0:T(8,128)(2,1)S(1)} %get-tuple-element.25.theirs), channel_id=1, source_target_pairs={{0,8},{8,0},{16,24},{24,16},{1,9},{9,1},{17,25},{25,17},{2,10},{10... | collective-permute-start | bytes 3145736 | tf_op jit(solution)/shard_map/ppermute | solution.py:535
  2.6 2.6 %collective-permute-start.3 = (bf16[2,32,2048]{2,1,0:T(8,128)(2,1)S(1)}, bf16[2,32,2048]{2,1,0:T(8,128)(2,1)S(1)}, u32[]{:S(2)}, u32[]{:S(2)}) collective-permute-start(bf16[2,32,2048]{2,1,0:T(8,128)(2,1)S(1)} %get-tuple-element.24.after), channel_id=1, source_target_pairs={{0,24},{8,16},{16,8},{24,0},{1,25},{9,17},{17,9},{25,1},{2,26},{10... | collective-permute-start | bytes 786440 | tf_op jit(solution)/shard_map/ppermute | solution.py:535
  5.2 0.0 copy-start
  5.2 1.4 %fetch_mine.1.mine = bf16[4,64,2048]{2,1,0:T(8,128)(2,1)S(1)} custom-call(bf16[128,2048]{1,0:T(8,128)(2,1)} %bitcast.16, bf16[128,2048]{1,0:T(8,128)(2,1)} %bitcast.18, bf16[128,2048]{1,0:T(8,128)(2,1)} %bitcast.20, bf16[128,2048]{1,0:T(8,128)(2,1)} %bitcast.22, bf16[2,32,2048]{2,1,0:T(8,128)(2,1)S(1)} %get-tuple-element.24.after), custom_call_target="tpu_custom_call" | custom-call | flops 1 | bytes 1 | tf_op jit(solution)/shard_map/fetch_mine/pallas_call | solution.py:541
  6.6 0.0 copy-done
  6.6 0.0 collective-permute-done.near
  6.6 1.5 %local_scores.1 = (f32[64,128]{1,0:T(8,128)S(1)}, f32[8,128]{1,0:T(8,128)S(1)}, bf16[2,32,2048]{2,1,0:T(8,128)(2,1)S(1)}, bf16[32,2304]{1,0:T(8,128)(2,1)S(1)}, ...) custom-call(f32[8,128]{1,0:T(8,128)S(1)} %pad.4.table, bf16[4,64,2048]{2,1,0:T(8,128)(2,1)S(1)} %fetch_mine.1.mine, ...), custom_call_target="tpu_custom_call" | custom-call | flops 1 | bytes 1 | tf_op jit(solution)/shard_map/local_scores/pallas_call | solution.py:541
  8.1 1.1 %collective-permute-start.1 = (bf16[32,2304]{1,0:T(8,128)(2,1)S(1)}, bf16[32,2304]{1,0:T(8,128)(2,1)S(1)}, u32[]{:S(2)}, u32[]{:S(2)}) collective-permute-start(bf16[32,2304]{1,0:T(8,128)(2,1)S(1)} %get-tuple-element.28), channel_id=1, source_target_pairs={{0,16},{8,24},{16,0},{24,8},{1,17},{9,25},{17,1},{25,9},{2,18},{10... | collective-permute-start | bytes 442376 | tf_op jit(solution)/shard_map/ppermute | solution.py:535
  9.3 0.9 %collective-permute-start.2 = (bf16[32,2304]{1,0:T(8,128)(2,1)S(1)}, bf16[32,2304]{1,0:T(8,128)(2,1)S(1)}, u32[]{:S(2)}, u32[]{:S(2)}) collective-permute-start(bf16[32,2304]{1,0:T(8,128)(2,1)S(1)} %get-tuple-element.29), channel_id=1, source_target_pairs={{0,16},{8,24},{16,0},{24,8},{1,17},{9,25},{17,1},{25,9},{2,18},{10... | collective-permute-start | bytes 442376 | tf_op jit(solution)/shard_map/ppermute | solution.py:535
  10.2 1.1 %collective-permute-start.4 = (bf16[2,32,2304]{2,1,0:T(8,128)(2,1)S(1)}, bf16[2,32,2304]{2,1,0:T(8,128)(2,1)S(1)}, u32[]{:S(2)}, u32[]{:S(2)}) collective-permute-start(bf16[2,32,2304]{2,1,0:T(8,128)(2,1)S(1)} %get-tuple-element.32), channel_id=1, source_target_pairs={{0,16},{8,24},{16,0},{24,8},{1,17},{9,25},{17,1},{25,9},{2,18},{10... | collective-permute-start | bytes 884744 | tf_op jit(solution)/shard_map/ppermute | solution.py:535
  11.3 0.0 collective-permute-start.5
  11.3 0.6 %collective-permute-done.3.refs_2_ = bf16[2,32,2048]{2,1,0:T(8,128)(2,1)S(1)} collective-permute-done((bf16[2,32,2048]{2,1,0:T(8,128)(2,1)S(1)}, bf16[2,32,2048]{2,1,0:T(8,128)(2,1)S(1)}, u32[]{:S(2)}, u32[]{:S(2)}) %collective-permute-start.3) | collective-permute-done | bytes 262176 | tf_op jit(solution)/shard_map/ppermute | solution.py:535
  11.8 3.6 %collective-permute-done.1.refs_0_ = bf16[32,2304]{1,0:T(8,128)(2,1)S(1)} collective-permute-done((bf16[32,2304]{1,0:T(8,128)(2,1)S(1)}, bf16[32,2304]{1,0:T(8,128)(2,1)S(1)}, u32[]{:S(2)}, u32[]{:S(2)}) %collective-permute-start.1) | collective-permute-done | bytes 147488 | tf_op jit(solution)/shard_map/ppermute | solution.py:535
  15.5 3.2 %collective-permute-done.2.refs_1_ = bf16[32,2304]{1,0:T(8,128)(2,1)S(1)} collective-permute-done((bf16[32,2304]{1,0:T(8,128)(2,1)S(1)}, bf16[32,2304]{1,0:T(8,128)(2,1)S(1)}, u32[]{:S(2)}, u32[]{:S(2)}) %collective-permute-start.2) | collective-permute-done | bytes 147488 | tf_op jit(solution)/shard_map/ppermute | solution.py:535
  18.6 0.8 %scores.1 = (bf16[14,32,128]{2,1,0:T(8,128)(2,1)S(1)}, f32[4,16]{1,0:T(4,128)S(1)}) custom-call(f32[8,128]{1,0:T(8,128)S(1)} %pad.4.table, f32[64,128]{1,0:T(8,128)S(1)} %get-tuple-element.26.small, f32[8,128]{1,0:T(8,128)S(1)} %get-tuple-element.27.bias, bf16[4,64,2048]{2,1,0:T(8,128)(2,1)S(1)} %fetch_mine.1.mine, ...), custom_call_target="tpu_custom_call" | custom-call | flops 1 | bytes 1 | tf_op jit(solution)/shard_map/scores/pallas_call | solution.py:541
  19.5 0.6 %collective-permute-start.12 = (f32[4,16]{1,0:T(4,128)S(1)}, f32[4,16]{1,0:T(4,128)S(1)}, u32[]{:S(2)}, u32[]{:S(2)}) collective-permute-start(f32[4,16]{1,0:T(4,128)S(1)} %get-tuple-element.39), channel_id=1, source_target_pairs={{0,9},{1,8},{2,11},{3,10},{4,13},{5,12},{6,15},{7,14},{8,1},{9,0},... | collective-permute-start | bytes 776 | tf_op jit(solution)/shard_map/ppermute | solution.py:501
  20.1 1.5 %collective-permute-start.11 = (f32[4,16]{1,0:T(4,128)S(1)}, f32[4,16]{1,0:T(4,128)S(1)}, u32[]{:S(2)}, u32[]{:S(2)}) collective-permute-start(f32[4,16]{1,0:T(4,128)S(1)} %get-tuple-element.39), channel_id=1, source_target_pairs={{0,1},{1,0},{2,3},{3,2},{4,5},{5,4},{6,7},{7,6},{8,9},{9,8},{10,11... | collective-permute-start | bytes 776 | tf_op jit(solution)/shard_map/ppermute | solution.py:501
  21.6 0.0 collective-permute-start.10
  21.6 0.8 %gradients.1 = (bf16[3,32,2048]{2,1,0:T(8,128)(2,1)S(1)}, bf16[3,32,2048]{2,1,0:T(8,128)(2,1)S(1)}) custom-call(bf16[14,32,128]{2,1,0:T(8,128)(2,1)S(1)} %get-tuple-element.30.items_ref, bf16[4,64,2048]{2,1,0:T(8,128)(2,1)S(1)} %fetch_mine.1.mine, bf16[4,64,2048]{2,1,0:T(8,128)(2,1)S(1)} %collective-permute-done.near, ...), custom_call_target="tpu_custom_call" | custom-call | flops 1 | bytes 1 | tf_op jit(solution)/shard_map/gradients/pallas_call | solution.py:541
  22.4 0.1 collective-permute-done.12
  22.5 0.7 %collective-permute-start.6 = (bf16[3,32,2048]{2,1,0:T(8,128)(2,1)S(1)}, bf16[3,32,2048]{2,1,0:T(8,128)(2,1)S(1)}, u32[]{:S(2)}, u32[]{:S(2)}) collective-permute-start(bf16[3,32,2048]{2,1,0:T(8,128)(2,1)S(1)} %get-tuple-element.35), channel_id=1, source_target_pairs={{0,8},{8,0},{16,24},{24,16},{1,9},{9,1},{17,25},{25,17},{2,10},{10... | collective-permute-start | bytes 1179656 | tf_op jit(solution)/shard_map/ppermute | solution.py:535
  23.2 0.5 %collective-permute-done.11 = f32[4,16]{1,0:T(4,128)S(1)} collective-permute-done((f32[4,16]{1,0:T(4,128)S(1)}, f32[4,16]{1,0:T(4,128)S(1)}, u32[]{:S(2)}, u32[]{:S(2)}) %collective-permute-start.11) | collective-permute-done | bytes 288 | tf_op jit(solution)/shard_map/ppermute | solution.py:501
  23.7 0.0 collective-permute-done.10
  23.7 3.7 %collective-permute-start.15 = (f32[4,16]{1,0:T(4,128)S(1)}, f32[4,16]{1,0:T(4,128)S(1)}, u32[]{:S(2)}, u32[]{:S(2)}) collective-permute-start(f32[4,16]{1,0:T(4,128)S(1)} %add_add_fusion.1), channel_id=1, source_target_pairs={{0,6},{1,7},{2,4},{3,5},{4,2},{5,3},{6,0},{7,1},{8,14},{9,15},{10,... | collective-permute-start | bytes 776 | tf_op jit(solution)/shard_map/ppermute | solution.py:501
  27.4 0.0 collective-permute-start.14
  27.4 2.7 %collective-permute-done.5.refs_1_ = bf16[2,32,2048]{2,1,0:T(8,128)(2,1)S(1)} collective-permute-done((bf16[2,32,2048]{2,1,0:T(8,128)(2,1)S(1)}, bf16[2,32,2048]{2,1,0:T(8,128)(2,1)S(1)}, u32[]{:S(2)}, u32[]{:S(2)}) %collective-permute-start.5) | collective-permute-done | bytes 262176 | tf_op jit(solution)/shard_map/ppermute | solution.py:535
  30.1 1.5 %collective-permute-start.13 = (f32[4,16]{1,0:T(4,128)S(1)}, f32[4,16]{1,0:T(4,128)S(1)}, u32[]{:S(2)}, u32[]{:S(2)}) collective-permute-start(f32[4,16]{1,0:T(4,128)S(1)} %add_add_fusion.1), channel_id=1, source_target_pairs={{0,2},{1,3},{2,0},{3,1},{4,6},{5,7},{6,4},{7,5},{8,10},{9,11},{10,... | collective-permute-start | bytes 776 | tf_op jit(solution)/shard_map/ppermute | solution.py:501
  31.5 0.0 collective-permute-done.4.refs_0_
  31.5 1.7 %scores_and_gradients.1 = (bf16[3,32,2048]{2,1,0:T(8,128)(2,1)S(1)}, bf16[32,2048]{1,0:T(8,128)(2,1)S(1)}, bf16[32,2048]{1,0:T(8,128)(2,1)S(1)}, bf16[32,2048]{1,0:T(8,128)(2,1)S(1)}) custom-call(f32[8,128]{1,0:T(8,128)S(1)} %pad.4.table, f32[64,128]{1,0:T(8,128)S(1)} %get-tuple-element.26.small, bf16[4,64,2048]{2,1,0:T(8,128)(2,1)S(1)} %fetch_mine.1.mine, ...), custom_call_target="tpu_custom_call" | custom-call | flops 1 | bytes 1 | tf_op jit(solution)/shard_map/scores_and_gradients/pallas_call | solution.py:541
  33.3 0.1 collective-permute-start.7
  33.4 0.0 collective-permute-done.15
  33.4 0.4 %collective-permute-start.8 = (bf16[32,2048]{1,0:T(8,128)(2,1)S(1)}, bf16[32,2048]{1,0:T(8,128)(2,1)S(1)}, u32[]{:S(2)}, u32[]{:S(2)}) collective-permute-start(bf16[32,2048]{1,0:T(8,128)(2,1)S(1)} %get-tuple-element.37), channel_id=1, source_target_pairs={{0,8},{8,0},{16,24},{24,16},{1,9},{9,1},{17,25},{25,17},{2,10},{10... | collective-permute-start | bytes 393224 | tf_op jit(solution)/shard_map/ppermute | solution.py:535
  33.9 0.0 collective-permute-done.14
  33.9 0.1 collective-permute-start.9
  34.0 0.0 collective-permute-done.13
  34.0 1.2 %collective-permute-start.16 = (f32[4,16]{1,0:T(4,128)S(1)}, f32[4,16]{1,0:T(4,128)S(1)}, u32[]{:S(2)}, u32[]{:S(2)}) collective-permute-start(f32[4,16]{1,0:T(4,128)S(1)} %add_add_fusion.refs_6_), channel_id=1, source_target_pairs={{0,16},{1,17},{2,18},{3,19},{4,20},{5,21},{6,22},{7,23},{8,24},{9,... | collective-permute-start | bytes 776 | tf_op jit(solution)/shard_map/ppermute | solution.py:517
  35.2 2.4 %collective-permute-done.16.refs_7_ = f32[4,16]{1,0:T(4,128)S(1)} collective-permute-done((f32[4,16]{1,0:T(4,128)S(1)}, f32[4,16]{1,0:T(4,128)S(1)}, u32[]{:S(2)}, u32[]{:S(2)}) %collective-permute-start.16) | collective-permute-done | bytes 288 | tf_op jit(solution)/shard_map/ppermute | solution.py:517
  37.6 0.0 collective-permute-done.7.refs_3_
  37.6 0.0 collective-permute-done.8.refs_4_
  37.6 0.0 collective-permute-done.9.refs_5_
  37.6 0.0 collective-permute-done.6.refs_2_
  37.6 1.3 %outputs.1 = (bf16[128,2048]{1,0:T(8,128)(2,1)}, bf16[128,2048]{1,0:T(8,128)(2,1)}, bf16[128,2048]{1,0:T(8,128)(2,1)}, f32[4,16]{1,0:T(4,128)}) custom-call(bf16[3,32,2048]{2,1,0:T(8,128)(2,1)S(1)} %get-tuple-element.31.refs_0_, bf16[3,32,2048]{2,1,0:T(8,128)(2,1)S(1)} %get-tuple-element.34.refs_1_, bf16[3,32,2048]{2,1,0:T(8,128)(2,1)S(1)} %collective-permute-done.6.refs_2_, ...), custom_call_target="tpu_custom_call" | custom-call | flops 1 | bytes 1 | tf_op jit(solution)/shard_map/outputs/pallas_call | solution.py:541
  (3 shorter events, 0.0 us)
Async XLA Ops:
  2.0 4.6 %collective-permute-start = (bf16[4,64,2048]{2,1,0:T(8,128)(2,1)S(1)}, bf16[4,64,2048]{2,1,0:T(8,128)(2,1)S(1)}, u32[]{:S(2)}, u32[]{:S(2)}) collective-permute-start(bf16[4,64,2048]{2,1,0:T(8,128)(2,1)S(1)} %get-tuple-element.25.theirs), channel_id=1, source_target_pairs={{0,8},{8,0},{16,24},{24,16},{1,9},{9,1},{17,25},{25,17},{2,10},{10... | collective-permute-start | bytes 3145736 | tf_op jit(solution)/shard_map/ppermute | solution.py:535
  2.6 9.3 %collective-permute-start.3 = (bf16[2,32,2048]{2,1,0:T(8,128)(2,1)S(1)}, bf16[2,32,2048]{2,1,0:T(8,128)(2,1)S(1)}, u32[]{:S(2)}, u32[]{:S(2)}) collective-permute-start(bf16[2,32,2048]{2,1,0:T(8,128)(2,1)S(1)} %get-tuple-element.24.after), channel_id=1, source_target_pairs={{0,24},{8,16},{16,8},{24,0},{1,25},{9,17},{17,9},{25,1},{2,26},{10... | collective-permute-start | bytes 786440 | tf_op jit(solution)/shard_map/ppermute | solution.py:535
  5.2 1.4 %copy-start = (f32[16,4]{0,1:T(4,128)S(1)}, f32[16,4]{0,1:T(4,128)}, u32[]{:S(2)}) copy-start(f32[16,4]{0,1:T(4,128)} %param.9) | copy-start | bytes 772
  8.1 7.4 %collective-permute-start.1 = (bf16[32,2304]{1,0:T(8,128)(2,1)S(1)}, bf16[32,2304]{1,0:T(8,128)(2,1)S(1)}, u32[]{:S(2)}, u32[]{:S(2)}) collective-permute-start(bf16[32,2304]{1,0:T(8,128)(2,1)S(1)} %get-tuple-element.28), channel_id=1, source_target_pairs={{0,16},{8,24},{16,0},{24,8},{1,17},{9,25},{17,1},{25,9},{2,18},{10... | collective-permute-start | bytes 442376 | tf_op jit(solution)/shard_map/ppermute | solution.py:535
  9.3 9.4 %collective-permute-start.2 = (bf16[32,2304]{1,0:T(8,128)(2,1)S(1)}, bf16[32,2304]{1,0:T(8,128)(2,1)S(1)}, u32[]{:S(2)}, u32[]{:S(2)}) collective-permute-start(bf16[32,2304]{1,0:T(8,128)(2,1)S(1)} %get-tuple-element.29), channel_id=1, source_target_pairs={{0,16},{8,24},{16,0},{24,8},{1,17},{9,25},{17,1},{25,9},{2,18},{10... | collective-permute-start | bytes 442376 | tf_op jit(solution)/shard_map/ppermute | solution.py:535
  10.2 21.3 %collective-permute-start.4 = (bf16[2,32,2304]{2,1,0:T(8,128)(2,1)S(1)}, bf16[2,32,2304]{2,1,0:T(8,128)(2,1)S(1)}, u32[]{:S(2)}, u32[]{:S(2)}) collective-permute-start(bf16[2,32,2304]{2,1,0:T(8,128)(2,1)S(1)} %get-tuple-element.32), channel_id=1, source_target_pairs={{0,16},{8,24},{16,0},{24,8},{1,17},{9,25},{17,1},{25,9},{2,18},{10... | collective-permute-start | bytes 884744 | tf_op jit(solution)/shard_map/ppermute | solution.py:535
  11.3 18.8 %collective-permute-start.5 = (bf16[2,32,2048]{2,1,0:T(8,128)(2,1)S(1)}, bf16[2,32,2048]{2,1,0:T(8,128)(2,1)S(1)}, u32[]{:S(2)}, u32[]{:S(2)}) collective-permute-start(bf16[2,32,2048]{2,1,0:T(8,128)(2,1)S(1)} %get-tuple-element.33), channel_id=1, source_target_pairs={{0,24},{8,16},{16,8},{24,0},{1,25},{9,17},{17,9},{25,1},{2,26},{10... | collective-permute-start | bytes 786440 | tf_op jit(solution)/shard_map/ppermute | solution.py:535
  19.5 3.1 %collective-permute-start.12 = (f32[4,16]{1,0:T(4,128)S(1)}, f32[4,16]{1,0:T(4,128)S(1)}, u32[]{:S(2)}, u32[]{:S(2)}) collective-permute-start(f32[4,16]{1,0:T(4,128)S(1)} %get-tuple-element.39), channel_id=1, source_target_pairs={{0,9},{1,8},{2,11},{3,10},{4,13},{5,12},{6,15},{7,14},{8,1},{9,0},... | collective-permute-start | bytes 776 | tf_op jit(solution)/shard_map/ppermute | solution.py:501
  20.1 3.6 %collective-permute-start.11 = (f32[4,16]{1,0:T(4,128)S(1)}, f32[4,16]{1,0:T(4,128)S(1)}, u32[]{:S(2)}, u32[]{:S(2)}) collective-permute-start(f32[4,16]{1,0:T(4,128)S(1)} %get-tuple-element.39), channel_id=1, source_target_pairs={{0,1},{1,0},{2,3},{3,2},{4,5},{5,4},{6,7},{7,6},{8,9},{9,8},{10,11... | collective-permute-start | bytes 776 | tf_op jit(solution)/shard_map/ppermute | solution.py:501
  21.6 2.1 %collective-permute-start.10 = (f32[4,16]{1,0:T(4,128)S(1)}, f32[4,16]{1,0:T(4,128)S(1)}, u32[]{:S(2)}, u32[]{:S(2)}) collective-permute-start(f32[4,16]{1,0:T(4,128)S(1)} %get-tuple-element.39), channel_id=1, source_target_pairs={{0,8},{1,9},{2,10},{3,11},{4,12},{5,13},{6,14},{7,15},{8,0},{9,1},... | collective-permute-start | bytes 776 | tf_op jit(solution)/shard_map/ppermute | solution.py:501
  22.5 15.1 %collective-permute-start.6 = (bf16[3,32,2048]{2,1,0:T(8,128)(2,1)S(1)}, bf16[3,32,2048]{2,1,0:T(8,128)(2,1)S(1)}, u32[]{:S(2)}, u32[]{:S(2)}) collective-permute-start(bf16[3,32,2048]{2,1,0:T(8,128)(2,1)S(1)} %get-tuple-element.35), channel_id=1, source_target_pairs={{0,8},{8,0},{16,24},{24,16},{1,9},{9,1},{17,25},{25,17},{2,10},{10... | collective-permute-start | bytes 1179656 | tf_op jit(solution)/shard_map/ppermute | solution.py:535
  23.7 9.7 %collective-permute-start.15 = (f32[4,16]{1,0:T(4,128)S(1)}, f32[4,16]{1,0:T(4,128)S(1)}, u32[]{:S(2)}, u32[]{:S(2)}) collective-permute-start(f32[4,16]{1,0:T(4,128)S(1)} %add_add_fusion.1), channel_id=1, source_target_pairs={{0,6},{1,7},{2,4},{3,5},{4,2},{5,3},{6,0},{7,1},{8,14},{9,15},{10,... | collective-permute-start | bytes 776 | tf_op jit(solution)/shard_map/ppermute | solution.py:501
  27.4 6.5 %collective-permute-start.14 = (f32[4,16]{1,0:T(4,128)S(1)}, f32[4,16]{1,0:T(4,128)S(1)}, u32[]{:S(2)}, u32[]{:S(2)}) collective-permute-start(f32[4,16]{1,0:T(4,128)S(1)} %add_add_fusion.1), channel_id=1, source_target_pairs={{0,4},{1,5},{2,6},{3,7},{4,0},{5,1},{6,2},{7,3},{8,12},{9,13},{10,... | collective-permute-start | bytes 776 | tf_op jit(solution)/shard_map/ppermute | solution.py:501
  30.1 3.9 %collective-permute-start.13 = (f32[4,16]{1,0:T(4,128)S(1)}, f32[4,16]{1,0:T(4,128)S(1)}, u32[]{:S(2)}, u32[]{:S(2)}) collective-permute-start(f32[4,16]{1,0:T(4,128)S(1)} %add_add_fusion.1), channel_id=1, source_target_pairs={{0,2},{1,3},{2,0},{3,1},{4,6},{5,7},{6,4},{7,5},{8,10},{9,11},{10,... | collective-permute-start | bytes 776 | tf_op jit(solution)/shard_map/ppermute | solution.py:501
  33.3 4.3 %collective-permute-start.7 = (bf16[32,2048]{1,0:T(8,128)(2,1)S(1)}, bf16[32,2048]{1,0:T(8,128)(2,1)S(1)}, u32[]{:S(2)}, u32[]{:S(2)}) collective-permute-start(bf16[32,2048]{1,0:T(8,128)(2,1)S(1)} %get-tuple-element.36), channel_id=1, source_target_pairs={{0,8},{8,0},{16,24},{24,16},{1,9},{9,1},{17,25},{25,17},{2,10},{10... | collective-permute-start | bytes 393224 | tf_op jit(solution)/shard_map/ppermute | solution.py:535
  33.4 4.2 %collective-permute-start.8 = (bf16[32,2048]{1,0:T(8,128)(2,1)S(1)}, bf16[32,2048]{1,0:T(8,128)(2,1)S(1)}, u32[]{:S(2)}, u32[]{:S(2)}) collective-permute-start(bf16[32,2048]{1,0:T(8,128)(2,1)S(1)} %get-tuple-element.37), channel_id=1, source_target_pairs={{0,8},{8,0},{16,24},{24,16},{1,9},{9,1},{17,25},{25,17},{2,10},{10... | collective-permute-start | bytes 393224 | tf_op jit(solution)/shard_map/ppermute | solution.py:535
  33.9 3.7 %collective-permute-start.9 = (bf16[32,2048]{1,0:T(8,128)(2,1)S(1)}, bf16[32,2048]{1,0:T(8,128)(2,1)S(1)}, u32[]{:S(2)}, u32[]{:S(2)}) collective-permute-start(bf16[32,2048]{1,0:T(8,128)(2,1)S(1)} %get-tuple-element.38), channel_id=1, source_target_pairs={{0,8},{8,0},{16,24},{24,16},{1,9},{9,1},{17,25},{25,17},{2,10},{10... | collective-permute-start | bytes 393224 | tf_op jit(solution)/shard_map/ppermute | solution.py:535
  34.0 3.6 %collective-permute-start.16 = (f32[4,16]{1,0:T(4,128)S(1)}, f32[4,16]{1,0:T(4,128)S(1)}, u32[]{:S(2)}, u32[]{:S(2)}) collective-permute-start(f32[4,16]{1,0:T(4,128)S(1)} %add_add_fusion.refs_6_), channel_id=1, source_target_pairs={{0,16},{1,17},{2,18},{3,19},{4,20},{5,21},{6,22},{7,23},{8,24},{9,... | collective-permute-start | bytes 776 | tf_op jit(solution)/shard_map/ppermute | solution.py:517

commit v2 on v1

--- a/solution.py
+++ b/solution.py
@@ -10,7 +10,6 @@
 
 LANES = 128
 TILE = 16
-COPY_ROWS = 16
 LITTLE = pl.CostEstimate(flops=1, bytes_accessed=1, transcendentals=0)
 CHUNKS = 2
 
@@ -209,19 +208,15 @@
     return jnp.where(my_place()[1] == 0, chunk, CHUNKS - 1 - chunk) * size
 
 
-def sent_start(chunk, size):
-    return jnp.where(my_place()[1] == 1, chunk, CHUNKS - 1 - chunk) * size
-
-
-def copy_rows(sources, start, out, sems, rows):
+def copy_chunks(sources, core, outs, sems):
+    size = outs[0].shape[1]
     copies = []
-    for j, ref in enumerate(sources):
-        for row in range(0, out.shape[1], rows):
+    for c, out in enumerate(outs):
+        start = pl.multiple_of(core * CHUNKS * size + chunk_start(c, size), TILE)
+        for j, ref in enumerate(sources):
             copies.append(
                 pltpu.make_async_copy(
-                    ref.at[pl.ds(pl.multiple_of(start + row, rows), rows)],
-                    out.at[j, pl.ds(row, rows)],
-                    sems.at[len(copies)],
+                    ref.at[pl.ds(start, size)], out.at[j], sems.at[len(copies)]
                 )
             )
     for copy in copies:
@@ -230,49 +225,61 @@
         copy.wait()
 
 
-def take_far(refs, row, outs):
+def take_far(refs, outs):
     chip = my_place()[1]
 
     def take(places):
         for out, place in zip(outs, places):
-            for step in range(0, out.shape[0], TILE):
-                out[step : step + TILE, : refs[place].shape[1]] = refs[place][
-                    tile_at(row + step), :
-                ]
+            for row in range(0, out.shape[0], TILE):
+                rows = slice(row, row + TILE)
+                out[rows, : refs[place].shape[1]] = refs[place][rows, :]
 
     pl.when(chip == 0)(lambda: take((1, 2)))
     pl.when(chip == 1)(lambda: take((0, 3)))
 
 
-def fetch_theirs_kernel(q, k, v, o, near, other, sems):
-    half, size = near.shape[1], other.shape[1]
-    copy_rows((q, k, v, o), (1 - my_place()[0]) * half, near, sems, COPY_ROWS)
-    take_far(planes(near), sent_start(0, size), planes(other))
-
-
-def fetch_mine_kernel(q, k, v, o, after, mine, sems):
-    copy_rows((q, k, v, o), my_place()[0] * mine.shape[1], mine, sems, COPY_ROWS)
-
-
-def split_wide(value):
-    parts = []
-    for _ in range(3):
-        part = value.astype(jnp.bfloat16)
-        value = value - part.astype(jnp.float32)
-        parts.append(part)
-    return parts
-
-
-def local_kernel(heads, scale, table, mine, near, theirs, small, out_bias, *outs):
-    others = outs[: CHUNKS - 1]
-    sames = [outs[CHUNKS - 1 : CHUNKS + 1]] + [planes(out) for out in outs[CHUNKS + 1 :]]
+def fetch_theirs_kernel(q, k, v, o, *refs):
+    nears, other, sems = refs[:CHUNKS], refs[CHUNKS], refs[CHUNKS + 1]
+    copy_chunks((q, k, v, o), 1 - my_place()[0], nears, sems)
+    take_far(planes(nears[CHUNKS - 1]), planes(other))
+
+
+def fetch_mine_kernel(q, k, v, o, after, *refs):
+    copy_chunks((q, k, v, o), my_place()[0], refs[:-1], refs[-1])
+
+
+def packed_small(value, heads):
+    used = 6 * heads
+    place = lax.broadcasted_iota(jnp.int32, value.shape, 1)
+    high = value.astype(jnp.bfloat16).astype(jnp.float32)
+    middle = (value - high).astype(jnp.bfloat16).astype(jnp.float32)
+    rest = (value - high) - middle
+    first = jnp.where(place < used, high, pltpu.roll(rest, used, axis=1))
+    second = jnp.where(place < used, middle, pltpu.roll(rest, 2 * used - LANES, axis=1))
+    return first.astype(jnp.bfloat16), second.astype(jnp.bfloat16)
+
+
+def unpacked_small(first, second, heads):
+    used = 6 * heads
+    first, second = first.astype(jnp.float32), second.astype(jnp.float32)
+    place = lax.broadcasted_iota(jnp.int32, first.shape, 1)
+    rest = jnp.where(
+        place < LANES - used,
+        pltpu.roll(first, LANES - used, axis=1),
+        pltpu.roll(second, 2 * (LANES - used), axis=1),
+    )
+    return first + second + jnp.where(place < 3 * heads, rest, 0.0)
+
+
+def local_kernel(heads, scale, table, *refs):
+    mines, nears, theirs, refs = refs[:2], refs[2:4], refs[4], refs[5:]
+    smalls, out_bias, other, sames = refs[:2], refs[2], refs[3], (refs[4:6], planes(refs[6]))
     core, chip = my_place()
-    half, size, width = mine.shape[1], sames[0][0].shape[0], mine.shape[2]
-    own, other = shifted(planes(mine), 0), shifted(planes(near), 0)
+    size, width = mines[0].shape[1:]
     offset = [table[d : d + 1, :] for d in range(4)]
     out_bias[...] = jnp.zeros_like(out_bias)
 
-    def run(a, b):
+    def run(a, b, small):
         def tile(row):
             at, bt = tiles_of(a, row), tiles_of(b, row)
             held = pair_dots(
@@ -286,23 +293,21 @@
             lines = bias_lines([[d0[0], d1[1]], [d1[0]], [], []])
             out_bias[...] += jnp.where(chip == 0, lines, jnp.zeros_like(lines))
 
-        over_tiles(half, tile)
-
-    pl.when(core == 0)(lambda: run(own, other))
-    pl.when(core == 1)(lambda: run(other, own))
-
-    for c, out in enumerate(others):
-        take_far(planes(theirs), sent_start(c + 1, size), planes(out))
+        over_tiles(size, tile)
+
+    for mine, near, small in zip(mines, nears, smalls):
+        own, neighbour = shifted(planes(mine), 0), shifted(planes(near), 0)
+        pl.when(core == 0)(functools.partial(run, own, neighbour, small))
+        pl.when(core == 1)(functools.partial(run, neighbour, own, small))
+
+    take_far(planes(theirs), planes(other))
     for c, out in enumerate(sames):
-        start = sent_start(c, size)
-        take_far(planes(mine), start, out)
-        for step in range(0, size, TILE):
-            parts = split_wide(small[tile_at(start + step), :])
-            rows = slice(step, step + TILE)
-            out[0][rows, width : width + LANES] = parts[0]
-            out[0][rows, width + LANES :] = parts[1]
-            out[1][rows, width : width + LANES] = parts[2]
-            out[1][rows, width + LANES :] = jnp.zeros((TILE, LANES), jnp.bfloat16)
+        take_far(planes(mines[1 - c]), out)
+        for row in range(0, size, TILE):
+            rows = slice(row, row + TILE)
+            parts = packed_small(smalls[1 - c][rows, :], heads)
+            for ref, part in zip(sames[0], parts):
+                ref[rows, width + c * LANES : width + (c + 1) * LANES] = part
 
 
 EARLY, LATE = 14, 10
@@ -384,11 +389,11 @@
     return tuple(ref.at[j] for j in range(ref.shape[0]))
 
 
-def frames_of(mine, near, far, start):
+def frames_of(mine, near, far):
     *same, other = far
     return (
-        shifted(planes(mine), start) + shifted(pair_of(same), 0),
-        shifted(planes(near), start) + shifted(planes(other), 0),
+        shifted(planes(mine) + pair_of(same), 0),
+        shifted(planes(near) + planes(other), 0),
     )
 
 
@@ -396,40 +401,48 @@
     return tuple(same) if len(same) == 2 else planes(same[0])
 
 
-def far_small(far, rows, width):
-    first, second = pair_of(far[:-1])
-    parts = [first[rows, width : width + LANES], first[rows, width + LANES :]]
-    parts += [second[rows, width : width + LANES]]
-    return functools.reduce(jnp.add, [part.astype(jnp.float32) for part in parts])
-
-
-def score_kernel(heads, scale, chunk, table, small, bias, mine, near, *refs):
-    *far, out_items, out_bias, lines_ref = refs
-    size, width = out_items.shape[1], mine.shape[2]
-    start = chunk_start(chunk, size)
+def far_small(far, rows, width, heads, chunk):
+    at = slice(width + chunk * LANES, width + (chunk + 1) * LANES)
+    return unpacked_small(*(ref[rows, at] for ref in pair_of(far[:-1])), heads)
+
+
+def score_kernel(heads, scale, table, small, bias, mine, near, *refs):
+    far, (out_items, out_shares, out_small), lines_ref = refs[:3], refs[3:6], refs[6]
+    size, width = mine.shape[1:]
     lines_ref[...] = bias[...]
 
     def work(chip, a, b):
         def tile(row):
+            rows = tile_at(row)
             items, lines = score_tile(
                 heads, scale, chip, tiles_of(a, row), tiles_of(b, row), table,
-                small[tile_at(start + row), :], far_small(far, tile_at(row), width),
+                small[rows, :], far_small(far, rows, width, heads, 0),
             )
+            out_small[rows, :] = far_small(far, rows, width, heads, 1)
             for j, item in enumerate(items):
-                out_items[j, tile_at(row), :] = item
+                out_items[j, rows, :] = item
             lines_ref[...] += lines
 
         over_tiles(size, tile)
 
-    with_frames(*frames_of(mine, near, far, start), work)
-    out_bias[...] = lines_ref[: out_bias.shape[0], : out_bias.shape[1]]
-
-
-def gradient_kernel(heads, scale, chunk, items_ref, mine, near, *refs):
-    *far, out_own, out_other = refs
-    size = out_own.shape[1]
-    own, neighbour = frames_of(mine, near, far, chunk_start(chunk, size))
-    own_out, other_out = shifted(planes(out_own), 0), shifted(planes(out_other), 0)
+    with_frames(*frames_of(mine, near, far), work)
+    for j in range(out_shares.shape[0]):
+        out_shares[j] = lines_ref[: out_shares.shape[1], :]
+
+
+def output_copies(which, piece, outs, chunk, sems, at):
+    size = piece[0].shape[0]
+    start = pl.multiple_of(which * CHUNKS * size + chunk_start(chunk, size), TILE)
+    return [
+        pltpu.make_async_copy(part, out.at[pl.ds(start, size)], sems.at[at + j])
+        for j, (part, out) in enumerate(zip(piece, outs))
+    ]
+
+
+def gradient_kernel(heads, scale, items_ref, mine, near, *refs):
+    far, out_other, outs, kept, sems = refs[:3], refs[3], refs[4:7], refs[7], refs[8]
+    own, neighbour = frames_of(mine, near, far)
+    own_out, other_out = shifted(planes(kept), 0), shifted(planes(out_other), 0)
 
     def work(chip, a, b):
         out_a, out_b = (own_out, other_out) if a is own else (other_out, own_out)
@@ -441,80 +454,55 @@
                 tiles_of(out_a, row), tiles_of(out_b, row),
             )
 
-        over_tiles(size, tile)
+        over_tiles(mine.shape[1], tile)
 
     with_frames(own, neighbour, work)
-
-
-def whole_kernel(heads, scale, chunk, table, small, mine, near, *refs):
-    *far, out_own = refs[:-3]
-    out_others = refs[-3:]
-    size, width = out_own.shape[1], mine.shape[2]
-    start = chunk_start(chunk, size)
-    own, neighbour = frames_of(mine, near, far, start)
+    copies = output_copies(my_place()[0], planes(kept), outs, 0, sems, 0)
+    for copy in copies:
+        copy.start()
+    for copy in copies:
+        copy.wait()
+
+
+def whole_kernel(heads, scale, table, small, small_far, mine, near, *refs):
+    far, out_own, out_others = refs[:2], refs[2], refs[3:6]
+    own, neighbour = frames_of(mine, near, far)
     own_out, other_out = shifted(planes(out_own), 0), shifted(out_others, 0)
 
     def work(chip, a, b):
         out_a, out_b = (own_out, other_out) if a is own else (other_out, own_out)
 
         def tile(row):
-            at, bt = tiles_of(a, row), tiles_of(b, row)
+            at, bt, rows = tiles_of(a, row), tiles_of(b, row), tile_at(row)
             items, _ = score_tile(
-                heads, scale, chip, at, bt, table,
-                small[tile_at(start + row), :], far_small(far, tile_at(row), width),
+                heads, scale, chip, at, bt, table, small[rows, :], small_far[rows, :]
             )
             gradient_tile(
                 heads, scale, chip, at, bt, items, tiles_of(out_a, row), tiles_of(out_b, row)
             )
 
-        over_tiles(size, tile)
+        over_tiles(mine.shape[1], tile)
 
     with_frames(own, neighbour, work)
 
 
 def output_kernel(*refs):
-    kept, refs = refs[:CHUNKS], refs[CHUNKS:]
-    *backs, left, right = refs[:-6]
-    outs, (out_bias, total, sems) = refs[-6:-3], refs[-3:]
-    backs = [planes(backs[0])] + [backs[j : j + 3] for j in range(1, len(backs), 3)]
-    size = kept[0].shape[1]
-    half = CHUNKS * size
+    first_back, kept, back, shares = planes(refs[0]), planes(refs[1]), refs[2:5], refs[5]
+    outs, out_bias, total, sems = refs[9:12], *refs[12:]
     core = my_place()[0]
-    total[...] = left[...] + right[...]
-    copies = [pltpu.make_async_copy(total, out_bias, sems.at[0])]
-    for c in range(CHUNKS):
-        for which, piece in ((core, planes(kept[c])), (1 - core, backs[c])):
-            start = pl.multiple_of(which * half + chunk_start(c, size), TILE)
-            for part, out in zip(piece, outs):
-                copies.append(
-                    pltpu.make_async_copy(part, out.at[pl.ds(start, size)], sems.at[len(copies)])
-                )
+    copies = output_copies(1 - core, first_back, outs, 0, sems, 0)
+    copies += output_copies(core, kept, outs, 1, sems, 3)
+    copies += output_copies(1 - core, back, outs, 1, sems, 6)
     for copy in copies:
         copy.start()
+    parts = [shares[j] for j in range(shares.shape[0])]
+    while len(parts) > 1:
+        parts = [a + b for a, b in zip(parts[::2], parts[1::2])]
+    total[...] = parts[0][: total.shape[0], : total.shape[1]]
+    copies.append(pltpu.make_async_copy(total, out_bias, sems.at[9]))
+    copies[-1].start()
     for copy in copies:
         copy.wait()
-
-
-def four_way(value, axes, masks, count):
-    first, second = masks
-    got = [
-        lax.ppermute(value, axes, [(i, i ^ mask) for i in range(count)])
-        for mask in (first, second, first ^ second)
-    ]
-    return (value + got[0]) + (got[1] + got[2])
-
-
-def sum_group(value, sizes):
-    axes = tuple(axis for axis, _ in sizes)
-    (_, tm), (_, patch) = sizes
-    count = tm * patch
-    masks = [patch] + [1 << j for j in range(patch.bit_length() - 1)] + [2 * patch]
-    while len(masks) > 2:
-        value = four_way(value, axes, masks[:2], count)
-        masks = masks[2:]
-    if len(masks) == 2:
-        value = value + lax.ppermute(value, axes, [(i, i ^ masks[0]) for i in range(count)])
-    return value, lax.ppermute(value, axes, [(i, i ^ masks[-1]) for i in range(count)])
 
 
 def by_chips(query_vectors, key_vectors, value_vectors, grad_output, time_bias, sizes):
@@ -537,78 +525,91 @@
     def shape(*dims, dtype=jnp.bfloat16):
         return jax.ShapeDtypeStruct(dims, dtype)
 
-    def call(kernel, name, out_shape, *args, scratch=(), hbm=0, out_spec=vmem_spec):
+    def call(kernel, name, out_shape, *args, scratch=(), hbm=(), hbm_out=(), aliases={}):
         return pl.pallas_call(
             kernel,
-            in_specs=[any_spec] * hbm + [vmem_spec] * (len(args) - hbm),
-            out_specs=[out_spec] * len(out_shape),
+            in_specs=[any_spec if j in hbm else vmem_spec for j in range(len(args))],
+            out_specs=[any_spec if j in hbm_out else vmem_spec for j in range(len(out_shape))],
             out_shape=out_shape,
             scratch_shapes=scratch,
+            input_output_aliases=aliases,
             compiler_params=pltpu.CompilerParams(vmem_limit_bytes=16 * 2**20),
             cost_estimate=LITTLE,
             name=name,
         )(*args)
 
     wide = jnp.float32
-    copies = [pltpu.SemaphoreType.DMA((4 * half // COPY_ROWS,))]
-    far_shape, same_shape = shape(2, size, width), shape(2, size, width + 2 * LANES)
+    lines = shape(8, LANES, dtype=wide)
+    chunk_shape, far_shape = shape(4, size, width), shape(2, size, width)
+    copies = [pltpu.SemaphoreType.DMA((4 * CHUNKS,))]
     table = jnp.pad(time_bias.T, ((0, 8 - frames), (0, LANES - heads)))
-    theirs, other = call(
-        fetch_theirs_kernel, "fetch_theirs", [shape(4, half, width), far_shape], *own,
-        scratch=copies, hbm=4,
-    )
-    near = swap(theirs, 1)
+
+    *theirs, other = call(
+        fetch_theirs_kernel, "fetch_theirs", [chunk_shape] * CHUNKS + [far_shape], *own,
+        scratch=copies, hbm=range(4),
+    )
+    nears = [swap(x, 1) for x in theirs]
     others = [swap(other, 3)]
-    (mine,) = call(
-        fetch_mine_kernel, "fetch_mine", [shape(4, half, width)], *own, other, scratch=copies, hbm=5
-    )
-    small, bias, *sent = call(
+    mines = call(
+        fetch_mine_kernel, "fetch_mine", [chunk_shape] * CHUNKS, *own, other,
+        scratch=copies, hbm=range(5),
+    )
+
+    *smalls, bias, other, same_first, same_second, same = call(
         functools.partial(local_kernel, heads, scale),
         "local_scores",
-        [shape(half, LANES, dtype=wide), shape(8, LANES, dtype=wide)]
-        + [far_shape] * (CHUNKS - 1)
-        + [shape(size, width + 2 * LANES)] * 2
-        + [same_shape] * (CHUNKS - 1),
-        table, mine, near, theirs,
-    )
-    sames = [[swap(x, 2) for x in sent[CHUNKS - 1 : CHUNKS + 1]]]
-    sames += [[swap(x, 2)] for x in sent[CHUNKS + 1 :]]
-    others += [swap(x, 3) for x in sent[: CHUNKS - 1]]
-
-    kept, backs = [], []
-    pieces = [shape(3, size, width)] * 2
-    for c in range(CHUNKS):
-        arrays = (mine, near, *sames[c], others[c])
-        if c == 0:
-            items, bias = call(
-                functools.partial(score_kernel, heads, scale, c),
-                "scores",
-                [shape(EARLY, size, LANES), shape(frames, heads, dtype=wide)],
-                table, small, bias, *arrays,
-                scratch=[pltpu.VMEM((8, LANES), wide)],
-            )
-            bias = sum_group(bias, sizes)
-            piece, *back = call(
-                functools.partial(gradient_kernel, heads, scale, c), "gradients", pieces,
-                items, *arrays,
-            )
-        else:
-            piece, *back = call(
-                functools.partial(whole_kernel, heads, scale, c), "scores_and_gradients",
-                pieces[:1] + [shape(size, width)] * 3, table, small, *arrays,
-            )
-        kept.append(piece)
-        backs.append([swap(x, 1) for x in back])
+        [shape(size, LANES, dtype=wide)] * CHUNKS
+        + [lines, far_shape]
+        + [shape(size, width + CHUNKS * LANES)] * 2
+        + [far_shape],
+        table, *mines, *nears, theirs[0],
+    )
+    sames = [[swap(same_first, 2), swap(same_second, 2)], [swap(same, 2)]]
+    others.append(swap(other, 3))
+
+    whole = pltpu.HBM((rows, width), jnp.bfloat16)
+    stack, piece = shape(3, size, width), shape(size, width)
+    output_sems = pltpu.SemaphoreType.DMA((10,))
+    first = (mines[0], nears[0], *sames[0], others[0])
+    items, shares, small_far = call(
+        functools.partial(score_kernel, heads, scale),
+        "scores",
+        [
+            shape(EARLY, size, LANES),
+            shape(math.prod(count for _, count in sizes), 8, LANES, dtype=wide),
+            shape(size, LANES, dtype=wide),
+        ],
+        table, smalls[0], bias, *first,
+        scratch=[pltpu.VMEM((8, LANES), wide)],
+    )
+    shares = lax.all_to_all(shares, tuple(axis for axis, _ in sizes), 0, 0, tiled=True)
+    back, *grads = call(
+        functools.partial(gradient_kernel, heads, scale),
+        "gradients",
+        [stack] + [whole] * 3,
+        items, *first,
+        scratch=[pltpu.VMEM((3, size, width), jnp.bfloat16), output_sems],
+        hbm_out=range(1, 4),
+    )
+    first_back = swap(back, 1)
+
+    kept, *back = call(
+        functools.partial(whole_kernel, heads, scale),
+        "scores_and_gradients",
+        [stack] + [piece] * 3,
+        table, smalls[1], small_far, mines[1], nears[1], *sames[1], others[1],
+    )
+    back = [swap(x, 1) for x in back]
+    grads = [pltpu.with_memory_space_constraint(x, pltpu.HBM) for x in grads]
     *grads, bias = call(
         output_kernel,
         "outputs",
-        [shape(rows, width)] * 3 + [shape(frames, heads, dtype=wide)],
-        *kept, *(x for back in backs for x in back), *bias,
-        scratch=[
-            pltpu.VMEM((frames, heads), wide),
-            pltpu.SemaphoreType.DMA((1 + 6 * CHUNKS,)),
-        ],
-        out_spec=any_spec,
+        [whole] * 3 + [shape(frames, heads, dtype=wide)],
+        first_back, kept, *back, shares, *grads,
+        scratch=[pltpu.VMEM((frames, heads), wide), output_sems],
+        hbm=range(6, 9),
+        hbm_out=range(4),
+        aliases={6 + j: j for j in range(3)},
     )
     return (*[x.reshape(query_vectors.shape) for x in grads], bias.T)
 
@@ -623,7 +624,7 @@
             and frames == 4
             and args[0].shape[1] == 1
             and heads * LANES == args[0].shape[3]
-            and heads * 6 <= LANES
+            and 3 * heads <= 2 * (LANES - 6 * heads)
             and heads % 2 == 0
             and args[0].shape[0] * args[0].shape[2] % (2 * TILE * CHUNKS) == 0
             and mesh.shape["patch"].bit_count() == 1

time: 39.1 us -> 37.3 us (0.954)
  starting transfers between devices: 16.2 us -> 13.3 us
  Pallas kernels: 8.85 us -> 10.3 us
  waiting for transfers between devices: 13.1 us -> 12.7 us
    ppermute x7 -> x0, starting transfers between devices: 8.55 us -> none  [the longest x6 7.33 us: four_way(): lax.ppermute(value, axes, [(i, i ^ mask) for i in range(count)])]
    all_to_all x0 -> x1, starting transfers between devices: none -> 6 us  [by_chips(): lax.all_to_all(shares, tuple((axis for axis, _ in sizes)), 0, 0, tiled=True)]
    ppermute x7 -> x0, waiting for transfers between devices: 3.04 us -> none  [the longest x1 2.42 us: sum_group(): lax.ppermute(value, axes, [(i, i ^ masks[-1]) for i in range(count)])]
    all_to_all x0 -> x1, waiting for transfers between devices: none -> 2.93 us  [by_chips(): lax.all_to_all(shares, tuple((axis for axis, _ in sizes)), 0, 0, tiled=True)]
    pallas_call x7, Pallas kernels: 8.85 us -> 10.3 us  [call(): pl.pallas_call(kernel, in_specs=[any_spec if j in hbm else vmem_spec for...]
    ppermute x10 -> x11, starting transfers between devices: 7.66 us -> 7.29 us  [swap(): return lax.ppermute(x, 'tm', [(i, i ^ bits) for i in range(4)])]
    ppermute x10 -> x11, waiting for transfers between devices: 10 us -> 9.78 us  [swap(): return lax.ppermute(x, 'tm', [(i, i ^ bits) for i in range(4)])]
  transfers between devices with their start and end apart: 17 -> 12, of which waited for: 7 -> 8; matrix products, arithmetic and copies ran while one was open for 0% -> 0% of each run, Pallas kernels for 16% -> 21%
where the time goes in v2:
time: 37.3 us; the launch traced here: 37 us
  starting transfers between devices  13.3 us (36%)
  waiting for transfers between devices  12.7 us (34%)
  Pallas kernels  10.3 us (28%)
  between operations  0.73 us (2%)
    pallas_call x7, Pallas kernels, call(): pl.pallas_call(kernel, in_specs=[any_spec if j in hbm else vmem_spec for...  10.3 us
    ppermute x11, waiting for transfers between devices, swap(): return lax.ppermute(x, 'tm', [(i, i ^ bits) for i in range(4)])  9.78 us
    ppermute x11, starting transfers between devices, swap(): return lax.ppermute(x, 'tm', [(i, i ^ bits) for i in range(4)])  7.29 us
    all_to_all x1, starting transfers between devices, by_chips(): lax.all_to_all(shares, tuple((axis for axis, _ in sizes)), 0, 0, tiled=True)  6 us
    all_to_all x1, waiting for transfers between devices, by_chips(): lax.all_to_all(shares, tuple((axis for axis, _ in sizes)), 0, 0, tiled=True)  2.93 us
  transfers between devices with their start and end apart: 12, of which 8 were waited for; matrix products, arithmetic and copies ran while one was open for 0% of the time, Pallas kernels for 21%

profile of v2, /device:TPU:0, one launch (start us, length us, event | category | flops | bytes accessed | tf_op | source)
XLA Modules:
  0.0 37.0 jit_solution(18219220826253003691)
XLA Ops:
  0.6 1.4 %fetch_theirs.1 = (bf16[4,32,2048]{2,1,0:T(8,128)(2,1)S(1)}, bf16[4,32,2048]{2,1,0:T(8,128)(2,1)S(1)}, bf16[2,32,2048]{2,1,0:T(8,128)(2,1)S(1)}) custom-call(bf16[128,2048]{1,0:T(8,128)(2,1)} %bitcast.15, bf16[128,2048]{1,0:T(8,128)(2,1)} %bitcast.17, bf16[128,2048]{1,0:T(8,128)(2,1)} %bitcast.19, bf16[128,2048]{1,0:T(8,128)(2,1)} %bitcast.21), custom_call_target="tpu_custom_call" | custom-call | flops 1 | bytes 1 | tf_op jit(solution)/shard_map/fetch_theirs/pallas_call | solution.py:529
  2.0 0.5 %collective-permute-start = (bf16[4,32,2048]{2,1,0:T(8,128)(2,1)S(1)}, bf16[4,32,2048]{2,1,0:T(8,128)(2,1)S(1)}, u32[]{:S(2)}, u32[]{:S(2)}) collective-permute-start(bf16[4,32,2048]{2,1,0:T(8,128)(2,1)S(1)} %get-tuple-element.34.refs_4_), channel_id=1, source_target_pairs={{0,8},{8,0},{16,24},{24,16},{1,9},{9,1},{17,25},{25,17},{2,10},{10... | collective-permute-start | bytes 1572872 | tf_op jit(solution)/shard_map/ppermute | solution.py:523
  2.5 0.1 collective-permute-start.1
  2.6 2.6 %collective-permute-start.4 = (bf16[2,32,2048]{2,1,0:T(8,128)(2,1)S(1)}, bf16[2,32,2048]{2,1,0:T(8,128)(2,1)S(1)}, u32[]{:S(2)}, u32[]{:S(2)}) collective-permute-start(bf16[2,32,2048]{2,1,0:T(8,128)(2,1)S(1)} %get-tuple-element.31.after), channel_id=1, source_target_pairs={{0,24},{8,16},{16,8},{24,0},{1,25},{9,17},{17,9},{25,1},{2,26},{10... | collective-permute-start | bytes 786440 | tf_op jit(solution)/shard_map/ppermute | solution.py:523
  5.3 0.0 copy-start
  5.3 1.4 %fetch_mine.1 = (bf16[4,32,2048]{2,1,0:T(8,128)(2,1)S(1)}, bf16[4,32,2048]{2,1,0:T(8,128)(2,1)S(1)}) custom-call(bf16[128,2048]{1,0:T(8,128)(2,1)} %bitcast.16, bf16[128,2048]{1,0:T(8,128)(2,1)} %bitcast.18, bf16[128,2048]{1,0:T(8,128)(2,1)} %bitcast.20, bf16[128,2048]{1,0:T(8,128)(2,1)} %bitcast.22, bf16[2,32,2048]{2,1,0:T(8,128)(2,1)S(1)} %get-tuple-element.31.after), custom_call_target="tpu_custom_call" | custom-call | flops 1 | bytes 1 | tf_op jit(solution)/shard_map/fetch_mine/pallas_call | solution.py:529
  6.6 0.0 copy-done
  6.6 0.0 collective-permute-done.refs_2_.near
  6.7 0.0 collective-permute-done.1.refs_3_.near
  6.7 1.6 %local_scores.1 = (f32[32,128]{1,0:T(8,128)S(1)}, f32[32,128]{1,0:T(8,128)S(1)}, f32[8,128]{1,0:T(8,128)S(1)}, bf16[2,32,2048]{2,1,0:T(8,128)(2,1)S(1)}, bf16[32...) custom-call(f32[8,128]{1,0:T(8,128)S(1)} %pad.4.table, ...), custom_call_target="tpu_custom_call" | custom-call | flops 1 | bytes 1 | tf_op jit(solution)/shard_map/local_scores/pallas_call | solution.py:529
  8.3 1.0 %collective-permute-start.2 = (bf16[32,2304]{1,0:T(8,128)(2,1)S(1)}, bf16[32,2304]{1,0:T(8,128)(2,1)S(1)}, u32[]{:S(2)}, u32[]{:S(2)}) collective-permute-start(bf16[32,2304]{1,0:T(8,128)(2,1)S(1)} %get-tuple-element.38), channel_id=1, source_target_pairs={{0,16},{8,24},{16,0},{24,8},{1,17},{9,25},{17,1},{25,9},{2,18},{10... | collective-permute-start | bytes 442376 | tf_op jit(solution)/shard_map/ppermute | solution.py:523
  9.3 1.0 %collective-permute-start.3 = (bf16[32,2304]{1,0:T(8,128)(2,1)S(1)}, bf16[32,2304]{1,0:T(8,128)(2,1)S(1)}, u32[]{:S(2)}, u32[]{:S(2)}) collective-permute-start(bf16[32,2304]{1,0:T(8,128)(2,1)S(1)} %get-tuple-element.39), channel_id=1, source_target_pairs={{0,16},{8,24},{16,0},{24,8},{1,17},{9,25},{17,1},{25,9},{2,18},{10... | collective-permute-start | bytes 442376 | tf_op jit(solution)/shard_map/ppermute | solution.py:523
  10.3 1.0 %collective-permute-start.6 = (bf16[2,32,2048]{2,1,0:T(8,128)(2,1)S(1)}, bf16[2,32,2048]{2,1,0:T(8,128)(2,1)S(1)}, u32[]{:S(2)}, u32[]{:S(2)}) collective-permute-start(bf16[2,32,2048]{2,1,0:T(8,128)(2,1)S(1)} %get-tuple-element.44), channel_id=1, source_target_pairs={{0,16},{8,24},{16,0},{24,8},{1,17},{9,25},{17,1},{25,9},{2,18},{10... | collective-permute-start | bytes 786440 | tf_op jit(solution)/shard_map/ppermute | solution.py:523
  11.3 0.2 collective-permute-start.7
  11.5 0.4 %collective-permute-done.4.refs_2_ = bf16[2,32,2048]{2,1,0:T(8,128)(2,1)S(1)} collective-permute-done((bf16[2,32,2048]{2,1,0:T(8,128)(2,1)S(1)}, bf16[2,32,2048]{2,1,0:T(8,128)(2,1)S(1)}, u32[]{:S(2)}, u32[]{:S(2)}) %collective-permute-start.4) | collective-permute-done | bytes 262176 | tf_op jit(solution)/shard_map/ppermute | solution.py:523
  12.0 3.9 %collective-permute-done.2.refs_0_ = bf16[32,2304]{1,0:T(8,128)(2,1)S(1)} collective-permute-done((bf16[32,2304]{1,0:T(8,128)(2,1)S(1)}, bf16[32,2304]{1,0:T(8,128)(2,1)S(1)}, u32[]{:S(2)}, u32[]{:S(2)}) %collective-permute-start.2) | collective-permute-done | bytes 147488 | tf_op jit(solution)/shard_map/ppermute | solution.py:523
  15.8 3.2 %collective-permute-done.3.refs_1_ = bf16[32,2304]{1,0:T(8,128)(2,1)S(1)} collective-permute-done((bf16[32,2304]{1,0:T(8,128)(2,1)S(1)}, bf16[32,2304]{1,0:T(8,128)(2,1)S(1)}, u32[]{:S(2)}, u32[]{:S(2)}) %collective-permute-start.3) | collective-permute-done | bytes 147488 | tf_op jit(solution)/shard_map/ppermute | solution.py:523
  19.0 1.5 %scores.1 = (bf16[14,32,128]{2,1,0:T(8,128)(2,1)S(1)}, f32[32,8,128]{2,1,0:T(8,128)}, f32[32,128]{1,0:T(8,128)S(1)}) custom-call(f32[8,128]{1,0:T(8,128)S(1)} %pad.4.table, f32[32,128]{1,0:T(8,128)S(1)} %get-tuple-element.36.small, f32[8,128]{1,0:T(8,128)S(1)} %get-tuple-element.37.bias, bf16[4,32,2048]{2,1,0:T(8,128)(2,1)S(1)} %get-tuple-element.32.refs_0_.mine, ...), custom_call_target="tpu_custom_call" | custom-call | flops 1 | bytes 1 | tf_op jit(solution)/shard_map/scores/pallas_call | solution.py:529
  20.5 1.6 %gradients.1 = (bf16[3,32,2048]{2,1,0:T(8,128)(2,1)S(1)}, bf16[128,2048]{1,0:T(8,128)(2,1)}, bf16[128,2048]{1,0:T(8,128)(2,1)}, bf16[128,2048]{1,0:T(8,128)(2,1)}) custom-call(bf16[14,32,128]{2,1,0:T(8,128)(2,1)S(1)} %get-tuple-element.40.items_ref, bf16[4,32,2048]{2,1,0:T(8,128)(2,1)S(1)} %get-tuple-element.32.refs_0_.mine, ...), custom_call_target="tpu_custom_call" | custom-call | flops 1 | bytes 1 | tf_op jit(solution)/shard_map/gradients/pallas_call | solution.py:529
  22.1 0.1 collective-permute-start.5
  22.2 6.0 %all-to-all-start = ((f32[32,8,128]{2,1,0:T(8,128)}), f32[32,8,128]{2,1,0:T(8,128)S(1)}, u32[]{:S(2)}, u32[]{:S(2)}) async-start(f32[32,8,128]{2,1,0:T(8,128)} %get-tuple-element.50), calls=%async_computation | async-start | bytes 262144 | tf_op jit(solution)/shard_map/all_to_all | solution.py:585
  28.2 0.0 collective-permute-done.6.refs_0_
  28.2 1.1 %collective-permute-done.7.refs_1_ = bf16[2,32,2048]{2,1,0:T(8,128)(2,1)S(1)} collective-permute-done((bf16[2,32,2048]{2,1,0:T(8,128)(2,1)S(1)}, bf16[2,32,2048]{2,1,0:T(8,128)(2,1)S(1)}, u32[]{:S(2)}, u32[]{:S(2)}) %collective-permute-start.7) | collective-permute-done | bytes 262176 | tf_op jit(solution)/shard_map/ppermute | solution.py:523
  29.3 1.7 %scores_and_gradients.1 = (bf16[3,32,2048]{2,1,0:T(8,128)(2,1)S(1)}, bf16[32,2048]{1,0:T(8,128)(2,1)S(1)}, bf16[32,2048]{1,0:T(8,128)(2,1)S(1)}, bf16[32,2048]{1,0:T(8,128)(2,1)S(1)}) custom-call(f32[8,128]{1,0:T(8,128)S(1)} %pad.4.table, f32[32,128]{1,0:T(8,128)S(1)} %get-tuple-element.42.small, f32[32,128]{1,0:T(8,128)S(1)} %get-tuple-element.43.small_far, ...), custom_call_target="tpu_custom_call" | custom-call | flops 1 | bytes 1 | tf_op jit(solution)/shard_map/scores_and_gradients/pallas_call | solution.py:529
  31.1 0.2 collective-permute-start.10
  31.3 0.4 collective-permute-start.8
  31.7 0.2 collective-permute-start.9
  31.8 0.7 %collective-permute-done.10.refs_4_ = bf16[32,2048]{1,0:T(8,128)(2,1)S(1)} collective-permute-done((bf16[32,2048]{1,0:T(8,128)(2,1)S(1)}, bf16[32,2048]{1,0:T(8,128)(2,1)S(1)}, u32[]{:S(2)}, u32[]{:S(2)}) %collective-permute-start.10) | collective-permute-done | bytes 131104 | tf_op jit(solution)/shard_map/ppermute | solution.py:523
  32.5 0.2 collective-permute-done.8.refs_2_
  32.7 0.3 collective-permute-done.9.refs_3_
  33.0 2.9 %all-to-all-done.refs_5_ = f32[32,8,128]{2,1,0:T(8,128)S(1)} async-done(((f32[32,8,128]{2,1,0:T(8,128)}), f32[32,8,128]{2,1,0:T(8,128)S(1)}, u32[]{:S(2)}, u32[]{:S(2)}) %all-to-all-start) | async-done | bytes 131104 | tf_op jit(solution)/shard_map/all_to_all | solution.py:585
  35.9 0.0 collective-permute-done.5.refs_0_
  35.9 1.1 %outputs.1 = (bf16[128,2048]{1,0:T(8,128)(2,1)}, bf16[128,2048]{1,0:T(8,128)(2,1)}, bf16[128,2048]{1,0:T(8,128)(2,1)}, f32[4,16]{1,0:T(4,128)}) custom-call(bf16[3,32,2048]{2,1,0:T(8,128)(2,1)S(1)} %collective-permute-done.5.refs_0_, bf16[3,32,2048]{2,1,0:T(8,128)(2,1)S(1)} %get-tuple-element.46.refs_1_, ...), custom_call_target="tpu_custom_call", output_to_operand_aliasing={{0}: (6, {}), {1}: (7, {}), {2}: (8, {})} | custom-call | flops 1 | bytes 1 | tf_op jit(solution)/shard_map/outputs/pallas_call | solution.py:529
  (1 shorter events, 0.0 us)
Async XLA Ops:
  2.0 4.6 %collective-permute-start = (bf16[4,32,2048]{2,1,0:T(8,128)(2,1)S(1)}, bf16[4,32,2048]{2,1,0:T(8,128)(2,1)S(1)}, u32[]{:S(2)}, u32[]{:S(2)}) collective-permute-start(bf16[4,32,2048]{2,1,0:T(8,128)(2,1)S(1)} %get-tuple-element.34.refs_4_), channel_id=1, source_target_pairs={{0,8},{8,0},{16,24},{24,16},{1,9},{9,1},{17,25},{25,17},{2,10},{10... | collective-permute-start | bytes 1572872 | tf_op jit(solution)/shard_map/ppermute | solution.py:523
  2.5 4.1 %collective-permute-start.1 = (bf16[4,32,2048]{2,1,0:T(8,128)(2,1)S(1)}, bf16[4,32,2048]{2,1,0:T(8,128)(2,1)S(1)}, u32[]{:S(2)}, u32[]{:S(2)}) collective-permute-start(bf16[4,32,2048]{2,1,0:T(8,128)(2,1)S(1)} %get-tuple-element.35), channel_id=1, source_target_pairs={{0,8},{8,0},{16,24},{24,16},{1,9},{9,1},{17,25},{25,17},{2,10},{10... | collective-permute-start | bytes 1572872 | tf_op jit(solution)/shard_map/ppermute | solution.py:523
  2.6 9.3 %collective-permute-start.4 = (bf16[2,32,2048]{2,1,0:T(8,128)(2,1)S(1)}, bf16[2,32,2048]{2,1,0:T(8,128)(2,1)S(1)}, u32[]{:S(2)}, u32[]{:S(2)}) collective-permute-start(bf16[2,32,2048]{2,1,0:T(8,128)(2,1)S(1)} %get-tuple-element.31.after), channel_id=1, source_target_pairs={{0,24},{8,16},{16,8},{24,0},{1,25},{9,17},{17,9},{25,1},{2,26},{10... | collective-permute-start | bytes 786440 | tf_op jit(solution)/shard_map/ppermute | solution.py:523
  5.3 1.4 %copy-start = (f32[16,4]{0,1:T(4,128)S(1)}, f32[16,4]{0,1:T(4,128)}, u32[]{:S(2)}) copy-start(f32[16,4]{0,1:T(4,128)} %param.9) | copy-start | bytes 772
  8.3 7.6 %collective-permute-start.2 = (bf16[32,2304]{1,0:T(8,128)(2,1)S(1)}, bf16[32,2304]{1,0:T(8,128)(2,1)S(1)}, u32[]{:S(2)}, u32[]{:S(2)}) collective-permute-start(bf16[32,2304]{1,0:T(8,128)(2,1)S(1)} %get-tuple-element.38), channel_id=1, source_target_pairs={{0,16},{8,24},{16,0},{24,8},{1,17},{9,25},{17,1},{25,9},{2,18},{10... | collective-permute-start | bytes 442376 | tf_op jit(solution)/shard_map/ppermute | solution.py:523
  9.3 9.7 %collective-permute-start.3 = (bf16[32,2304]{1,0:T(8,128)(2,1)S(1)}, bf16[32,2304]{1,0:T(8,128)(2,1)S(1)}, u32[]{:S(2)}, u32[]{:S(2)}) collective-permute-start(bf16[32,2304]{1,0:T(8,128)(2,1)S(1)} %get-tuple-element.39), channel_id=1, source_target_pairs={{0,16},{8,24},{16,0},{24,8},{1,17},{9,25},{17,1},{25,9},{2,18},{10... | collective-permute-start | bytes 442376 | tf_op jit(solution)/shard_map/ppermute | solution.py:523
  10.3 17.9 %collective-permute-start.6 = (bf16[2,32,2048]{2,1,0:T(8,128)(2,1)S(1)}, bf16[2,32,2048]{2,1,0:T(8,128)(2,1)S(1)}, u32[]{:S(2)}, u32[]{:S(2)}) collective-permute-start(bf16[2,32,2048]{2,1,0:T(8,128)(2,1)S(1)} %get-tuple-element.44), channel_id=1, source_target_pairs={{0,16},{8,24},{16,0},{24,8},{1,17},{9,25},{17,1},{25,9},{2,18},{10... | collective-permute-start | bytes 786440 | tf_op jit(solution)/shard_map/ppermute | solution.py:523
  11.3 18.0 %collective-permute-start.7 = (bf16[2,32,2048]{2,1,0:T(8,128)(2,1)S(1)}, bf16[2,32,2048]{2,1,0:T(8,128)(2,1)S(1)}, u32[]{:S(2)}, u32[]{:S(2)}) collective-permute-start(bf16[2,32,2048]{2,1,0:T(8,128)(2,1)S(1)} %get-tuple-element.45), channel_id=1, source_target_pairs={{0,24},{8,16},{16,8},{24,0},{1,25},{9,17},{17,9},{25,1},{2,26},{10... | collective-permute-start | bytes 786440 | tf_op jit(solution)/shard_map/ppermute | solution.py:523
  22.1 13.8 %collective-permute-start.5 = (bf16[3,32,2048]{2,1,0:T(8,128)(2,1)S(1)}, bf16[3,32,2048]{2,1,0:T(8,128)(2,1)S(1)}, u32[]{:S(2)}, u32[]{:S(2)}) collective-permute-start(bf16[3,32,2048]{2,1,0:T(8,128)(2,1)S(1)} %get-tuple-element.41), channel_id=1, source_target_pairs={{0,8},{8,0},{16,24},{24,16},{1,9},{9,1},{17,25},{25,17},{2,10},{10... | collective-permute-start | bytes 1179656 | tf_op jit(solution)/shard_map/ppermute | solution.py:523
  22.2 13.8 %all-to-all-start = ((f32[32,8,128]{2,1,0:T(8,128)}), f32[32,8,128]{2,1,0:T(8,128)S(1)}, u32[]{:S(2)}, u32[]{:S(2)}) async-start(f32[32,8,128]{2,1,0:T(8,128)} %get-tuple-element.50), calls=%async_computation | async-start | bytes 262144 | tf_op jit(solution)/shard_map/all_to_all | solution.py:585
  31.1 1.4 %collective-permute-start.10 = (bf16[32,2048]{1,0:T(8,128)(2,1)S(1)}, bf16[32,2048]{1,0:T(8,128)(2,1)S(1)}, u32[]{:S(2)}, u32[]{:S(2)}) collective-permute-start(bf16[32,2048]{1,0:T(8,128)(2,1)S(1)} %get-tuple-element.49), channel_id=1, source_target_pairs={{0,8},{8,0},{16,24},{24,16},{1,9},{9,1},{17,25},{25,17},{2,10},{10... | collective-permute-start | bytes 393224 | tf_op jit(solution)/shard_map/ppermute | solution.py:523
  31.3 1.4 %collective-permute-start.8 = (bf16[32,2048]{1,0:T(8,128)(2,1)S(1)}, bf16[32,2048]{1,0:T(8,128)(2,1)S(1)}, u32[]{:S(2)}, u32[]{:S(2)}) collective-permute-start(bf16[32,2048]{1,0:T(8,128)(2,1)S(1)} %get-tuple-element.47), channel_id=1, source_target_pairs={{0,8},{8,0},{16,24},{24,16},{1,9},{9,1},{17,25},{25,17},{2,10},{10... | collective-permute-start | bytes 393224 | tf_op jit(solution)/shard_map/ppermute | solution.py:523
  31.7 1.3 %collective-permute-start.9 = (bf16[32,2048]{1,0:T(8,128)(2,1)S(1)}, bf16[32,2048]{1,0:T(8,128)(2,1)S(1)}, u32[]{:S(2)}, u32[]{:S(2)}) collective-permute-start(bf16[32,2048]{1,0:T(8,128)(2,1)S(1)} %get-tuple-element.48), channel_id=1, source_target_pairs={{0,8},{8,0},{16,24},{24,16},{1,9},{9,1},{17,25},{25,17},{2,10},{10... | collective-permute-start | bytes 393224 | tf_op jit(solution)/shard_map/ppermute | solution.py:523

commit v3 on v2

--- a/solution.py
+++ b/solution.py
@@ -407,7 +407,7 @@
 
 
 def score_kernel(heads, scale, table, small, bias, mine, near, *refs):
-    far, (out_items, out_shares, out_small), lines_ref = refs[:3], refs[3:6], refs[6]
+    far, (out_items, out_shares, out_small, out_lines), lines_ref = refs[:3], refs[3:7], refs[7]
     size, width = mine.shape[1:]
     lines_ref[...] = bias[...]
 
@@ -426,23 +426,25 @@
         over_tiles(size, tile)
 
     with_frames(*frames_of(mine, near, far), work)
+    out_lines[...] = lines_ref[...]
     for j in range(out_shares.shape[0]):
         out_shares[j] = lines_ref[: out_shares.shape[1], :]
 
 
-def output_copies(which, piece, outs, chunk, sems, at):
-    size = piece[0].shape[0]
-    start = pl.multiple_of(which * CHUNKS * size + chunk_start(chunk, size), TILE)
+def output_copies(which, piece, outs, chunk, sems, at, offset=0):
+    half = outs[0].shape[0] // 2
+    start = which * half + chunk_start(chunk, half // CHUNKS) + offset
+    rows = pl.ds(pl.multiple_of(start, TILE), piece[0].shape[0])
     return [
-        pltpu.make_async_copy(part, out.at[pl.ds(start, size)], sems.at[at + j])
+        pltpu.make_async_copy(part, out.at[rows], sems.at[at + j])
         for j, (part, out) in enumerate(zip(piece, outs))
     ]
 
 
 def gradient_kernel(heads, scale, items_ref, mine, near, *refs):
-    far, out_other, outs, kept, sems = refs[:3], refs[3], refs[4:7], refs[7], refs[8]
+    far, out_others, outs, kept, given, sems = refs[:3], refs[3:5], refs[5:8], *refs[8:]
     own, neighbour = frames_of(mine, near, far)
-    own_out, other_out = shifted(planes(kept), 0), shifted(planes(out_other), 0)
+    own_out, other_out = shifted(planes(kept), 0), shifted(planes(given), 0)
 
     def work(chip, a, b):
         out_a, out_b = (own_out, other_out) if a is own else (other_out, own_out)
@@ -460,11 +462,17 @@
     copies = output_copies(my_place()[0], planes(kept), outs, 0, sems, 0)
     for copy in copies:
         copy.start()
+    start = 0
+    for out in out_others:
+        for row in range(0, out.shape[1], TILE):
+            for j in range(3):
+                out[j, row : row + TILE, :] = given[j, start + row : start + row + TILE, :]
+        start += out.shape[1]
     for copy in copies:
         copy.wait()
 
 
-def whole_kernel(heads, scale, table, small, small_far, mine, near, *refs):
+def whole_kernel(heads, scale, after, table, small, small_far, mine, near, *refs):
     far, out_own, out_others = refs[:2], refs[2], refs[3:6]
     own, neighbour = frames_of(mine, near, far)
     own_out, other_out = shifted(planes(out_own), 0), shifted(out_others, 0)
@@ -487,19 +495,22 @@
 
 
 def output_kernel(*refs):
-    first_back, kept, back, shares = planes(refs[0]), planes(refs[1]), refs[2:5], refs[5]
-    outs, out_bias, total, sems = refs[9:12], *refs[12:]
+    first_backs, kept, back, shares = refs[:2], planes(refs[2]), refs[3:6], refs[6]
+    outs, out_bias, total, sems = refs[10:13], *refs[13:]
     core = my_place()[0]
-    copies = output_copies(1 - core, first_back, outs, 0, sems, 0)
-    copies += output_copies(core, kept, outs, 1, sems, 3)
-    copies += output_copies(1 - core, back, outs, 1, sems, 6)
+    copies = output_copies(core, kept, outs, 1, sems, 0)
+    copies += output_copies(1 - core, back, outs, 1, sems, 3)
+    offset = 0
+    for j, ref in enumerate(first_backs):
+        copies += output_copies(1 - core, planes(ref), outs, 0, sems, 6 + 3 * j, offset)
+        offset += ref.shape[1]
     for copy in copies:
         copy.start()
     parts = [shares[j] for j in range(shares.shape[0])]
     while len(parts) > 1:
         parts = [a + b for a, b in zip(parts[::2], parts[1::2])]
     total[...] = parts[0][: total.shape[0], : total.shape[1]]
-    copies.append(pltpu.make_async_copy(total, out_bias, sems.at[9]))
+    copies.append(pltpu.make_async_copy(total, out_bias, sems.at[12]))
     copies[-1].start()
     for copy in copies:
         copy.wait()
@@ -569,35 +580,37 @@
 
     whole = pltpu.HBM((rows, width), jnp.bfloat16)
     stack, piece = shape(3, size, width), shape(size, width)
-    output_sems = pltpu.SemaphoreType.DMA((10,))
+    output_sems = pltpu.SemaphoreType.DMA((13,))
     first = (mines[0], nears[0], *sames[0], others[0])
-    items, shares, small_far = call(
+    items, shares, small_far, token = call(
         functools.partial(score_kernel, heads, scale),
         "scores",
         [
             shape(EARLY, size, LANES),
             shape(math.prod(count for _, count in sizes), 8, LANES, dtype=wide),
             shape(size, LANES, dtype=wide),
+            lines,
         ],
         table, smalls[0], bias, *first,
         scratch=[pltpu.VMEM((8, LANES), wide)],
     )
     shares = lax.all_to_all(shares, tuple(axis for axis, _ in sizes), 0, 0, tiled=True)
-    back, *grads = call(
+    *back, grad_queries, grad_keys, grad_values = call(
         functools.partial(gradient_kernel, heads, scale),
         "gradients",
-        [stack] + [whole] * 3,
+        [shape(3, size // 2, width)] * 2 + [whole] * 3,
         items, *first,
-        scratch=[pltpu.VMEM((3, size, width), jnp.bfloat16), output_sems],
-        hbm_out=range(1, 4),
-    )
-    first_back = swap(back, 1)
+        scratch=[pltpu.VMEM((3, size, width), jnp.bfloat16)] * 2 + [output_sems],
+        hbm_out=range(2, 5),
+    )
+    grads = (grad_queries, grad_keys, grad_values)
+    first_backs = [swap(x, 1) for x in back]
 
     kept, *back = call(
         functools.partial(whole_kernel, heads, scale),
         "scores_and_gradients",
         [stack] + [piece] * 3,
-        table, smalls[1], small_far, mines[1], nears[1], *sames[1], others[1],
+        swap(token, 1), table, smalls[1], small_far, mines[1], nears[1], *sames[1], others[1],
     )
     back = [swap(x, 1) for x in back]
     grads = [pltpu.with_memory_space_constraint(x, pltpu.HBM) for x in grads]
@@ -605,11 +618,11 @@
         output_kernel,
         "outputs",
         [whole] * 3 + [shape(frames, heads, dtype=wide)],
-        first_back, kept, *back, shares, *grads,
+        *first_backs, kept, *back, shares, *grads,
         scratch=[pltpu.VMEM((frames, heads), wide), output_sems],
-        hbm=range(6, 9),
+        hbm=range(7, 10),
         hbm_out=range(4),
-        aliases={6 + j: j for j in range(3)},
+        aliases={7 + j: j for j in range(3)},
     )
     return (*[x.reshape(query_vectors.shape) for x in grads], bias.T)
 

time: 37.3 us -> 35.6 us (0.954)
  waiting for transfers between devices: 12.7 us -> 9.23 us
  starting transfers between devices: 13.3 us -> 14.4 us
  Pallas kernels: 10.3 us -> 11.1 us
    all_to_all x1, waiting for transfers between devices: 2.93 us -> 0.59 us  [by_chips(): lax.all_to_all(shares, tuple((axis for axis, _ in sizes)), 0, 0, tiled=True)]
    ppermute x11 -> x13, waiting for transfers between devices: 9.78 us -> 8.64 us  [swap(): return lax.ppermute(x, 'tm', [(i, i ^ bits) for i in range(4)])]
    ppermute x11 -> x13, starting transfers between devices: 7.29 us -> 8.12 us  [swap(): return lax.ppermute(x, 'tm', [(i, i ^ bits) for i in range(4)])]
    pallas_call x7, Pallas kernels: 10.3 us -> 11.1 us  [call(): pl.pallas_call(kernel, in_specs=[any_spec if j in hbm else vmem_spec for...]
  transfers between devices with their start and end apart: 12 -> 14, of which waited for: 8 -> 7; matrix products, arithmetic and copies ran while one was open for 0% -> 0% of each run, Pallas kernels for 21% -> 24%
where the time goes in v3:
time: 35.6 us; the launch traced here: 35.4 us
  starting transfers between devices  14.4 us (40%)
  Pallas kernels  11.1 us (31%)
  waiting for transfers between devices  9.23 us (26%)
  between operations  0.72 us (2%)
    pallas_call x7, Pallas kernels, call(): pl.pallas_call(kernel, in_specs=[any_spec if j in hbm else vmem_spec for...  11.1 us
    ppermute x13, waiting for transfers between devices, swap(): return lax.ppermute(x, 'tm', [(i, i ^ bits) for i in range(4)])  8.64 us
    ppermute x13, starting transfers between devices, swap(): return lax.ppermute(x, 'tm', [(i, i ^ bits) for i in range(4)])  8.12 us
    all_to_all x1, starting transfers between devices, by_chips(): lax.all_to_all(shares, tuple((axis for axis, _ in sizes)), 0, 0, tiled=True)  6.23 us
  transfers between devices with their start and end apart: 14, of which 7 were waited for; matrix products, arithmetic and copies ran while one was open for 0% of the time, Pallas kernels for 24%

profile of v3, /device:TPU:0, one launch (start us, length us, event | category | flops | bytes accessed | tf_op | source)
XLA Modules:
  0.0 35.4 jit_solution(3123485004104737796)
XLA Ops:
  0.6 1.4 %fetch_theirs.1 = (bf16[4,32,2048]{2,1,0:T(8,128)(2,1)S(1)}, bf16[4,32,2048]{2,1,0:T(8,128)(2,1)S(1)}, bf16[2,32,2048]{2,1,0:T(8,128)(2,1)S(1)}) custom-call(bf16[128,2048]{1,0:T(8,128)(2,1)} %bitcast.15, bf16[128,2048]{1,0:T(8,128)(2,1)} %bitcast.17, bf16[128,2048]{1,0:T(8,128)(2,1)} %bitcast.19, bf16[128,2048]{1,0:T(8,128)(2,1)} %bitcast.21), custom_call_target="tpu_custom_call" | custom-call | flops 1 | bytes 1 | tf_op jit(solution)/shard_map/fetch_theirs/pallas_call | solution.py:540
  2.0 0.5 %collective-permute-start = (bf16[4,32,2048]{2,1,0:T(8,128)(2,1)S(1)}, bf16[4,32,2048]{2,1,0:T(8,128)(2,1)S(1)}, u32[]{:S(2)}, u32[]{:S(2)}) collective-permute-start(bf16[4,32,2048]{2,1,0:T(8,128)(2,1)S(1)} %get-tuple-element.36.refs_4_), channel_id=1, source_target_pairs={{0,8},{8,0},{16,24},{24,16},{1,9},{9,1},{17,25},{25,17},{2,10},{10... | collective-permute-start | bytes 1572872 | tf_op jit(solution)/shard_map/ppermute | solution.py:534
  2.5 0.1 collective-permute-start.1
  2.6 2.6 %collective-permute-start.4 = (bf16[2,32,2048]{2,1,0:T(8,128)(2,1)S(1)}, bf16[2,32,2048]{2,1,0:T(8,128)(2,1)S(1)}, u32[]{:S(2)}, u32[]{:S(2)}) collective-permute-start(bf16[2,32,2048]{2,1,0:T(8,128)(2,1)S(1)} %get-tuple-element.33.after), channel_id=1, source_target_pairs={{0,24},{8,16},{16,8},{24,0},{1,25},{9,17},{17,9},{25,1},{2,26},{10... | collective-permute-start | bytes 786440 | tf_op jit(solution)/shard_map/ppermute | solution.py:534
  5.3 0.0 copy-start
  5.3 1.4 %fetch_mine.1 = (bf16[4,32,2048]{2,1,0:T(8,128)(2,1)S(1)}, bf16[4,32,2048]{2,1,0:T(8,128)(2,1)S(1)}) custom-call(bf16[128,2048]{1,0:T(8,128)(2,1)} %bitcast.16, bf16[128,2048]{1,0:T(8,128)(2,1)} %bitcast.18, bf16[128,2048]{1,0:T(8,128)(2,1)} %bitcast.20, bf16[128,2048]{1,0:T(8,128)(2,1)} %bitcast.22, bf16[2,32,2048]{2,1,0:T(8,128)(2,1)S(1)} %get-tuple-element.33.after), custom_call_target="tpu_custom_call" | custom-call | flops 1 | bytes 1 | tf_op jit(solution)/shard_map/fetch_mine/pallas_call | solution.py:540
  6.6 0.0 copy-done
  6.6 0.0 collective-permute-done.refs_2_.near
  6.7 0.0 collective-permute-done.1.refs_3_.near
  6.7 2.3 %local_scores.1 = (f32[32,128]{1,0:T(8,128)S(1)}, f32[32,128]{1,0:T(8,128)S(1)}, f32[8,128]{1,0:T(8,128)S(1)}, bf16[2,32,2048]{2,1,0:T(8,128)(2,1)}, bf16[32,230...) custom-call(f32[8,128]{1,0:T(8,128)S(1)} %pad.4.table, ...), custom_call_target="tpu_custom_call" | custom-call | flops 1 | bytes 1 | tf_op jit(solution)/shard_map/local_scores/pallas_call | solution.py:540
  9.0 1.0 %collective-permute-start.2 = (bf16[32,2304]{1,0:T(8,128)(2,1)S(1)}, bf16[32,2304]{1,0:T(8,128)(2,1)S(1)}, u32[]{:S(2)}, u32[]{:S(2)}) collective-permute-start(bf16[32,2304]{1,0:T(8,128)(2,1)S(1)} %get-tuple-element.40), channel_id=1, source_target_pairs={{0,16},{8,24},{16,0},{24,8},{1,17},{9,25},{17,1},{25,9},{2,18},{10... | collective-permute-start | bytes 442376 | tf_op jit(solution)/shard_map/ppermute | solution.py:534
  10.0 1.0 %collective-permute-start.3 = (bf16[32,2304]{1,0:T(8,128)(2,1)S(1)}, bf16[32,2304]{1,0:T(8,128)(2,1)S(1)}, u32[]{:S(2)}, u32[]{:S(2)}) collective-permute-start(bf16[32,2304]{1,0:T(8,128)(2,1)S(1)} %get-tuple-element.41), channel_id=1, source_target_pairs={{0,16},{8,24},{16,0},{24,8},{1,17},{9,25},{17,1},{25,9},{2,18},{10... | collective-permute-start | bytes 442376 | tf_op jit(solution)/shard_map/ppermute | solution.py:534
  11.0 1.0 %collective-permute-start.8 = (bf16[2,32,2048]{2,1,0:T(8,128)(2,1)}, bf16[2,32,2048]{2,1,0:T(8,128)(2,1)S(1)}, u32[]{:S(2)}, u32[]{:S(2)}) collective-permute-start(bf16[2,32,2048]{2,1,0:T(8,128)(2,1)} %get-tuple-element.48), channel_id=1, source_target_pairs={{0,16},{8,24},{16,0},{24,8},{1,17},{9,25},{17,1},{25,9},{2,18},{10... | collective-permute-start | bytes 786440 | tf_op jit(solution)/shard_map/ppermute | solution.py:534
  12.1 0.2 collective-permute-start.9
  12.3 0.0 collective-permute-done.4.refs_2_
  12.3 3.4 %collective-permute-done.2.refs_0_ = bf16[32,2304]{1,0:T(8,128)(2,1)S(1)} collective-permute-done((bf16[32,2304]{1,0:T(8,128)(2,1)S(1)}, bf16[32,2304]{1,0:T(8,128)(2,1)S(1)}, u32[]{:S(2)}, u32[]{:S(2)}) %collective-permute-start.2) | collective-permute-done | bytes 147488 | tf_op jit(solution)/shard_map/ppermute | solution.py:534
  15.7 3.2 %collective-permute-done.3.refs_1_ = bf16[32,2304]{1,0:T(8,128)(2,1)S(1)} collective-permute-done((bf16[32,2304]{1,0:T(8,128)(2,1)S(1)}, bf16[32,2304]{1,0:T(8,128)(2,1)S(1)}, u32[]{:S(2)}, u32[]{:S(2)}) %collective-permute-start.3) | collective-permute-done | bytes 147488 | tf_op jit(solution)/shard_map/ppermute | solution.py:534
  18.8 1.5 %scores.1 = (bf16[14,32,128]{2,1,0:T(8,128)(2,1)S(1)}, f32[32,8,128]{2,1,0:T(8,128)}, f32[32,128]{1,0:T(8,128)S(1)}, f32[8,128]{1,0:T(8,128)S(1)}) custom-call(f32[8,128]{1,0:T(8,128)S(1)} %pad.4.table, f32[32,128]{1,0:T(8,128)S(1)} %get-tuple-element.38.small, f32[8,128]{1,0:T(8,128)S(1)} %get-tuple-element.39.bias, ...), custom_call_target="tpu_custom_call" | custom-call | flops 1 | bytes 1 | tf_op jit(solution)/shard_map/scores/pallas_call | solution.py:540
  20.3 6.2 %all-to-all-start = ((f32[32,8,128]{2,1,0:T(8,128)}), f32[32,8,128]{2,1,0:T(8,128)S(1)}, u32[]{:S(2)}, u32[]{:S(2)}) async-start(f32[32,8,128]{2,1,0:T(8,128)} %get-tuple-element.54), calls=%async_computation | async-start | bytes 262144 | tf_op jit(solution)/shard_map/all_to_all | solution.py:597
  26.6 1.6 %gradients.1 = (bf16[3,16,2048]{2,1,0:T(8,128)(2,1)S(1)}, bf16[3,16,2048]{2,1,0:T(8,128)(2,1)S(1)}, bf16[128,2048]{1,0:T(8,128)(2,1)}, bf16[128,2048]{1,0:T(8,128)(2,1)}, bf16[128,2048]{1,0:T(8,128)(2,1)}) custom-call(bf16[14,32,128]{2,1,0:T(8,128)(2,1)S(1)} %get-tuple-element.42.items_ref, bf16[4,32,2048]{2,1,0:T(8,128)(2,1)S(1)} %get-tuple-element.34.refs_0_.mine, ...), custom_call_target="tpu_custom_call" | custom-call | flops 1 | bytes 1 | tf_op jit(solution)/shard_map/gradients/pallas_call | solution.py:540
  28.2 0.3 collective-permute-start.5
  28.5 0.3 collective-permute-start.6
  28.8 0.3 collective-permute-start.7
  29.0 1.0 %collective-permute-done.7.after = f32[8,128]{1,0:T(8,128)S(1)} collective-permute-done((f32[8,128]{1,0:T(8,128)S(1)}, f32[8,128]{1,0:T(8,128)S(1)}, u32[]{:S(2)}, u32[]{:S(2)}) %collective-permute-start.7) | collective-permute-done | bytes 4128 | tf_op jit(solution)/shard_map/ppermute | solution.py:534
  30.0 0.0 collective-permute-done.8.refs_0_
  30.0 0.0 collective-permute-done.9.refs_1_
  30.0 1.8 %scores_and_gradients.1 = (bf16[3,32,2048]{2,1,0:T(8,128)(2,1)S(1)}, bf16[32,2048]{1,0:T(8,128)(2,1)S(1)}, bf16[32,2048]{1,0:T(8,128)(2,1)S(1)}, bf16[32,2048]{1,0:T(8,128)(2,1)S(1)}) custom-call(f32[8,128]{1,0:T(8,128)S(1)} %collective-permute-done.7.after, f32[8,128]{1,0:T(8,128)S(1)} %pad.4.table, f32[32,128]{1,0:T(8,128)S(1)} %get-tuple-element.46.small, ...), custom_call_target="tpu_custom_call" | custom-call | flops 1 | bytes 1 | tf_op jit(solution)/shard_map/scores_and_gradients/pallas_call | solution.py:540
  31.8 0.3 collective-permute-start.10
  32.1 0.3 collective-permute-start.11
  32.4 0.2 collective-permute-start.12
  32.6 0.0 collective-permute-done.5.refs_0_
  32.6 0.0 collective-permute-done.6.refs_1_
  32.6 0.6 %collective-permute-done.10.refs_3_ = bf16[32,2048]{1,0:T(8,128)(2,1)S(1)} collective-permute-done((bf16[32,2048]{1,0:T(8,128)(2,1)S(1)}, bf16[32,2048]{1,0:T(8,128)(2,1)S(1)}, u32[]{:S(2)}, u32[]{:S(2)}) %collective-permute-start.10) | collective-permute-done | bytes 131104 | tf_op jit(solution)/shard_map/ppermute | solution.py:534
  33.2 0.2 collective-permute-done.11.refs_4_
  33.4 0.3 collective-permute-done.12.refs_5_
  33.7 0.6 %all-to-all-done.refs_6_ = f32[32,8,128]{2,1,0:T(8,128)S(1)} async-done(((f32[32,8,128]{2,1,0:T(8,128)}), f32[32,8,128]{2,1,0:T(8,128)S(1)}, u32[]{:S(2)}, u32[]{:S(2)}) %all-to-all-start) | async-done | bytes 131104 | tf_op jit(solution)/shard_map/all_to_all | solution.py:597
  34.3 1.1 %outputs.1 = (bf16[128,2048]{1,0:T(8,128)(2,1)}, bf16[128,2048]{1,0:T(8,128)(2,1)}, bf16[128,2048]{1,0:T(8,128)(2,1)}, f32[4,16]{1,0:T(4,128)}) custom-call(bf16[3,16,2048]{2,1,0:T(8,128)(2,1)S(1)} %collective-permute-done.5.refs_0_, ...), custom_call_target="tpu_custom_call", output_to_operand_aliasing={{0}: (7, {}), {1}: (8, {}), {2}: (9, {})} | custom-call | flops 1 | bytes 1 | tf_op jit(solution)/shard_map/outputs/pallas_call | solution.py:540
  (1 shorter events, 0.0 us)
Async XLA Ops:
  2.0 4.6 %collective-permute-start = (bf16[4,32,2048]{2,1,0:T(8,128)(2,1)S(1)}, bf16[4,32,2048]{2,1,0:T(8,128)(2,1)S(1)}, u32[]{:S(2)}, u32[]{:S(2)}) collective-permute-start(bf16[4,32,2048]{2,1,0:T(8,128)(2,1)S(1)} %get-tuple-element.36.refs_4_), channel_id=1, source_target_pairs={{0,8},{8,0},{16,24},{24,16},{1,9},{9,1},{17,25},{25,17},{2,10},{10... | collective-permute-start | bytes 1572872 | tf_op jit(solution)/shard_map/ppermute | solution.py:534
  2.5 4.1 %collective-permute-start.1 = (bf16[4,32,2048]{2,1,0:T(8,128)(2,1)S(1)}, bf16[4,32,2048]{2,1,0:T(8,128)(2,1)S(1)}, u32[]{:S(2)}, u32[]{:S(2)}) collective-permute-start(bf16[4,32,2048]{2,1,0:T(8,128)(2,1)S(1)} %get-tuple-element.37), channel_id=1, source_target_pairs={{0,8},{8,0},{16,24},{24,16},{1,9},{9,1},{17,25},{25,17},{2,10},{10... | collective-permute-start | bytes 1572872 | tf_op jit(solution)/shard_map/ppermute | solution.py:534
  2.6 9.6 %collective-permute-start.4 = (bf16[2,32,2048]{2,1,0:T(8,128)(2,1)S(1)}, bf16[2,32,2048]{2,1,0:T(8,128)(2,1)S(1)}, u32[]{:S(2)}, u32[]{:S(2)}) collective-permute-start(bf16[2,32,2048]{2,1,0:T(8,128)(2,1)S(1)} %get-tuple-element.33.after), channel_id=1, source_target_pairs={{0,24},{8,16},{16,8},{24,0},{1,25},{9,17},{17,9},{25,1},{2,26},{10... | collective-permute-start | bytes 786440 | tf_op jit(solution)/shard_map/ppermute | solution.py:534
  5.3 1.4 %copy-start = (f32[16,4]{0,1:T(4,128)S(1)}, f32[16,4]{0,1:T(4,128)}, u32[]{:S(2)}) copy-start(f32[16,4]{0,1:T(4,128)} %param.9) | copy-start | bytes 772
  9.0 6.7 %collective-permute-start.2 = (bf16[32,2304]{1,0:T(8,128)(2,1)S(1)}, bf16[32,2304]{1,0:T(8,128)(2,1)S(1)}, u32[]{:S(2)}, u32[]{:S(2)}) collective-permute-start(bf16[32,2304]{1,0:T(8,128)(2,1)S(1)} %get-tuple-element.40), channel_id=1, source_target_pairs={{0,16},{8,24},{16,0},{24,8},{1,17},{9,25},{17,1},{25,9},{2,18},{10... | collective-permute-start | bytes 442376 | tf_op jit(solution)/shard_map/ppermute | solution.py:534
  10.0 8.8 %collective-permute-start.3 = (bf16[32,2304]{1,0:T(8,128)(2,1)S(1)}, bf16[32,2304]{1,0:T(8,128)(2,1)S(1)}, u32[]{:S(2)}, u32[]{:S(2)}) collective-permute-start(bf16[32,2304]{1,0:T(8,128)(2,1)S(1)} %get-tuple-element.41), channel_id=1, source_target_pairs={{0,16},{8,24},{16,0},{24,8},{1,17},{9,25},{17,1},{25,9},{2,18},{10... | collective-permute-start | bytes 442376 | tf_op jit(solution)/shard_map/ppermute | solution.py:534
  11.0 19.0 %collective-permute-start.8 = (bf16[2,32,2048]{2,1,0:T(8,128)(2,1)}, bf16[2,32,2048]{2,1,0:T(8,128)(2,1)S(1)}, u32[]{:S(2)}, u32[]{:S(2)}) collective-permute-start(bf16[2,32,2048]{2,1,0:T(8,128)(2,1)} %get-tuple-element.48), channel_id=1, source_target_pairs={{0,16},{8,24},{16,0},{24,8},{1,17},{9,25},{17,1},{25,9},{2,18},{10... | collective-permute-start | bytes 786440 | tf_op jit(solution)/shard_map/ppermute | solution.py:534
  12.1 18.0 %collective-permute-start.9 = (bf16[2,32,2048]{2,1,0:T(8,128)(2,1)}, bf16[2,32,2048]{2,1,0:T(8,128)(2,1)S(1)}, u32[]{:S(2)}, u32[]{:S(2)}) collective-permute-start(bf16[2,32,2048]{2,1,0:T(8,128)(2,1)} %get-tuple-element.49), channel_id=1, source_target_pairs={{0,24},{8,16},{16,8},{24,0},{1,25},{9,17},{17,9},{25,1},{2,26},{10... | collective-permute-start | bytes 786440 | tf_op jit(solution)/shard_map/ppermute | solution.py:534
  20.3 14.0 %all-to-all-start = ((f32[32,8,128]{2,1,0:T(8,128)}), f32[32,8,128]{2,1,0:T(8,128)S(1)}, u32[]{:S(2)}, u32[]{:S(2)}) async-start(f32[32,8,128]{2,1,0:T(8,128)} %get-tuple-element.54), calls=%async_computation | async-start | bytes 262144 | tf_op jit(solution)/shard_map/all_to_all | solution.py:597
  28.2 4.4 %collective-permute-start.5 = (bf16[3,16,2048]{2,1,0:T(8,128)(2,1)S(1)}, bf16[3,16,2048]{2,1,0:T(8,128)(2,1)S(1)}, u32[]{:S(2)}, u32[]{:S(2)}) collective-permute-start(bf16[3,16,2048]{2,1,0:T(8,128)(2,1)S(1)} %get-tuple-element.43), channel_id=1, source_target_pairs={{0,8},{8,0},{16,24},{24,16},{1,9},{9,1},{17,25},{25,17},{2,10},{10... | collective-permute-start | bytes 589832 | tf_op jit(solution)/shard_map/ppermute | solution.py:534
  28.5 4.1 %collective-permute-start.6 = (bf16[3,16,2048]{2,1,0:T(8,128)(2,1)S(1)}, bf16[3,16,2048]{2,1,0:T(8,128)(2,1)S(1)}, u32[]{:S(2)}, u32[]{:S(2)}) collective-permute-start(bf16[3,16,2048]{2,1,0:T(8,128)(2,1)S(1)} %get-tuple-element.44), channel_id=1, source_target_pairs={{0,8},{8,0},{16,24},{24,16},{1,9},{9,1},{17,25},{25,17},{2,10},{10... | collective-permute-start | bytes 589832 | tf_op jit(solution)/shard_map/ppermute | solution.py:534
  28.8 1.2 %collective-permute-start.7 = (f32[8,128]{1,0:T(8,128)S(1)}, f32[8,128]{1,0:T(8,128)S(1)}, u32[]{:S(2)}, u32[]{:S(2)}) collective-permute-start(f32[8,128]{1,0:T(8,128)S(1)} %get-tuple-element.45), channel_id=1, source_target_pairs={{0,8},{8,0},{16,24},{24,16},{1,9},{9,1},{17,25},{25,17},{2,10},{10... | collective-permute-start | bytes 12296 | tf_op jit(solution)/shard_map/ppermute | solution.py:534
  31.8 1.4 %collective-permute-start.10 = (bf16[32,2048]{1,0:T(8,128)(2,1)S(1)}, bf16[32,2048]{1,0:T(8,128)(2,1)S(1)}, u32[]{:S(2)}, u32[]{:S(2)}) collective-permute-start(bf16[32,2048]{1,0:T(8,128)(2,1)S(1)} %get-tuple-element.51), channel_id=1, source_target_pairs={{0,8},{8,0},{16,24},{24,16},{1,9},{9,1},{17,25},{25,17},{2,10},{10... | collective-permute-start | bytes 393224 | tf_op jit(solution)/shard_map/ppermute | solution.py:534
  32.1 1.3 %collective-permute-start.11 = (bf16[32,2048]{1,0:T(8,128)(2,1)S(1)}, bf16[32,2048]{1,0:T(8,128)(2,1)S(1)}, u32[]{:S(2)}, u32[]{:S(2)}) collective-permute-start(bf16[32,2048]{1,0:T(8,128)(2,1)S(1)} %get-tuple-element.52), channel_id=1, source_target_pairs={{0,8},{8,0},{16,24},{24,16},{1,9},{9,1},{17,25},{25,17},{2,10},{10... | collective-permute-start | bytes 393224 | tf_op jit(solution)/shard_map/ppermute | solution.py:534
  32.4 1.3 %collective-permute-start.12 = (bf16[32,2048]{1,0:T(8,128)(2,1)S(1)}, bf16[32,2048]{1,0:T(8,128)(2,1)S(1)}, u32[]{:S(2)}, u32[]{:S(2)}) collective-permute-start(bf16[32,2048]{1,0:T(8,128)(2,1)S(1)} %get-tuple-element.53), channel_id=1, source_target_pairs={{0,8},{8,0},{16,24},{24,16},{1,9},{9,1},{17,25},{25,17},{2,10},{10... | collective-permute-start | bytes 393224 | tf_op jit(solution)/shard_map/ppermute | solution.py:534

commit v4 on v3

--- a/solution.py
+++ b/solution.py
@@ -406,12 +406,15 @@
     return unpacked_small(*(ref[rows, at] for ref in pair_of(far[:-1])), heads)
 
 
-def score_kernel(heads, scale, table, small, bias, mine, near, *refs):
-    far, (out_items, out_shares, out_small, out_lines), lines_ref = refs[:3], refs[3:7], refs[7]
+def first_kernel(heads, scale, table, small, bias, mine, near, *refs):
+    far, kept, out_others, out_small, out_shares = refs[:3], refs[3], refs[4:6], refs[6], refs[7]
+    items_ref, shares, lines_ref, given, sem = refs[8:]
     size, width = mine.shape[1:]
+    own, neighbour = frames_of(mine, near, far)
+    own_out, other_out = shifted(planes(kept), 0), shifted(planes(given), 0)
     lines_ref[...] = bias[...]
 
-    def work(chip, a, b):
+    def scores(chip, a, b):
         def tile(row):
             rows = tile_at(row)
             items, lines = score_tile(
@@ -420,15 +423,36 @@
             )
             out_small[rows, :] = far_small(far, rows, width, heads, 1)
             for j, item in enumerate(items):
-                out_items[j, rows, :] = item
+                items_ref[j, rows, :] = item
             lines_ref[...] += lines
 
         over_tiles(size, tile)
 
-    with_frames(*frames_of(mine, near, far), work)
-    out_lines[...] = lines_ref[...]
-    for j in range(out_shares.shape[0]):
-        out_shares[j] = lines_ref[: out_shares.shape[1], :]
+    def gradients(chip, a, b):
+        out_a, out_b = (own_out, other_out) if a is own else (other_out, own_out)
+
+        def tile(row):
+            items = [items_ref[j, tile_at(row), :] for j in range(LATE if chip else EARLY)]
+            gradient_tile(
+                heads, scale, chip, tiles_of(a, row), tiles_of(b, row), items,
+                tiles_of(out_a, row), tiles_of(out_b, row),
+            )
+
+        over_tiles(size, tile)
+
+    with_frames(own, neighbour, scores)
+    for j in range(shares.shape[0]):
+        shares[j] = lines_ref[...]
+    copy = pltpu.make_async_copy(shares, out_shares, sem)
+    copy.start()
+    with_frames(own, neighbour, gradients)
+    start = 0
+    for out in out_others:
+        for row in range(0, out.shape[1], TILE):
+            for j in range(3):
+                out[j, row : row + TILE, :] = given[j, start + row : start + row + TILE, :]
+        start += out.shape[1]
+    copy.wait()
 
 
 def output_copies(which, piece, outs, chunk, sems, at, offset=0):
@@ -441,41 +465,13 @@
     ]
 
 
-def gradient_kernel(heads, scale, items_ref, mine, near, *refs):
-    far, out_others, outs, kept, given, sems = refs[:3], refs[3:5], refs[5:8], *refs[8:]
+def last_kernel(heads, scale, table, small, small_far, first_kept, mine, near, *refs):
+    far, out_own, out_others, outs, sems = refs[:2], refs[2], refs[3:6], refs[6:9], refs[9]
     own, neighbour = frames_of(mine, near, far)
-    own_out, other_out = shifted(planes(kept), 0), shifted(planes(given), 0)
-
-    def work(chip, a, b):
-        out_a, out_b = (own_out, other_out) if a is own else (other_out, own_out)
-
-        def tile(row):
-            items = [items_ref[j, tile_at(row), :] for j in range(LATE if chip else EARLY)]
-            gradient_tile(
-                heads, scale, chip, tiles_of(a, row), tiles_of(b, row), items,
-                tiles_of(out_a, row), tiles_of(out_b, row),
-            )
-
-        over_tiles(mine.shape[1], tile)
-
-    with_frames(own, neighbour, work)
-    copies = output_copies(my_place()[0], planes(kept), outs, 0, sems, 0)
+    own_out, other_out = shifted(planes(out_own), 0), shifted(out_others, 0)
+    copies = output_copies(my_place()[0], planes(first_kept), outs, 0, sems, 0)
     for copy in copies:
         copy.start()
-    start = 0
-    for out in out_others:
-        for row in range(0, out.shape[1], TILE):
-            for j in range(3):
-                out[j, row : row + TILE, :] = given[j, start + row : start + row + TILE, :]
-        start += out.shape[1]
-    for copy in copies:
-        copy.wait()
-
-
-def whole_kernel(heads, scale, after, table, small, small_far, mine, near, *refs):
-    far, out_own, out_others = refs[:2], refs[2], refs[3:6]
-    own, neighbour = frames_of(mine, near, far)
-    own_out, other_out = shifted(planes(out_own), 0), shifted(out_others, 0)
 
     def work(chip, a, b):
         out_a, out_b = (own_out, other_out) if a is own else (other_out, own_out)
@@ -492,6 +488,8 @@
         over_tiles(mine.shape[1], tile)
 
     with_frames(own, neighbour, work)
+    for copy in copies:
+        copy.wait()
 
 
 def output_kernel(*refs):
@@ -580,40 +578,35 @@
 
     whole = pltpu.HBM((rows, width), jnp.bfloat16)
     stack, piece = shape(3, size, width), shape(size, width)
+    everyone = shape(math.prod(count for _, count in sizes), 8, LANES, dtype=wide)
     output_sems = pltpu.SemaphoreType.DMA((13,))
-    first = (mines[0], nears[0], *sames[0], others[0])
-    items, shares, small_far, token = call(
-        functools.partial(score_kernel, heads, scale),
-        "scores",
-        [
-            shape(EARLY, size, LANES),
-            shape(math.prod(count for _, count in sizes), 8, LANES, dtype=wide),
-            shape(size, LANES, dtype=wide),
-            lines,
+    first_kept, *back, small_far, shares = call(
+        functools.partial(first_kernel, heads, scale),
+        "first_chunk",
+        [stack] + [shape(3, size // 2, width)] * 2 + [shape(size, LANES, dtype=wide), everyone],
+        table, smalls[0], bias, mines[0], nears[0], *sames[0], others[0],
+        scratch=[
+            pltpu.VMEM((EARLY, size, LANES), jnp.bfloat16),
+            pltpu.VMEM(everyone.shape, wide),
+            pltpu.VMEM((8, LANES), wide),
+            pltpu.VMEM((3, size, width), jnp.bfloat16),
+            pltpu.SemaphoreType.DMA,
         ],
-        table, smalls[0], bias, *first,
-        scratch=[pltpu.VMEM((8, LANES), wide)],
+        hbm_out=(4,),
     )
     shares = lax.all_to_all(shares, tuple(axis for axis, _ in sizes), 0, 0, tiled=True)
-    *back, grad_queries, grad_keys, grad_values = call(
-        functools.partial(gradient_kernel, heads, scale),
-        "gradients",
-        [shape(3, size // 2, width)] * 2 + [whole] * 3,
-        items, *first,
-        scratch=[pltpu.VMEM((3, size, width), jnp.bfloat16)] * 2 + [output_sems],
-        hbm_out=range(2, 5),
-    )
-    grads = (grad_queries, grad_keys, grad_values)
     first_backs = [swap(x, 1) for x in back]
 
-    kept, *back = call(
-        functools.partial(whole_kernel, heads, scale),
-        "scores_and_gradients",
-        [stack] + [piece] * 3,
-        swap(token, 1), table, smalls[1], small_far, mines[1], nears[1], *sames[1], others[1],
-    )
-    back = [swap(x, 1) for x in back]
-    grads = [pltpu.with_memory_space_constraint(x, pltpu.HBM) for x in grads]
+    kept, *rest = call(
+        functools.partial(last_kernel, heads, scale),
+        "last_chunk",
+        [stack] + [piece] * 3 + [whole] * 3,
+        table, smalls[1], small_far, first_kept, mines[1], nears[1], *sames[1], others[1],
+        scratch=[output_sems],
+        hbm_out=range(4, 7),
+    )
+    back = [swap(x, 1) for x in rest[:3]]
+    grads = [pltpu.with_memory_space_constraint(x, pltpu.HBM) for x in rest[3:]]
     *grads, bias = call(
         output_kernel,
         "outputs",

time: 35.6 us -> 36.3 us (1.020)
  waiting for transfers between devices: 9.23 us -> 12.1 us
  Pallas kernels: 11.1 us -> 9.67 us
  starting transfers between devices: 14.4 us -> 13.7 us
    ppermute x13 -> x12, waiting for transfers between devices: 8.64 us -> 10.3 us  [swap(): return lax.ppermute(x, 'tm', [(i, i ^ bits) for i in range(4)])]
    pallas_call x7 -> x6, Pallas kernels: 11.1 us -> 9.67 us  [call(): pl.pallas_call(kernel, in_specs=[any_spec if j in hbm else vmem_spec for...]
    all_to_all x1, waiting for transfers between devices: 0.59 us -> 1.8 us  [by_chips(): lax.all_to_all(shares, tuple((axis for axis, _ in sizes)), 0, 0, tiled=True)]
    ppermute x13 -> x12, starting transfers between devices: 8.12 us -> 7.73 us  [swap(): return lax.ppermute(x, 'tm', [(i, i ^ bits) for i in range(4)])]
  transfers between devices with their start and end apart: 14 -> 13, of which waited for: 7 -> 8; matrix products, arithmetic and copies ran while one was open for 0% -> 0% of each run, Pallas kernels for 24% -> 20%
where the time goes in v4:
time: 36.3 us; the launch traced here: 36.1 us
  starting transfers between devices  13.7 us (38%)
  waiting for transfers between devices  12.1 us (33%)
  Pallas kernels  9.67 us (27%)
  between operations  0.71 us (2%)
    ppermute x12, waiting for transfers between devices, swap(): return lax.ppermute(x, 'tm', [(i, i ^ bits) for i in range(4)])  10.3 us
    pallas_call x6, Pallas kernels, call(): pl.pallas_call(kernel, in_specs=[any_spec if j in hbm else vmem_spec for...  9.67 us
    ppermute x12, starting transfers between devices, swap(): return lax.ppermute(x, 'tm', [(i, i ^ bits) for i in range(4)])  7.73 us
    all_to_all x1, starting transfers between devices, by_chips(): lax.all_to_all(shares, tuple((axis for axis, _ in sizes)), 0, 0, tiled=True)  5.92 us
    all_to_all x1, waiting for transfers between devices, by_chips(): lax.all_to_all(shares, tuple((axis for axis, _ in sizes)), 0, 0, tiled=True)  1.8 us
  transfers between devices with their start and end apart: 13, of which 8 were waited for; matrix products, arithmetic and copies ran while one was open for 0% of the time, Pallas kernels for 20%

profile of v4, /device:TPU:0, one launch (start us, length us, event | category | flops | bytes accessed | tf_op | source)
XLA Modules:
  0.0 36.1 jit_solution(12772696951343480549)
XLA Ops:
  0.6 1.4 %fetch_theirs.1 = (bf16[4,32,2048]{2,1,0:T(8,128)(2,1)S(1)}, bf16[4,32,2048]{2,1,0:T(8,128)(2,1)S(1)}, bf16[2,32,2048]{2,1,0:T(8,128)(2,1)S(1)}) custom-call(bf16[128,2048]{1,0:T(8,128)(2,1)} %bitcast.15, bf16[128,2048]{1,0:T(8,128)(2,1)} %bitcast.17, bf16[128,2048]{1,0:T(8,128)(2,1)} %bitcast.19, bf16[128,2048]{1,0:T(8,128)(2,1)} %bitcast.21), custom_call_target="tpu_custom_call" | custom-call | flops 1 | bytes 1 | tf_op jit(solution)/shard_map/fetch_theirs/pallas_call | solution.py:538
  2.0 0.5 %collective-permute-start.1 = (bf16[4,32,2048]{2,1,0:T(8,128)(2,1)S(1)}, bf16[4,32,2048]{2,1,0:T(8,128)(2,1)S(1)}, u32[]{:S(2)}, u32[]{:S(2)}) collective-permute-start(bf16[4,32,2048]{2,1,0:T(8,128)(2,1)S(1)} %get-tuple-element.36), channel_id=1, source_target_pairs={{0,8},{8,0},{16,24},{24,16},{1,9},{9,1},{17,25},{25,17},{2,10},{10... | collective-permute-start | bytes 1572872 | tf_op jit(solution)/shard_map/ppermute | solution.py:532
  2.5 0.1 collective-permute-start
  2.6 2.6 %collective-permute-start.4 = (bf16[2,32,2048]{2,1,0:T(8,128)(2,1)S(1)}, bf16[2,32,2048]{2,1,0:T(8,128)(2,1)S(1)}, u32[]{:S(2)}, u32[]{:S(2)}) collective-permute-start(bf16[2,32,2048]{2,1,0:T(8,128)(2,1)S(1)} %get-tuple-element.32.after), channel_id=1, source_target_pairs={{0,24},{8,16},{16,8},{24,0},{1,25},{9,17},{17,9},{25,1},{2,26},{10... | collective-permute-start | bytes 786440 | tf_op jit(solution)/shard_map/ppermute | solution.py:532
  5.3 0.0 copy-start
  5.3 1.4 %fetch_mine.1 = (bf16[4,32,2048]{2,1,0:T(8,128)(2,1)S(1)}, bf16[4,32,2048]{2,1,0:T(8,128)(2,1)S(1)}) custom-call(bf16[128,2048]{1,0:T(8,128)(2,1)} %bitcast.16, bf16[128,2048]{1,0:T(8,128)(2,1)} %bitcast.18, bf16[128,2048]{1,0:T(8,128)(2,1)} %bitcast.20, bf16[128,2048]{1,0:T(8,128)(2,1)} %bitcast.22, bf16[2,32,2048]{2,1,0:T(8,128)(2,1)S(1)} %get-tuple-element.32.after), custom_call_target="tpu_custom_call" | custom-call | flops 1 | bytes 1 | tf_op jit(solution)/shard_map/fetch_mine/pallas_call | solution.py:538
  6.6 0.0 copy-done
  6.6 0.0 collective-permute-done.1.refs_3_.near
  6.7 0.0 collective-permute-done.refs_2_.near
  6.7 1.6 %local_scores.1 = (f32[32,128]{1,0:T(8,128)S(1)}, f32[32,128]{1,0:T(8,128)S(1)}, f32[8,128]{1,0:T(8,128)S(1)}, bf16[2,32,2048]{2,1,0:T(8,128)(2,1)S(1)}, bf16[32...) custom-call(f32[8,128]{1,0:T(8,128)S(1)} %pad.4.table, ...), custom_call_target="tpu_custom_call" | custom-call | flops 1 | bytes 1 | tf_op jit(solution)/shard_map/local_scores/pallas_call | solution.py:538
  8.3 1.0 %collective-permute-start.2 = (bf16[32,2304]{1,0:T(8,128)(2,1)S(1)}, bf16[32,2304]{1,0:T(8,128)(2,1)S(1)}, u32[]{:S(2)}, u32[]{:S(2)}) collective-permute-start(bf16[32,2304]{1,0:T(8,128)(2,1)S(1)} %get-tuple-element.39), channel_id=1, source_target_pairs={{0,16},{8,24},{16,0},{24,8},{1,17},{9,25},{17,1},{25,9},{2,18},{10... | collective-permute-start | bytes 442376 | tf_op jit(solution)/shard_map/ppermute | solution.py:532
  9.3 1.0 %collective-permute-start.3 = (bf16[32,2304]{1,0:T(8,128)(2,1)S(1)}, bf16[32,2304]{1,0:T(8,128)(2,1)S(1)}, u32[]{:S(2)}, u32[]{:S(2)}) collective-permute-start(bf16[32,2304]{1,0:T(8,128)(2,1)S(1)} %get-tuple-element.40), channel_id=1, source_target_pairs={{0,16},{8,24},{16,0},{24,8},{1,17},{9,25},{17,1},{25,9},{2,18},{10... | collective-permute-start | bytes 442376 | tf_op jit(solution)/shard_map/ppermute | solution.py:532
  10.3 1.0 %collective-permute-start.7 = (bf16[2,32,2048]{2,1,0:T(8,128)(2,1)S(1)}, bf16[2,32,2048]{2,1,0:T(8,128)(2,1)S(1)}, u32[]{:S(2)}, u32[]{:S(2)}) collective-permute-start(bf16[2,32,2048]{2,1,0:T(8,128)(2,1)S(1)} %get-tuple-element.46), channel_id=1, source_target_pairs={{0,16},{8,24},{16,0},{24,8},{1,17},{9,25},{17,1},{25,9},{2,18},{10... | collective-permute-start | bytes 786440 | tf_op jit(solution)/shard_map/ppermute | solution.py:532
  11.3 0.2 collective-permute-start.8
  11.5 0.4 %collective-permute-done.4.refs_2_ = bf16[2,32,2048]{2,1,0:T(8,128)(2,1)S(1)} collective-permute-done((bf16[2,32,2048]{2,1,0:T(8,128)(2,1)S(1)}, bf16[2,32,2048]{2,1,0:T(8,128)(2,1)S(1)}, u32[]{:S(2)}, u32[]{:S(2)}) %collective-permute-start.4) | collective-permute-done | bytes 262176 | tf_op jit(solution)/shard_map/ppermute | solution.py:532
  12.0 3.9 %collective-permute-done.2.refs_0_ = bf16[32,2304]{1,0:T(8,128)(2,1)S(1)} collective-permute-done((bf16[32,2304]{1,0:T(8,128)(2,1)S(1)}, bf16[32,2304]{1,0:T(8,128)(2,1)S(1)}, u32[]{:S(2)}, u32[]{:S(2)}) %collective-permute-start.2) | collective-permute-done | bytes 147488 | tf_op jit(solution)/shard_map/ppermute | solution.py:532
  15.8 3.2 %collective-permute-done.3.refs_1_ = bf16[32,2304]{1,0:T(8,128)(2,1)S(1)} collective-permute-done((bf16[32,2304]{1,0:T(8,128)(2,1)S(1)}, bf16[32,2304]{1,0:T(8,128)(2,1)S(1)}, u32[]{:S(2)}, u32[]{:S(2)}) %collective-permute-start.3) | collective-permute-done | bytes 147488 | tf_op jit(solution)/shard_map/ppermute | solution.py:532
  19.0 2.3 %first_chunk.1 = (bf16[3,32,2048]{2,1,0:T(8,128)(2,1)S(1)}, bf16[3,16,2048]{2,1,0:T(8,128)(2,1)}, bf16[3,16,2048]{2,1,0:T(8,128)(2,1)S(1)}, f32[32,128]{1,0:T(8,128)S(1)}, f32[32,8,128]{2,1,0:T(8,128)}) custom-call(f32[8,128]{1,0:T(8,128)S(1)} %pad.4.table, f32[32,128]{1,0:T(8,128)S(1)} %get-tuple-element.37.small, f32[8,128]{1,0:T(8,128)S(1)} %get-tuple-element.38.bias, ...), custom_call_target="tpu_custom_call" | custom-call | flops 1 | bytes 1 | tf_op jit(solution)/shard_map/first_chunk/pallas_call | solution.py:538
  21.3 5.9 %all-to-all-start = ((f32[32,8,128]{2,1,0:T(8,128)}), f32[32,8,128]{2,1,0:T(8,128)S(1)}, u32[]{:S(2)}, u32[]{:S(2)}) async-start(f32[32,8,128]{2,1,0:T(8,128)} %get-tuple-element.52), calls=%async_computation | async-start | bytes 262144 | tf_op jit(solution)/shard_map/all_to_all | solution.py:597
  27.2 0.3 collective-permute-start.5
  27.6 0.3 collective-permute-start.6
  27.8 0.0 collective-permute-done.7.refs_0_
  27.8 1.5 %collective-permute-done.8.refs_1_ = bf16[2,32,2048]{2,1,0:T(8,128)(2,1)S(1)} collective-permute-done((bf16[2,32,2048]{2,1,0:T(8,128)(2,1)S(1)}, bf16[2,32,2048]{2,1,0:T(8,128)(2,1)S(1)}, u32[]{:S(2)}, u32[]{:S(2)}) %collective-permute-start.8) | collective-permute-done | bytes 262176 | tf_op jit(solution)/shard_map/ppermute | solution.py:532
  29.4 1.9 %last_chunk.1 = (bf16[3,32,2048]{2,1,0:T(8,128)(2,1)S(1)}, bf16[32,2048]{1,0:T(8,128)(2,1)S(1)}, bf16[32,2048]{1,0:T(8,128)(2,1)S(1)}, bf16[32,2048]{1,0:T(8,128...) custom-call(f32[8,128]{1,0:T(8,128)S(1)} %pad.4.table, ...), custom_call_target="tpu_custom_call" | custom-call | flops 1 | bytes 1 | tf_op jit(solution)/shard_map/last_chunk/pallas_call | solution.py:538
  31.3 0.2 collective-permute-start.9
  31.4 0.4 %collective-permute-start.10 = (bf16[32,2048]{1,0:T(8,128)(2,1)S(1)}, bf16[32,2048]{1,0:T(8,128)(2,1)S(1)}, u32[]{:S(2)}, u32[]{:S(2)}) collective-permute-start(bf16[32,2048]{1,0:T(8,128)(2,1)S(1)} %get-tuple-element.50), channel_id=1, source_target_pairs={{0,8},{8,0},{16,24},{24,16},{1,9},{9,1},{17,25},{25,17},{2,10},{10... | collective-permute-start | bytes 393224 | tf_op jit(solution)/shard_map/ppermute | solution.py:532
  31.8 0.1 collective-permute-start.11
  31.9 0.0 collective-permute-done.5.refs_0_
  31.9 0.0 collective-permute-done.6.refs_1_
  31.9 0.7 %collective-permute-done.9.refs_3_ = bf16[32,2048]{1,0:T(8,128)(2,1)S(1)} collective-permute-done((bf16[32,2048]{1,0:T(8,128)(2,1)S(1)}, bf16[32,2048]{1,0:T(8,128)(2,1)S(1)}, u32[]{:S(2)}, u32[]{:S(2)}) %collective-permute-start.9) | collective-permute-done | bytes 131104 | tf_op jit(solution)/shard_map/ppermute | solution.py:532
  32.7 0.2 collective-permute-done.10.refs_4_
  32.9 0.3 collective-permute-done.11.refs_5_
  33.2 1.8 %all-to-all-done.refs_6_ = f32[32,8,128]{2,1,0:T(8,128)S(1)} async-done(((f32[32,8,128]{2,1,0:T(8,128)}), f32[32,8,128]{2,1,0:T(8,128)S(1)}, u32[]{:S(2)}, u32[]{:S(2)}) %all-to-all-start) | async-done | bytes 131104 | tf_op jit(solution)/shard_map/all_to_all | solution.py:597
  35.0 1.1 %outputs.1 = (bf16[128,2048]{1,0:T(8,128)(2,1)}, bf16[128,2048]{1,0:T(8,128)(2,1)}, bf16[128,2048]{1,0:T(8,128)(2,1)}, f32[4,16]{1,0:T(4,128)}) custom-call(bf16[3,16,2048]{2,1,0:T(8,128)(2,1)S(1)} %collective-permute-done.5.refs_0_, ...), custom_call_target="tpu_custom_call", output_to_operand_aliasing={{0}: (7, {}), {1}: (8, {}), {2}: (9, {})} | custom-call | flops 1 | bytes 1 | tf_op jit(solution)/shard_map/outputs/pallas_call | solution.py:538
  (1 shorter events, 0.0 us)
Async XLA Ops:
  2.0 4.6 %collective-permute-start.1 = (bf16[4,32,2048]{2,1,0:T(8,128)(2,1)S(1)}, bf16[4,32,2048]{2,1,0:T(8,128)(2,1)S(1)}, u32[]{:S(2)}, u32[]{:S(2)}) collective-permute-start(bf16[4,32,2048]{2,1,0:T(8,128)(2,1)S(1)} %get-tuple-element.36), channel_id=1, source_target_pairs={{0,8},{8,0},{16,24},{24,16},{1,9},{9,1},{17,25},{25,17},{2,10},{10... | collective-permute-start | bytes 1572872 | tf_op jit(solution)/shard_map/ppermute | solution.py:532
  2.5 4.1 %collective-permute-start = (bf16[4,32,2048]{2,1,0:T(8,128)(2,1)S(1)}, bf16[4,32,2048]{2,1,0:T(8,128)(2,1)S(1)}, u32[]{:S(2)}, u32[]{:S(2)}) collective-permute-start(bf16[4,32,2048]{2,1,0:T(8,128)(2,1)S(1)} %get-tuple-element.35.refs_4_), channel_id=1, source_target_pairs={{0,8},{8,0},{16,24},{24,16},{1,9},{9,1},{17,25},{25,17},{2,10},{10... | collective-permute-start | bytes 1572872 | tf_op jit(solution)/shard_map/ppermute | solution.py:532
  2.6 9.3 %collective-permute-start.4 = (bf16[2,32,2048]{2,1,0:T(8,128)(2,1)S(1)}, bf16[2,32,2048]{2,1,0:T(8,128)(2,1)S(1)}, u32[]{:S(2)}, u32[]{:S(2)}) collective-permute-start(bf16[2,32,2048]{2,1,0:T(8,128)(2,1)S(1)} %get-tuple-element.32.after), channel_id=1, source_target_pairs={{0,24},{8,16},{16,8},{24,0},{1,25},{9,17},{17,9},{25,1},{2,26},{10... | collective-permute-start | bytes 786440 | tf_op jit(solution)/shard_map/ppermute | solution.py:532
  5.3 1.4 %copy-start = (f32[16,4]{0,1:T(4,128)S(1)}, f32[16,4]{0,1:T(4,128)}, u32[]{:S(2)}) copy-start(f32[16,4]{0,1:T(4,128)} %param.9) | copy-start | bytes 772
  8.3 7.6 %collective-permute-start.2 = (bf16[32,2304]{1,0:T(8,128)(2,1)S(1)}, bf16[32,2304]{1,0:T(8,128)(2,1)S(1)}, u32[]{:S(2)}, u32[]{:S(2)}) collective-permute-start(bf16[32,2304]{1,0:T(8,128)(2,1)S(1)} %get-tuple-element.39), channel_id=1, source_target_pairs={{0,16},{8,24},{16,0},{24,8},{1,17},{9,25},{17,1},{25,9},{2,18},{10... | collective-permute-start | bytes 442376 | tf_op jit(solution)/shard_map/ppermute | solution.py:532
  9.3 9.7 %collective-permute-start.3 = (bf16[32,2304]{1,0:T(8,128)(2,1)S(1)}, bf16[32,2304]{1,0:T(8,128)(2,1)S(1)}, u32[]{:S(2)}, u32[]{:S(2)}) collective-permute-start(bf16[32,2304]{1,0:T(8,128)(2,1)S(1)} %get-tuple-element.40), channel_id=1, source_target_pairs={{0,16},{8,24},{16,0},{24,8},{1,17},{9,25},{17,1},{25,9},{2,18},{10... | collective-permute-start | bytes 442376 | tf_op jit(solution)/shard_map/ppermute | solution.py:532
  10.3 17.5 %collective-permute-start.7 = (bf16[2,32,2048]{2,1,0:T(8,128)(2,1)S(1)}, bf16[2,32,2048]{2,1,0:T(8,128)(2,1)S(1)}, u32[]{:S(2)}, u32[]{:S(2)}) collective-permute-start(bf16[2,32,2048]{2,1,0:T(8,128)(2,1)S(1)} %get-tuple-element.46), channel_id=1, source_target_pairs={{0,16},{8,24},{16,0},{24,8},{1,17},{9,25},{17,1},{25,9},{2,18},{10... | collective-permute-start | bytes 786440 | tf_op jit(solution)/shard_map/ppermute | solution.py:532
  11.3 18.0 %collective-permute-start.8 = (bf16[2,32,2048]{2,1,0:T(8,128)(2,1)S(1)}, bf16[2,32,2048]{2,1,0:T(8,128)(2,1)S(1)}, u32[]{:S(2)}, u32[]{:S(2)}) collective-permute-start(bf16[2,32,2048]{2,1,0:T(8,128)(2,1)S(1)} %get-tuple-element.47), channel_id=1, source_target_pairs={{0,24},{8,16},{16,8},{24,0},{1,25},{9,17},{17,9},{25,1},{2,26},{10... | collective-permute-start | bytes 786440 | tf_op jit(solution)/shard_map/ppermute | solution.py:532
  21.3 13.7 %all-to-all-start = ((f32[32,8,128]{2,1,0:T(8,128)}), f32[32,8,128]{2,1,0:T(8,128)S(1)}, u32[]{:S(2)}, u32[]{:S(2)}) async-start(f32[32,8,128]{2,1,0:T(8,128)} %get-tuple-element.52), calls=%async_computation | async-start | bytes 262144 | tf_op jit(solution)/shard_map/all_to_all | solution.py:597
  27.2 4.7 %collective-permute-start.5 = (bf16[3,16,2048]{2,1,0:T(8,128)(2,1)}, bf16[3,16,2048]{2,1,0:T(8,128)(2,1)S(1)}, u32[]{:S(2)}, u32[]{:S(2)}) collective-permute-start(bf16[3,16,2048]{2,1,0:T(8,128)(2,1)} %get-tuple-element.41), channel_id=1, source_target_pairs={{0,8},{8,0},{16,24},{24,16},{1,9},{9,1},{17,25},{25,17},{2,10},{10... | collective-permute-start | bytes 589832 | tf_op jit(solution)/shard_map/ppermute | solution.py:532
  27.6 4.4 %collective-permute-start.6 = (bf16[3,16,2048]{2,1,0:T(8,128)(2,1)S(1)}, bf16[3,16,2048]{2,1,0:T(8,128)(2,1)S(1)}, u32[]{:S(2)}, u32[]{:S(2)}) collective-permute-start(bf16[3,16,2048]{2,1,0:T(8,128)(2,1)S(1)} %get-tuple-element.42), channel_id=1, source_target_pairs={{0,8},{8,0},{16,24},{24,16},{1,9},{9,1},{17,25},{25,17},{2,10},{10... | collective-permute-start | bytes 589832 | tf_op jit(solution)/shard_map/ppermute | solution.py:532
  31.3 1.4 %collective-permute-start.9 = (bf16[32,2048]{1,0:T(8,128)(2,1)S(1)}, bf16[32,2048]{1,0:T(8,128)(2,1)S(1)}, u32[]{:S(2)}, u32[]{:S(2)}) collective-permute-start(bf16[32,2048]{1,0:T(8,128)(2,1)S(1)} %get-tuple-element.49), channel_id=1, source_target_pairs={{0,8},{8,0},{16,24},{24,16},{1,9},{9,1},{17,25},{25,17},{2,10},{10... | collective-permute-start | bytes 393224 | tf_op jit(solution)/shard_map/ppermute | solution.py:532
  31.4 1.4 %collective-permute-start.10 = (bf16[32,2048]{1,0:T(8,128)(2,1)S(1)}, bf16[32,2048]{1,0:T(8,128)(2,1)S(1)}, u32[]{:S(2)}, u32[]{:S(2)}) collective-permute-start(bf16[32,2048]{1,0:T(8,128)(2,1)S(1)} %get-tuple-element.50), channel_id=1, source_target_pairs={{0,8},{8,0},{16,24},{24,16},{1,9},{9,1},{17,25},{25,17},{2,10},{10... | collective-permute-start | bytes 393224 | tf_op jit(solution)/shard_map/ppermute | solution.py:532
  31.8 1.3 %collective-permute-start.11 = (bf16[32,2048]{1,0:T(8,128)(2,1)S(1)}, bf16[32,2048]{1,0:T(8,128)(2,1)S(1)}, u32[]{:S(2)}, u32[]{:S(2)}) collective-permute-start(bf16[32,2048]{1,0:T(8,128)(2,1)S(1)} %get-tuple-element.51), channel_id=1, source_target_pairs={{0,8},{8,0},{16,24},{24,16},{1,9},{9,1},{17,25},{25,17},{2,10},{10... | collective-permute-start | bytes 393224 | tf_op jit(solution)/shard_map/ppermute | solution.py:532

commit v5 on v3

--- a/solution.py
+++ b/solution.py
@@ -108,8 +108,10 @@
     for head in range(heads):
         at = slice(head * LANES, (head + 1) * LANES)
         here = place == head
-        load = lambda refs: [ref[at].astype(jnp.float32) for ref in refs]
-        q, k, o, v = load(queries), load(keys), load(grads), load(values)
+        load = lambda refs, used: {j: refs[j][at].astype(jnp.float32) for j in used}
+        late, early = {t for t, _ in pairs}, {u for _, u in pairs}
+        q, k = load(queries, sorted(late)), load(keys, sorted(early))
+        o, v = load(grads, sorted(late)), load(values, sorted(early))
         for j, (t, u) in enumerate(pairs):
             score = jnp.sum(q[t] * k[u], axis=1, keepdims=True)
             held[j] = jnp.where(here, score, held[j])
@@ -146,11 +148,11 @@
 
 
 def tiles_of(refs, row):
-    return tuple(ref.at_rows(row) for ref in refs)
+    return tuple(ref if ref is None else ref.at_rows(row) for ref in refs)
 
 
 def shifted(refs, start):
-    return tuple(Shifted(ref, start) for ref in refs)
+    return tuple(ref if ref is None else Shifted(ref, start) for ref in refs)
 
 
 def soft_row(scores, gains):
@@ -170,8 +172,10 @@
 CROSS = ((0, 0), (0, 1), (1, 0), (1, 1))
 
 
-def unpack(packed, heads):
-    return [packed if j == 0 else pltpu.roll(packed, LANES - heads * j, axis=1) for j in range(6)]
+def unpack(packed, heads, count=6):
+    return [
+        packed if j == 0 else pltpu.roll(packed, LANES - heads * j, axis=1) for j in range(count)
+    ]
 
 
 def bias_lines(terms):
@@ -313,16 +317,62 @@
 EARLY, LATE = 14, 10
 
 
-def score_tile(heads, scale, chip, a, b, table, small_own, small_far):
+def cross_sides(chip, a, b):
+    if chip == 0:
+        return ((a[4], a[5]), (b[4], b[5])), ((a[1], a[2]), (b[1], b[2]))
+    return ((a[0], a[3]), (b[0], b[3])), ((a[4], a[5]), (b[4], b[5]))
+
+
+def far_pairs(chip, parity):
+    return [pair for pair in CROSS if pair[chip] == parity]
+
+
+def cross_dots(queries, keys, pairs, heads):
+    return pair_dots(
+        [x[0] for x in queries], [x[0] for x in keys],
+        [x[1] for x in queries], [x[1] for x in keys], pairs, heads,
+    )
+
+
+def piece_kernel(heads, same, mine, near, *refs):
+    far, out = refs[:-1], refs[-1]
+    piece = far if len(far) == 2 else planes(far[0])
+    own, other = planes(mine), planes(near)
+    if same:
+        own, other = own + piece, other + (None, None)
+    else:
+        own, other = own + (None, None), other + piece
+    own, other = shifted(own, 0), shifted(other, 0)
+
+    def work(chip, a, b):
+        parity = int((a is own) != same)
+
+        def tile(row):
+            queries, keys = cross_sides(chip, tiles_of(a, row), tiles_of(b, row))
+            held = cross_dots(queries, keys, far_pairs(chip, parity), heads)
+            total = held[0]
+            for j in range(1, 4):
+                total = total + pltpu.roll(held[j], heads * j, axis=1)
+            out[tile_at(row), :] = total
+
+        over_tiles(out.shape[0], tile)
+
+    with_frames(own, other, work)
+
+
+def score_tile(heads, scale, chip, a, b, table, small_own, small_far, known, parity):
     offset = [table[d : d + 1, :] for d in range(4)]
-    if chip == 0:
-        queries, keys = ((a[4], a[5]), (b[4], b[5])), ((a[1], a[2]), (b[1], b[2]))
-    else:
-        queries, keys = ((a[0], a[3]), (b[0], b[3])), ((a[4], a[5]), (b[4], b[5]))
-    held = pair_dots(
-        [x[0] for x in queries], [x[0] for x in keys],
-        [x[1] for x in queries], [x[1] for x in keys], CROSS, heads,
-    )
+    queries, keys = cross_sides(chip, a, b)
+    held = [None] * 8
+    for pairs, values in (
+        (far_pairs(chip, parity), known),
+        (far_pairs(chip, 1 - parity), None),
+    ):
+        if values is None:
+            values = cross_dots(queries, keys, pairs, heads)
+        for j, pair in enumerate(pairs):
+            held[CROSS.index(pair)] = values[j]
+            held[4 + CROSS.index(pair)] = values[2 + j]
     diag = unpack(small_far if chip == 0 else small_own, heads)
     score = lambda j, d: held[j] * scale + offset[d]
     p2, d2 = soft_row(
@@ -406,10 +456,11 @@
     return unpacked_small(*(ref[rows, at] for ref in pair_of(far[:-1])), heads)
 
 
-def score_kernel(heads, scale, table, small, bias, mine, near, *refs):
-    far, (out_items, out_shares, out_small, out_lines), lines_ref = refs[:3], refs[3:7], refs[7]
+def score_kernel(heads, scale, known, table, small, bias, mine, near, *refs):
+    far, (out_items, out_shares, out_small), lines_ref = refs[:3], refs[3:6], refs[6]
     size, width = mine.shape[1:]
     lines_ref[...] = bias[...]
+    own, neighbour = frames_of(mine, near, far)
 
     def work(chip, a, b):
         def tile(row):
@@ -417,6 +468,7 @@
             items, lines = score_tile(
                 heads, scale, chip, tiles_of(a, row), tiles_of(b, row), table,
                 small[rows, :], far_small(far, rows, width, heads, 0),
+                unpack(known[rows, :], heads, 4), int(a is own),
             )
             out_small[rows, :] = far_small(far, rows, width, heads, 1)
             for j, item in enumerate(items):
@@ -425,8 +477,7 @@
 
         over_tiles(size, tile)
 
-    with_frames(*frames_of(mine, near, far), work)
-    out_lines[...] = lines_ref[...]
+    with_frames(own, neighbour, work)
     for j in range(out_shares.shape[0]):
         out_shares[j] = lines_ref[: out_shares.shape[1], :]
 
@@ -472,7 +523,7 @@
         copy.wait()
 
 
-def whole_kernel(heads, scale, after, table, small, small_far, mine, near, *refs):
+def whole_kernel(heads, scale, known, table, small, small_far, mine, near, *refs):
     far, out_own, out_others = refs[:2], refs[2], refs[3:6]
     own, neighbour = frames_of(mine, near, far)
     own_out, other_out = shifted(planes(out_own), 0), shifted(out_others, 0)
@@ -483,7 +534,8 @@
         def tile(row):
             at, bt, rows = tiles_of(a, row), tiles_of(b, row), tile_at(row)
             items, _ = score_tile(
-                heads, scale, chip, at, bt, table, small[rows, :], small_far[rows, :]
+                heads, scale, chip, at, bt, table, small[rows, :], small_far[rows, :],
+                unpack(known[rows, :], heads, 4), int(a is not own),
             )
             gradient_tile(
                 heads, scale, chip, at, bt, items, tiles_of(out_a, row), tiles_of(out_b, row)
@@ -582,16 +634,21 @@
     stack, piece = shape(3, size, width), shape(size, width)
     output_sems = pltpu.SemaphoreType.DMA((13,))
     first = (mines[0], nears[0], *sames[0], others[0])
-    items, shares, small_far, token = call(
+    (known,) = call(
+        functools.partial(piece_kernel, heads, False),
+        "first_dots",
+        [shape(size, LANES, dtype=wide)],
+        mines[0], nears[0], others[0],
+    )
+    items, shares, small_far = call(
         functools.partial(score_kernel, heads, scale),
         "scores",
         [
             shape(EARLY, size, LANES),
             shape(math.prod(count for _, count in sizes), 8, LANES, dtype=wide),
             shape(size, LANES, dtype=wide),
-            lines,
         ],
-        table, smalls[0], bias, *first,
+        known, table, smalls[0], bias, *first,
         scratch=[pltpu.VMEM((8, LANES), wide)],
     )
     shares = lax.all_to_all(shares, tuple(axis for axis, _ in sizes), 0, 0, tiled=True)
@@ -606,11 +663,17 @@
     grads = (grad_queries, grad_keys, grad_values)
     first_backs = [swap(x, 1) for x in back]
 
+    (known_last,) = call(
+        functools.partial(piece_kernel, heads, True),
+        "last_dots",
+        [shape(size, LANES, dtype=wide)],
+        mines[1], nears[1], *sames[1],
+    )
     kept, *back = call(
         functools.partial(whole_kernel, heads, scale),
         "scores_and_gradients",
         [stack] + [piece] * 3,
-        swap(token, 1), table, smalls[1], small_far, mines[1], nears[1], *sames[1], others[1],
+        known_last, table, smalls[1], small_far, mines[1], nears[1], *sames[1], others[1],
     )
     back = [swap(x, 1) for x in back]
     grads = [pltpu.with_memory_space_constraint(x, pltpu.HBM) for x in grads]

time: 35.6 us -> 35.4 us (level)
  Pallas kernels: 11.1 us -> 11.6 us
  starting transfers between devices: 14.4 us -> 13.9 us
  waiting for transfers between devices: 9.23 us -> 8.87 us
    pallas_call x7 -> x9, Pallas kernels: 11.1 us -> 11.6 us  [call(): pl.pallas_call(kernel, in_specs=[any_spec if j in hbm else vmem_spec for...]
    ppermute x13 -> x12, waiting for transfers between devices: 8.64 us -> 8.22 us  [swap(): return lax.ppermute(x, 'tm', [(i, i ^ bits) for i in range(4)])]
    ppermute x13 -> x12, starting transfers between devices: 8.12 us -> 7.7 us  [swap(): return lax.ppermute(x, 'tm', [(i, i ^ bits) for i in range(4)])]
  transfers between devices with their start and end apart: 14 -> 13, of which waited for: 7 -> 7; matrix products, arithmetic and copies ran while one was open for 0% -> 0% of each run, Pallas kernels for 24% -> 26%
where the time goes in v5:
time: 35.4 us; the launch traced here: 35.2 us
  starting transfers between devices  13.9 us (39%)
  Pallas kernels  11.6 us (33%)
  waiting for transfers between devices  8.87 us (25%)
  between operations  0.72 us (2%)
    pallas_call x9, Pallas kernels, call(): pl.pallas_call(kernel, in_specs=[any_spec if j in hbm else vmem_spec for...  11.6 us
    ppermute x12, waiting for transfers between devices, swap(): return lax.ppermute(x, 'tm', [(i, i ^ bits) for i in range(4)])  8.22 us
    ppermute x12, starting transfers between devices, swap(): return lax.ppermute(x, 'tm', [(i, i ^ bits) for i in range(4)])  7.7 us
    all_to_all x1, starting transfers between devices, by_chips(): lax.all_to_all(shares, tuple((axis for axis, _ in sizes)), 0, 0, tiled=True)  6.25 us
  transfers between devices with their start and end apart: 13, of which 7 were waited for; matrix products, arithmetic and copies ran while one was open for 0% of the time, Pallas kernels for 26%

profile of v5, /device:TPU:0, one launch (start us, length us, event | category | flops | bytes accessed | tf_op | source)
XLA Modules:
  0.0 35.2 jit_solution(4069003973661889438)
XLA Ops:
  0.6 1.4 %fetch_theirs.1 = (bf16[4,32,2048]{2,1,0:T(8,128)(2,1)S(1)}, bf16[4,32,2048]{2,1,0:T(8,128)(2,1)S(1)}, bf16[2,32,2048]{2,1,0:T(8,128)(2,1)S(1)}) custom-call(bf16[128,2048]{1,0:T(8,128)(2,1)} %bitcast.15, bf16[128,2048]{1,0:T(8,128)(2,1)} %bitcast.17, bf16[128,2048]{1,0:T(8,128)(2,1)} %bitcast.19, bf16[128,2048]{1,0:T(8,128)(2,1)} %bitcast.21), custom_call_target="tpu_custom_call" | custom-call | flops 1 | bytes 1 | tf_op jit(solution)/shard_map/fetch_theirs/pallas_call | solution.py:592
  2.0 0.5 %collective-permute-start = (bf16[4,32,2048]{2,1,0:T(8,128)(2,1)S(1)}, bf16[4,32,2048]{2,1,0:T(8,128)(2,1)S(1)}, u32[]{:S(2)}, u32[]{:S(2)}) collective-permute-start(bf16[4,32,2048]{2,1,0:T(8,128)(2,1)S(1)} %get-tuple-element.34.refs_4_), channel_id=1, source_target_pairs={{0,8},{8,0},{16,24},{24,16},{1,9},{9,1},{17,25},{25,17},{2,10},{10... | collective-permute-start | bytes 1572872 | tf_op jit(solution)/shard_map/ppermute | solution.py:586
  2.5 0.1 collective-permute-start.2
  2.6 2.6 %collective-permute-start.1 = (bf16[2,32,2048]{2,1,0:T(8,128)(2,1)S(1)}, bf16[2,32,2048]{2,1,0:T(8,128)(2,1)S(1)}, u32[]{:S(2)}, u32[]{:S(2)}) collective-permute-start(bf16[2,32,2048]{2,1,0:T(8,128)(2,1)S(1)} %get-tuple-element.32.after), channel_id=1, source_target_pairs={{0,24},{8,16},{16,8},{24,0},{1,25},{9,17},{17,9},{25,1},{2,26},{10... | collective-permute-start | bytes 786440 | tf_op jit(solution)/shard_map/ppermute | solution.py:586
  5.3 0.0 copy-start
  5.3 1.4 %fetch_mine.1 = (bf16[4,32,2048]{2,1,0:T(8,128)(2,1)S(1)}, bf16[4,32,2048]{2,1,0:T(8,128)(2,1)S(1)}) custom-call(bf16[128,2048]{1,0:T(8,128)(2,1)} %bitcast.16, bf16[128,2048]{1,0:T(8,128)(2,1)} %bitcast.18, bf16[128,2048]{1,0:T(8,128)(2,1)} %bitcast.20, bf16[128,2048]{1,0:T(8,128)(2,1)} %bitcast.22, bf16[2,32,2048]{2,1,0:T(8,128)(2,1)S(1)} %get-tuple-element.32.after), custom_call_target="tpu_custom_call" | custom-call | flops 1 | bytes 1 | tf_op jit(solution)/shard_map/fetch_mine/pallas_call | solution.py:592
  6.6 0.0 copy-done
  6.6 0.0 collective-permute-done.near.refs_2_
  6.7 0.0 collective-permute-done.2.refs_3_.near
  6.7 2.3 %local_scores.1 = (f32[32,128]{1,0:T(8,128)S(1)}, f32[32,128]{1,0:T(8,128)S(1)}, f32[8,128]{1,0:T(8,128)S(1)}, bf16[2,32,2048]{2,1,0:T(8,128)(2,1)}, bf16[32,230...) custom-call(f32[8,128]{1,0:T(8,128)S(1)} %pad.4.table, ...), custom_call_target="tpu_custom_call" | custom-call | flops 1 | bytes 1 | tf_op jit(solution)/shard_map/local_scores/pallas_call | solution.py:592
  9.0 1.0 %collective-permute-start.3 = (bf16[32,2304]{1,0:T(8,128)(2,1)S(1)}, bf16[32,2304]{1,0:T(8,128)(2,1)S(1)}, u32[]{:S(2)}, u32[]{:S(2)}) collective-permute-start(bf16[32,2304]{1,0:T(8,128)(2,1)S(1)} %get-tuple-element.39), channel_id=1, source_target_pairs={{0,16},{8,24},{16,0},{24,8},{1,17},{9,25},{17,1},{25,9},{2,18},{10... | collective-permute-start | bytes 442376 | tf_op jit(solution)/shard_map/ppermute | solution.py:586
  10.0 1.0 %collective-permute-start.4 = (bf16[32,2304]{1,0:T(8,128)(2,1)S(1)}, bf16[32,2304]{1,0:T(8,128)(2,1)S(1)}, u32[]{:S(2)}, u32[]{:S(2)}) collective-permute-start(bf16[32,2304]{1,0:T(8,128)(2,1)S(1)} %get-tuple-element.40), channel_id=1, source_target_pairs={{0,16},{8,24},{16,0},{24,8},{1,17},{9,25},{17,1},{25,9},{2,18},{10... | collective-permute-start | bytes 442376 | tf_op jit(solution)/shard_map/ppermute | solution.py:586
  11.0 1.0 %collective-permute-start.7 = (bf16[2,32,2048]{2,1,0:T(8,128)(2,1)}, bf16[2,32,2048]{2,1,0:T(8,128)(2,1)S(1)}, u32[]{:S(2)}, u32[]{:S(2)}) collective-permute-start(bf16[2,32,2048]{2,1,0:T(8,128)(2,1)} %get-tuple-element.44), channel_id=1, source_target_pairs={{0,16},{8,24},{16,0},{24,8},{1,17},{9,25},{17,1},{25,9},{2,18},{10... | collective-permute-start | bytes 786440 | tf_op jit(solution)/shard_map/ppermute | solution.py:586
  12.1 0.2 collective-permute-start.8
  12.3 0.0 collective-permute-done.1.refs_0_.refs_2_
  12.3 0.5 %first_dots.1.known = f32[32,128]{1,0:T(8,128)S(1)} custom-call(bf16[4,32,2048]{2,1,0:T(8,128)(2,1)S(1)} %get-tuple-element.33.mine.refs_0_, bf16[4,32,2048]{2,1,0:T(8,128)(2,1)S(1)} %collective-permute-done.near.refs_2_, bf16[2,32,2048]{2,1,0:T(8,128)(2,1)S(1)} %collective-permute-done.1.refs_0_.refs_2_), custom_call_target="tpu_custom_call" | custom-call | flops 1 | bytes 1 | tf_op jit(solution)/shard_map/first_dots/pallas_call | solution.py:592
  12.8 2.9 %collective-permute-done.3.refs_0_ = bf16[32,2304]{1,0:T(8,128)(2,1)S(1)} collective-permute-done((bf16[32,2304]{1,0:T(8,128)(2,1)S(1)}, bf16[32,2304]{1,0:T(8,128)(2,1)S(1)}, u32[]{:S(2)}, u32[]{:S(2)}) %collective-permute-start.3) | collective-permute-done | bytes 147488 | tf_op jit(solution)/shard_map/ppermute | solution.py:586
  15.7 3.2 %collective-permute-done.4.refs_1_ = bf16[32,2304]{1,0:T(8,128)(2,1)S(1)} collective-permute-done((bf16[32,2304]{1,0:T(8,128)(2,1)S(1)}, bf16[32,2304]{1,0:T(8,128)(2,1)S(1)}, u32[]{:S(2)}, u32[]{:S(2)}) %collective-permute-start.4) | collective-permute-done | bytes 147488 | tf_op jit(solution)/shard_map/ppermute | solution.py:586
  18.8 1.3 %scores.1 = (bf16[14,32,128]{2,1,0:T(8,128)(2,1)S(1)}, f32[32,8,128]{2,1,0:T(8,128)}, f32[32,128]{1,0:T(8,128)S(1)}) custom-call(f32[32,128]{1,0:T(8,128)S(1)} %first_dots.1.known, f32[8,128]{1,0:T(8,128)S(1)} %pad.4.table, f32[32,128]{1,0:T(8,128)S(1)} %get-tuple-element.37.small, f32[8,128]{1,0:T(8,128)S(1)} %get-tuple-element.38.bias, ...), custom_call_target="tpu_custom_call" | custom-call | flops 1 | bytes 1 | tf_op jit(solution)/shard_map/scores/pallas_call | solution.py:592
  20.1 6.2 %all-to-all-start = ((f32[32,8,128]{2,1,0:T(8,128)}), f32[32,8,128]{2,1,0:T(8,128)S(1)}, u32[]{:S(2)}, u32[]{:S(2)}) async-start(f32[32,8,128]{2,1,0:T(8,128)} %get-tuple-element.52), calls=%async_computation | async-start | bytes 262144 | tf_op jit(solution)/shard_map/all_to_all | solution.py:654
  26.3 1.6 %gradients.1 = (bf16[3,16,2048]{2,1,0:T(8,128)(2,1)S(1)}, bf16[3,16,2048]{2,1,0:T(8,128)(2,1)S(1)}, bf16[128,2048]{1,0:T(8,128)(2,1)}, bf16[128,2048]{1,0:T(8,128)(2,1)}, bf16[128,2048]{1,0:T(8,128)(2,1)}) custom-call(bf16[14,32,128]{2,1,0:T(8,128)(2,1)S(1)} %get-tuple-element.41.items_ref, bf16[4,32,2048]{2,1,0:T(8,128)(2,1)S(1)} %get-tuple-element.33.mine.refs_0_, ...), custom_call_target="tpu_custom_call" | custom-call | flops 1 | bytes 1 | tf_op jit(solution)/shard_map/gradients/pallas_call | solution.py:592
  28.0 0.3 collective-permute-start.5
  28.3 0.3 collective-permute-start.6
  28.6 0.0 collective-permute-done.7.refs_0_
  28.6 0.5 %last_dots.1.known = f32[32,128]{1,0:T(8,128)S(1)} custom-call(bf16[4,32,2048]{2,1,0:T(8,128)(2,1)S(1)} %get-tuple-element.35.refs_1_.mine, bf16[4,32,2048]{2,1,0:T(8,128)(2,1)S(1)} %collective-permute-done.2.refs_3_.near, bf16[2,32,2048]{2,1,0:T(8,128)(2,1)S(1)} %collective-permute-done.7.refs_0_), custom_call_target="tpu_custom_call" | custom-call | flops 1 | bytes 1 | tf_op jit(solution)/shard_map/last_dots/pallas_call | solution.py:592
  29.1 0.9 %collective-permute-done.8.refs_1_ = bf16[2,32,2048]{2,1,0:T(8,128)(2,1)S(1)} collective-permute-done((bf16[2,32,2048]{2,1,0:T(8,128)(2,1)}, bf16[2,32,2048]{2,1,0:T(8,128)(2,1)S(1)}, u32[]{:S(2)}, u32[]{:S(2)}) %collective-permute-start.8) | collective-permute-done | bytes 262176 | tf_op jit(solution)/shard_map/ppermute | solution.py:586
  30.0 1.5 %scores_and_gradients.1 = (bf16[3,32,2048]{2,1,0:T(8,128)(2,1)S(1)}, bf16[32,2048]{1,0:T(8,128)(2,1)S(1)}, bf16[32,2048]{1,0:T(8,128)(2,1)S(1)}, bf16[32,2048]{1,0:T(8,128)(2,1)S(1)}) custom-call(f32[32,128]{1,0:T(8,128)S(1)} %last_dots.1.known, f32[8,128]{1,0:T(8,128)S(1)} %pad.4.table, f32[32,128]{1,0:T(8,128)S(1)} %get-tuple-element.45.small, ...), custom_call_target="tpu_custom_call" | custom-call | flops 1 | bytes 1 | tf_op jit(solution)/shard_map/scores_and_gradients/pallas_call | solution.py:592
  31.5 0.1 collective-permute-start.10
  31.6 0.5 %collective-permute-start.11 = (bf16[32,2048]{1,0:T(8,128)(2,1)S(1)}, bf16[32,2048]{1,0:T(8,128)(2,1)S(1)}, u32[]{:S(2)}, u32[]{:S(2)}) collective-permute-start(bf16[32,2048]{1,0:T(8,128)(2,1)S(1)} %get-tuple-element.51), channel_id=1, source_target_pairs={{0,8},{8,0},{16,24},{24,16},{1,9},{9,1},{17,25},{25,17},{2,10},{10... | collective-permute-start | bytes 393224 | tf_op jit(solution)/shard_map/ppermute | solution.py:586
  32.1 0.1 collective-permute-start.9
  32.1 0.0 collective-permute-done.5.refs_0_
  32.1 0.0 collective-permute-done.6.refs_1_
  32.2 0.8 %collective-permute-done.10.refs_4_ = bf16[32,2048]{1,0:T(8,128)(2,1)S(1)} collective-permute-done((bf16[32,2048]{1,0:T(8,128)(2,1)S(1)}, bf16[32,2048]{1,0:T(8,128)(2,1)S(1)}, u32[]{:S(2)}, u32[]{:S(2)}) %collective-permute-start.10) | collective-permute-done | bytes 131104 | tf_op jit(solution)/shard_map/ppermute | solution.py:586
  32.9 0.2 collective-permute-done.11.refs_5_
  33.1 0.3 collective-permute-done.9.refs_3_
  33.4 0.7 %all-to-all-done.refs_6_ = f32[32,8,128]{2,1,0:T(8,128)S(1)} async-done(((f32[32,8,128]{2,1,0:T(8,128)}), f32[32,8,128]{2,1,0:T(8,128)S(1)}, u32[]{:S(2)}, u32[]{:S(2)}) %all-to-all-start) | async-done | bytes 131104 | tf_op jit(solution)/shard_map/all_to_all | solution.py:654
  34.1 1.1 %outputs.1 = (bf16[128,2048]{1,0:T(8,128)(2,1)}, bf16[128,2048]{1,0:T(8,128)(2,1)}, bf16[128,2048]{1,0:T(8,128)(2,1)}, f32[4,16]{1,0:T(4,128)}) custom-call(bf16[3,16,2048]{2,1,0:T(8,128)(2,1)S(1)} %collective-permute-done.5.refs_0_, ...), custom_call_target="tpu_custom_call", output_to_operand_aliasing={{0}: (7, {}), {1}: (8, {}), {2}: (9, {})} | custom-call | flops 1 | bytes 1 | tf_op jit(solution)/shard_map/outputs/pallas_call | solution.py:592
  (1 shorter events, 0.0 us)
Async XLA Ops:
  2.0 4.6 %collective-permute-start = (bf16[4,32,2048]{2,1,0:T(8,128)(2,1)S(1)}, bf16[4,32,2048]{2,1,0:T(8,128)(2,1)S(1)}, u32[]{:S(2)}, u32[]{:S(2)}) collective-permute-start(bf16[4,32,2048]{2,1,0:T(8,128)(2,1)S(1)} %get-tuple-element.34.refs_4_), channel_id=1, source_target_pairs={{0,8},{8,0},{16,24},{24,16},{1,9},{9,1},{17,25},{25,17},{2,10},{10... | collective-permute-start | bytes 1572872 | tf_op jit(solution)/shard_map/ppermute | solution.py:586
  2.5 4.1 %collective-permute-start.2 = (bf16[4,32,2048]{2,1,0:T(8,128)(2,1)S(1)}, bf16[4,32,2048]{2,1,0:T(8,128)(2,1)S(1)}, u32[]{:S(2)}, u32[]{:S(2)}) collective-permute-start(bf16[4,32,2048]{2,1,0:T(8,128)(2,1)S(1)} %get-tuple-element.36), channel_id=1, source_target_pairs={{0,8},{8,0},{16,24},{24,16},{1,9},{9,1},{17,25},{25,17},{2,10},{10... | collective-permute-start | bytes 1572872 | tf_op jit(solution)/shard_map/ppermute | solution.py:586
  2.6 9.6 %collective-permute-start.1 = (bf16[2,32,2048]{2,1,0:T(8,128)(2,1)S(1)}, bf16[2,32,2048]{2,1,0:T(8,128)(2,1)S(1)}, u32[]{:S(2)}, u32[]{:S(2)}) collective-permute-start(bf16[2,32,2048]{2,1,0:T(8,128)(2,1)S(1)} %get-tuple-element.32.after), channel_id=1, source_target_pairs={{0,24},{8,16},{16,8},{24,0},{1,25},{9,17},{17,9},{25,1},{2,26},{10... | collective-permute-start | bytes 786440 | tf_op jit(solution)/shard_map/ppermute | solution.py:586
  5.3 1.4 %copy-start = (f32[16,4]{0,1:T(4,128)S(1)}, f32[16,4]{0,1:T(4,128)}, u32[]{:S(2)}) copy-start(f32[16,4]{0,1:T(4,128)} %param.9) | copy-start | bytes 772
  9.0 6.7 %collective-permute-start.3 = (bf16[32,2304]{1,0:T(8,128)(2,1)S(1)}, bf16[32,2304]{1,0:T(8,128)(2,1)S(1)}, u32[]{:S(2)}, u32[]{:S(2)}) collective-permute-start(bf16[32,2304]{1,0:T(8,128)(2,1)S(1)} %get-tuple-element.39), channel_id=1, source_target_pairs={{0,16},{8,24},{16,0},{24,8},{1,17},{9,25},{17,1},{25,9},{2,18},{10... | collective-permute-start | bytes 442376 | tf_op jit(solution)/shard_map/ppermute | solution.py:586
  10.0 8.8 %collective-permute-start.4 = (bf16[32,2304]{1,0:T(8,128)(2,1)S(1)}, bf16[32,2304]{1,0:T(8,128)(2,1)S(1)}, u32[]{:S(2)}, u32[]{:S(2)}) collective-permute-start(bf16[32,2304]{1,0:T(8,128)(2,1)S(1)} %get-tuple-element.40), channel_id=1, source_target_pairs={{0,16},{8,24},{16,0},{24,8},{1,17},{9,25},{17,1},{25,9},{2,18},{10... | collective-permute-start | bytes 442376 | tf_op jit(solution)/shard_map/ppermute | solution.py:586
  11.0 17.5 %collective-permute-start.7 = (bf16[2,32,2048]{2,1,0:T(8,128)(2,1)}, bf16[2,32,2048]{2,1,0:T(8,128)(2,1)S(1)}, u32[]{:S(2)}, u32[]{:S(2)}) collective-permute-start(bf16[2,32,2048]{2,1,0:T(8,128)(2,1)} %get-tuple-element.44), channel_id=1, source_target_pairs={{0,16},{8,24},{16,0},{24,8},{1,17},{9,25},{17,1},{25,9},{2,18},{10... | collective-permute-start | bytes 786440 | tf_op jit(solution)/shard_map/ppermute | solution.py:586
  12.1 17.9 %collective-permute-start.8 = (bf16[2,32,2048]{2,1,0:T(8,128)(2,1)}, bf16[2,32,2048]{2,1,0:T(8,128)(2,1)S(1)}, u32[]{:S(2)}, u32[]{:S(2)}) collective-permute-start(bf16[2,32,2048]{2,1,0:T(8,128)(2,1)} %get-tuple-element.47), channel_id=1, source_target_pairs={{0,24},{8,16},{16,8},{24,0},{1,25},{9,17},{17,9},{25,1},{2,26},{10... | collective-permute-start | bytes 786440 | tf_op jit(solution)/shard_map/ppermute | solution.py:586
  20.1 14.0 %all-to-all-start = ((f32[32,8,128]{2,1,0:T(8,128)}), f32[32,8,128]{2,1,0:T(8,128)S(1)}, u32[]{:S(2)}, u32[]{:S(2)}) async-start(f32[32,8,128]{2,1,0:T(8,128)} %get-tuple-element.52), calls=%async_computation | async-start | bytes 262144 | tf_op jit(solution)/shard_map/all_to_all | solution.py:654
  28.0 4.2 %collective-permute-start.5 = (bf16[3,16,2048]{2,1,0:T(8,128)(2,1)S(1)}, bf16[3,16,2048]{2,1,0:T(8,128)(2,1)S(1)}, u32[]{:S(2)}, u32[]{:S(2)}) collective-permute-start(bf16[3,16,2048]{2,1,0:T(8,128)(2,1)S(1)} %get-tuple-element.42), channel_id=1, source_target_pairs={{0,8},{8,0},{16,24},{24,16},{1,9},{9,1},{17,25},{25,17},{2,10},{10... | collective-permute-start | bytes 589832 | tf_op jit(solution)/shard_map/ppermute | solution.py:586
  28.3 3.9 %collective-permute-start.6 = (bf16[3,16,2048]{2,1,0:T(8,128)(2,1)S(1)}, bf16[3,16,2048]{2,1,0:T(8,128)(2,1)S(1)}, u32[]{:S(2)}, u32[]{:S(2)}) collective-permute-start(bf16[3,16,2048]{2,1,0:T(8,128)(2,1)S(1)} %get-tuple-element.43), channel_id=1, source_target_pairs={{0,8},{8,0},{16,24},{24,16},{1,9},{9,1},{17,25},{25,17},{2,10},{10... | collective-permute-start | bytes 589832 | tf_op jit(solution)/shard_map/ppermute | solution.py:586
  31.5 1.4 %collective-permute-start.10 = (bf16[32,2048]{1,0:T(8,128)(2,1)S(1)}, bf16[32,2048]{1,0:T(8,128)(2,1)S(1)}, u32[]{:S(2)}, u32[]{:S(2)}) collective-permute-start(bf16[32,2048]{1,0:T(8,128)(2,1)S(1)} %get-tuple-element.50), channel_id=1, source_target_pairs={{0,8},{8,0},{16,24},{24,16},{1,9},{9,1},{17,25},{25,17},{2,10},{10... | collective-permute-start | bytes 393224 | tf_op jit(solution)/shard_map/ppermute | solution.py:586
  31.6 1.5 %collective-permute-start.11 = (bf16[32,2048]{1,0:T(8,128)(2,1)S(1)}, bf16[32,2048]{1,0:T(8,128)(2,1)S(1)}, u32[]{:S(2)}, u32[]{:S(2)}) collective-permute-start(bf16[32,2048]{1,0:T(8,128)(2,1)S(1)} %get-tuple-element.51), channel_id=1, source_target_pairs={{0,8},{8,0},{16,24},{24,16},{1,9},{9,1},{17,25},{25,17},{2,10},{10... | collective-permute-start | bytes 393224 | tf_op jit(solution)/shard_map/ppermute | solution.py:586
  32.1 1.3 %collective-permute-start.9 = (bf16[32,2048]{1,0:T(8,128)(2,1)S(1)}, bf16[32,2048]{1,0:T(8,128)(2,1)S(1)}, u32[]{:S(2)}, u32[]{:S(2)}) collective-permute-start(bf16[32,2048]{1,0:T(8,128)(2,1)S(1)} %get-tuple-element.49), channel_id=1, source_target_pairs={{0,8},{8,0},{16,24},{24,16},{1,9},{9,1},{17,25},{25,17},{2,10},{10... | collective-permute-start | bytes 393224 | tf_op jit(solution)/shard_map/ppermute | solution.py:586

commit v6 on v5

--- a/solution.py
+++ b/solution.py
@@ -546,23 +546,30 @@
     with_frames(own, neighbour, work)
 
 
-def output_kernel(*refs):
-    first_backs, kept, back, shares = refs[:2], planes(refs[2]), refs[3:6], refs[6]
-    outs, out_bias, total, sems = refs[10:13], *refs[13:]
+def early_output_kernel(*refs):
+    first_backs, kept, outs, sems = refs[:2], planes(refs[2]), refs[6:9], refs[9]
     core = my_place()[0]
     copies = output_copies(core, kept, outs, 1, sems, 0)
-    copies += output_copies(1 - core, back, outs, 1, sems, 3)
     offset = 0
     for j, ref in enumerate(first_backs):
-        copies += output_copies(1 - core, planes(ref), outs, 0, sems, 6 + 3 * j, offset)
+        copies += output_copies(1 - core, planes(ref), outs, 0, sems, 3 + 3 * j, offset)
         offset += ref.shape[1]
+    for copy in copies:
+        copy.start()
+    for copy in copies:
+        copy.wait()
+
+
+def output_kernel(*refs):
+    back, shares, outs, out_bias, total, sems = refs[:3], refs[3], refs[7:10], *refs[10:]
+    copies = output_copies(1 - my_place()[0], back, outs, 1, sems, 0)
     for copy in copies:
         copy.start()
     parts = [shares[j] for j in range(shares.shape[0])]
     while len(parts) > 1:
         parts = [a + b for a, b in zip(parts[::2], parts[1::2])]
     total[...] = parts[0][: total.shape[0], : total.shape[1]]
-    copies.append(pltpu.make_async_copy(total, out_bias, sems.at[12]))
+    copies.append(pltpu.make_async_copy(total, out_bias, sems.at[len(copies)]))
     copies[-1].start()
     for copy in copies:
         copy.wait()
@@ -676,16 +683,26 @@
         known_last, table, smalls[1], small_far, mines[1], nears[1], *sames[1], others[1],
     )
     back = [swap(x, 1) for x in back]
-    grads = [pltpu.with_memory_space_constraint(x, pltpu.HBM) for x in grads]
+    in_hbm = lambda arrays: [pltpu.with_memory_space_constraint(x, pltpu.HBM) for x in arrays]
+    grads = call(
+        early_output_kernel,
+        "early_outputs",
+        [whole] * 3,
+        *first_backs, kept, *in_hbm(grads),
+        scratch=[output_sems],
+        hbm=range(3, 6),
+        hbm_out=range(3),
+        aliases={3 + j: j for j in range(3)},
+    )
     *grads, bias = call(
         output_kernel,
         "outputs",
         [whole] * 3 + [shape(frames, heads, dtype=wide)],
-        *first_backs, kept, *back, shares, *grads,
+        *back, shares, *in_hbm(grads),
         scratch=[pltpu.VMEM((frames, heads), wide), output_sems],
-        hbm=range(7, 10),
+        hbm=range(4, 7),
         hbm_out=range(4),
-        aliases={7 + j: j for j in range(3)},
+        aliases={4 + j: j for j in range(3)},
     )
     return (*[x.reshape(query_vectors.shape) for x in grads], bias.T)
 

time: 35.4 us -> 35.2 us (level)
  waiting for transfers between devices: 8.87 us -> 7.86 us
  Pallas kernels: 11.6 us -> 12.4 us
    ppermute x12, waiting for transfers between devices: 8.22 us -> 7.21 us  [swap(): return lax.ppermute(x, 'tm', [(i, i ^ bits) for i in range(4)])]
    pallas_call x9 -> x10, Pallas kernels: 11.6 us -> 12.4 us  [call(): pl.pallas_call(kernel, in_specs=[any_spec if j in hbm else vmem_spec for...]
  transfers between devices with their start and end apart: 13 -> 13, of which waited for: 7 -> 5; matrix products, arithmetic and copies ran while one was open for 0% -> 0% of each run, Pallas kernels for 26% -> 29%
where the time goes in v6:
time: 35.2 us; the launch traced here: 34.9 us
  starting transfers between devices  13.9 us (39%)
  Pallas kernels  12.4 us (35%)
  waiting for transfers between devices  7.86 us (22%)
  between operations  0.75 us (2%)
    pallas_call x10, Pallas kernels, call(): pl.pallas_call(kernel, in_specs=[any_spec if j in hbm else vmem_spec for...  12.4 us
    ppermute x12, starting transfers between devices, swap(): return lax.ppermute(x, 'tm', [(i, i ^ bits) for i in range(4)])  7.7 us
    ppermute x12, waiting for transfers between devices, swap(): return lax.ppermute(x, 'tm', [(i, i ^ bits) for i in range(4)])  7.21 us
    all_to_all x1, starting transfers between devices, by_chips(): lax.all_to_all(shares, tuple((axis for axis, _ in sizes)), 0, 0, tiled=True)  6.25 us
  transfers between devices with their start and end apart: 13, of which 5 were waited for; matrix products, arithmetic and copies ran while one was open for 0% of the time, Pallas kernels for 29%

profile of v6, /device:TPU:0, one launch (start us, length us, event | category | flops | bytes accessed | tf_op | source)
XLA Modules:
  0.0 34.9 jit_solution(10535284771648367087)
XLA Ops:
  0.6 1.4 %fetch_theirs.1 = (bf16[4,32,2048]{2,1,0:T(8,128)(2,1)S(1)}, bf16[4,32,2048]{2,1,0:T(8,128)(2,1)S(1)}, bf16[2,32,2048]{2,1,0:T(8,128)(2,1)S(1)}) custom-call(bf16[128,2048]{1,0:T(8,128)(2,1)} %bitcast.15, bf16[128,2048]{1,0:T(8,128)(2,1)} %bitcast.17, bf16[128,2048]{1,0:T(8,128)(2,1)} %bitcast.19, bf16[128,2048]{1,0:T(8,128)(2,1)} %bitcast.21), custom_call_target="tpu_custom_call" | custom-call | flops 1 | bytes 1 | tf_op jit(solution)/shard_map/fetch_theirs/pallas_call | solution.py:599
  2.0 0.5 %collective-permute-start = (bf16[4,32,2048]{2,1,0:T(8,128)(2,1)S(1)}, bf16[4,32,2048]{2,1,0:T(8,128)(2,1)S(1)}, u32[]{:S(2)}, u32[]{:S(2)}) collective-permute-start(bf16[4,32,2048]{2,1,0:T(8,128)(2,1)S(1)} %get-tuple-element.37), channel_id=1, source_target_pairs={{0,8},{8,0},{16,24},{24,16},{1,9},{9,1},{17,25},{25,17},{2,10},{10... | collective-permute-start | bytes 1572872 | tf_op jit(solution)/shard_map/ppermute | solution.py:593
  2.5 0.1 collective-permute-start.1
  2.6 2.6 %collective-permute-start.3 = (bf16[2,32,2048]{2,1,0:T(8,128)(2,1)S(1)}, bf16[2,32,2048]{2,1,0:T(8,128)(2,1)S(1)}, u32[]{:S(2)}, u32[]{:S(2)}) collective-permute-start(bf16[2,32,2048]{2,1,0:T(8,128)(2,1)S(1)} %get-tuple-element.35.after), channel_id=1, source_target_pairs={{0,24},{8,16},{16,8},{24,0},{1,25},{9,17},{17,9},{25,1},{2,26},{10... | collective-permute-start | bytes 786440 | tf_op jit(solution)/shard_map/ppermute | solution.py:593
  5.3 0.0 copy-start
  5.3 1.4 %fetch_mine.1 = (bf16[4,32,2048]{2,1,0:T(8,128)(2,1)S(1)}, bf16[4,32,2048]{2,1,0:T(8,128)(2,1)S(1)}) custom-call(bf16[128,2048]{1,0:T(8,128)(2,1)} %bitcast.16, bf16[128,2048]{1,0:T(8,128)(2,1)} %bitcast.18, bf16[128,2048]{1,0:T(8,128)(2,1)} %bitcast.20, bf16[128,2048]{1,0:T(8,128)(2,1)} %bitcast.22, bf16[2,32,2048]{2,1,0:T(8,128)(2,1)S(1)} %get-tuple-element.35.after), custom_call_target="tpu_custom_call" | custom-call | flops 1 | bytes 1 | tf_op jit(solution)/shard_map/fetch_mine/pallas_call | solution.py:599
  6.6 0.0 copy-done
  6.6 0.0 collective-permute-done.refs_3_.near
  6.7 0.0 collective-permute-done.1.refs_2_.near
  6.7 2.3 %local_scores.1 = (f32[32,128]{1,0:T(8,128)S(1)}, f32[32,128]{1,0:T(8,128)S(1)}, f32[8,128]{1,0:T(8,128)S(1)}, bf16[2,32,2048]{2,1,0:T(8,128)(2,1)}, bf16[32,230...) custom-call(f32[8,128]{1,0:T(8,128)S(1)} %pad.4.table, ...), custom_call_target="tpu_custom_call" | custom-call | flops 1 | bytes 1 | tf_op jit(solution)/shard_map/local_scores/pallas_call | solution.py:599
  9.0 1.0 %collective-permute-start.4 = (bf16[32,2304]{1,0:T(8,128)(2,1)S(1)}, bf16[32,2304]{1,0:T(8,128)(2,1)S(1)}, u32[]{:S(2)}, u32[]{:S(2)}) collective-permute-start(bf16[32,2304]{1,0:T(8,128)(2,1)S(1)} %get-tuple-element.44), channel_id=1, source_target_pairs={{0,16},{8,24},{16,0},{24,8},{1,17},{9,25},{17,1},{25,9},{2,18},{10... | collective-permute-start | bytes 442376 | tf_op jit(solution)/shard_map/ppermute | solution.py:593
  10.0 1.0 %collective-permute-start.5 = (bf16[32,2304]{1,0:T(8,128)(2,1)S(1)}, bf16[32,2304]{1,0:T(8,128)(2,1)S(1)}, u32[]{:S(2)}, u32[]{:S(2)}) collective-permute-start(bf16[32,2304]{1,0:T(8,128)(2,1)S(1)} %get-tuple-element.45), channel_id=1, source_target_pairs={{0,16},{8,24},{16,0},{24,8},{1,17},{9,25},{17,1},{25,9},{2,18},{10... | collective-permute-start | bytes 442376 | tf_op jit(solution)/shard_map/ppermute | solution.py:593
  11.0 1.0 %collective-permute-start.2 = (bf16[2,32,2048]{2,1,0:T(8,128)(2,1)}, bf16[2,32,2048]{2,1,0:T(8,128)(2,1)S(1)}, u32[]{:S(2)}, u32[]{:S(2)}) collective-permute-start(bf16[2,32,2048]{2,1,0:T(8,128)(2,1)} %get-tuple-element.40), channel_id=1, source_target_pairs={{0,16},{8,24},{16,0},{24,8},{1,17},{9,25},{17,1},{25,9},{2,18},{10... | collective-permute-start | bytes 786440 | tf_op jit(solution)/shard_map/ppermute | solution.py:593
  12.1 0.2 collective-permute-start.6
  12.3 0.0 collective-permute-done.3.refs_0_.refs_2_
  12.3 0.5 %first_dots.1.known = f32[32,128]{1,0:T(8,128)S(1)} custom-call(bf16[4,32,2048]{2,1,0:T(8,128)(2,1)S(1)} %get-tuple-element.38.refs_0_.mine, bf16[4,32,2048]{2,1,0:T(8,128)(2,1)S(1)} %collective-permute-done.1.refs_2_.near, bf16[2,32,2048]{2,1,0:T(8,128)(2,1)S(1)} %collective-permute-done.3.refs_0_.refs_2_), custom_call_target="tpu_custom_call" | custom-call | flops 1 | bytes 1 | tf_op jit(solution)/shard_map/first_dots/pallas_call | solution.py:599
  12.8 2.9 %collective-permute-done.4.refs_0_ = bf16[32,2304]{1,0:T(8,128)(2,1)S(1)} collective-permute-done((bf16[32,2304]{1,0:T(8,128)(2,1)S(1)}, bf16[32,2304]{1,0:T(8,128)(2,1)S(1)}, u32[]{:S(2)}, u32[]{:S(2)}) %collective-permute-start.4) | collective-permute-done | bytes 147488 | tf_op jit(solution)/shard_map/ppermute | solution.py:593
  15.7 3.2 %collective-permute-done.5.refs_1_ = bf16[32,2304]{1,0:T(8,128)(2,1)S(1)} collective-permute-done((bf16[32,2304]{1,0:T(8,128)(2,1)S(1)}, bf16[32,2304]{1,0:T(8,128)(2,1)S(1)}, u32[]{:S(2)}, u32[]{:S(2)}) %collective-permute-start.5) | collective-permute-done | bytes 147488 | tf_op jit(solution)/shard_map/ppermute | solution.py:593
  18.8 1.3 %scores.1 = (bf16[14,32,128]{2,1,0:T(8,128)(2,1)S(1)}, f32[32,8,128]{2,1,0:T(8,128)}, f32[32,128]{1,0:T(8,128)S(1)}) custom-call(f32[32,128]{1,0:T(8,128)S(1)} %first_dots.1.known, f32[8,128]{1,0:T(8,128)S(1)} %pad.4.table, f32[32,128]{1,0:T(8,128)S(1)} %get-tuple-element.42.small, f32[8,128]{1,0:T(8,128)S(1)} %get-tuple-element.43.bias, ...), custom_call_target="tpu_custom_call" | custom-call | flops 1 | bytes 1 | tf_op jit(solution)/shard_map/scores/pallas_call | solution.py:599
  20.1 6.2 %all-to-all-start = ((f32[32,8,128]{2,1,0:T(8,128)}), f32[32,8,128]{2,1,0:T(8,128)S(1)}, u32[]{:S(2)}, u32[]{:S(2)}) async-start(f32[32,8,128]{2,1,0:T(8,128)} %get-tuple-element.51), calls=%async_computation | async-start | bytes 262144 | tf_op jit(solution)/shard_map/all_to_all | solution.py:661
  26.3 1.6 %gradients.1 = (bf16[3,16,2048]{2,1,0:T(8,128)(2,1)S(1)}, bf16[3,16,2048]{2,1,0:T(8,128)(2,1)S(1)}, bf16[128,2048]{1,0:T(8,128)(2,1)}, bf16[128,2048]{1,0:T(8,128)(2,1)}, bf16[128,2048]{1,0:T(8,128)(2,1)}) custom-call(bf16[14,32,128]{2,1,0:T(8,128)(2,1)S(1)} %get-tuple-element.52.items_ref, bf16[4,32,2048]{2,1,0:T(8,128)(2,1)S(1)} %get-tuple-element.38.refs_0_.mine, ...), custom_call_target="tpu_custom_call" | custom-call | flops 1 | bytes 1 | tf_op jit(solution)/shard_map/gradients/pallas_call | solution.py:599
  28.0 0.3 collective-permute-start.10
  28.3 0.3 collective-permute-start.11
  28.6 0.0 collective-permute-done.2.refs_0_
  28.6 0.5 %last_dots.1.known = f32[32,128]{1,0:T(8,128)S(1)} custom-call(bf16[4,32,2048]{2,1,0:T(8,128)(2,1)S(1)} %get-tuple-element.36.refs_1_.mine, bf16[4,32,2048]{2,1,0:T(8,128)(2,1)S(1)} %collective-permute-done.refs_3_.near, bf16[2,32,2048]{2,1,0:T(8,128)(2,1)S(1)} %collective-permute-done.2.refs_0_), custom_call_target="tpu_custom_call" | custom-call | flops 1 | bytes 1 | tf_op jit(solution)/shard_map/last_dots/pallas_call | solution.py:599
  29.1 0.9 %collective-permute-done.6.refs_1_ = bf16[2,32,2048]{2,1,0:T(8,128)(2,1)S(1)} collective-permute-done((bf16[2,32,2048]{2,1,0:T(8,128)(2,1)}, bf16[2,32,2048]{2,1,0:T(8,128)(2,1)S(1)}, u32[]{:S(2)}, u32[]{:S(2)}) %collective-permute-start.6) | collective-permute-done | bytes 262176 | tf_op jit(solution)/shard_map/ppermute | solution.py:593
  30.0 1.5 %scores_and_gradients.1 = (bf16[3,32,2048]{2,1,0:T(8,128)(2,1)S(1)}, bf16[32,2048]{1,0:T(8,128)(2,1)S(1)}, bf16[32,2048]{1,0:T(8,128)(2,1)S(1)}, bf16[32,2048]{1,0:T(8,128)(2,1)S(1)}) custom-call(f32[32,128]{1,0:T(8,128)S(1)} %last_dots.1.known, f32[8,128]{1,0:T(8,128)S(1)} %pad.4.table, f32[32,128]{1,0:T(8,128)S(1)} %get-tuple-element.41.small, ...), custom_call_target="tpu_custom_call" | custom-call | flops 1 | bytes 1 | tf_op jit(solution)/shard_map/scores_and_gradients/pallas_call | solution.py:599
  31.5 0.1 collective-permute-start.7
  31.6 0.5 %collective-permute-start.8 = (bf16[32,2048]{1,0:T(8,128)(2,1)S(1)}, bf16[32,2048]{1,0:T(8,128)(2,1)S(1)}, u32[]{:S(2)}, u32[]{:S(2)}) collective-permute-start(bf16[32,2048]{1,0:T(8,128)(2,1)S(1)} %get-tuple-element.49), channel_id=1, source_target_pairs={{0,8},{8,0},{16,24},{24,16},{1,9},{9,1},{17,25},{25,17},{2,10},{10... | collective-permute-start | bytes 393224 | tf_op jit(solution)/shard_map/ppermute | solution.py:593
  32.1 0.1 collective-permute-start.9
  32.1 0.0 collective-permute-done.10.refs_0_
  32.1 0.0 collective-permute-done.11.refs_1_
  32.2 1.0 %early_outputs.1 = (bf16[128,2048]{1,0:T(8,128)(2,1)}, bf16[128,2048]{1,0:T(8,128)(2,1)}, bf16[128,2048]{1,0:T(8,128)(2,1)}) custom-call(bf16[3,16,2048]{2,1,0:T(8,128)(2,1)S(1)} %collective-permute-done.10.refs_0_, bf16[3,16,2048]{2,1,0:T(8,128)(2,1)S(1)} %collective-permute-done.11.refs_1_, ...), custom_call_target="tpu_custom_call", output_to_operand_aliasing={{0}: (3, {}), {1}: (4, {}), {2}: (5, {})} | custom-call | flops 1 | bytes 1 | tf_op jit(solution)/shard_map/early_outputs/pallas_call | solution.py:599
  33.1 0.0 collective-permute-done.7.refs_0_
  33.1 0.0 collective-permute-done.8.refs_1_
  33.2 0.3 collective-permute-done.9.refs_2_
  33.4 0.7 %all-to-all-done.refs_3_ = f32[32,8,128]{2,1,0:T(8,128)S(1)} async-done(((f32[32,8,128]{2,1,0:T(8,128)}), f32[32,8,128]{2,1,0:T(8,128)S(1)}, u32[]{:S(2)}, u32[]{:S(2)}) %all-to-all-start) | async-done | bytes 131104 | tf_op jit(solution)/shard_map/all_to_all | solution.py:661
  34.1 0.9 %outputs.1 = (bf16[128,2048]{1,0:T(8,128)(2,1)}, bf16[128,2048]{1,0:T(8,128)(2,1)}, bf16[128,2048]{1,0:T(8,128)(2,1)}, f32[4,16]{1,0:T(4,128)}) custom-call(bf16[32,2048]{1,0:T(8,128)(2,1)S(1)} %collective-permute-done.7.refs_0_, bf16[32,2048]{1,0:T(8,128)(2,1)S(1)} %collective-permute-done.8.refs_1_, ...), custom_call_target="tpu_custom_call", output_to_operand_aliasing={{0}: (4, {}), {1}: (5, {}), {2}: (6, {})} | custom-call | flops 1 | bytes 1 | tf_op jit(solution)/shard_map/outputs/pallas_call | solution.py:599
  (1 shorter events, 0.0 us)
Async XLA Ops:
  2.0 4.6 %collective-permute-start = (bf16[4,32,2048]{2,1,0:T(8,128)(2,1)S(1)}, bf16[4,32,2048]{2,1,0:T(8,128)(2,1)S(1)}, u32[]{:S(2)}, u32[]{:S(2)}) collective-permute-start(bf16[4,32,2048]{2,1,0:T(8,128)(2,1)S(1)} %get-tuple-element.37), channel_id=1, source_target_pairs={{0,8},{8,0},{16,24},{24,16},{1,9},{9,1},{17,25},{25,17},{2,10},{10... | collective-permute-start | bytes 1572872 | tf_op jit(solution)/shard_map/ppermute | solution.py:593
  2.5 4.1 %collective-permute-start.1 = (bf16[4,32,2048]{2,1,0:T(8,128)(2,1)S(1)}, bf16[4,32,2048]{2,1,0:T(8,128)(2,1)S(1)}, u32[]{:S(2)}, u32[]{:S(2)}) collective-permute-start(bf16[4,32,2048]{2,1,0:T(8,128)(2,1)S(1)} %get-tuple-element.39.refs_4_), channel_id=1, source_target_pairs={{0,8},{8,0},{16,24},{24,16},{1,9},{9,1},{17,25},{25,17},{2,10},{10... | collective-permute-start | bytes 1572872 | tf_op jit(solution)/shard_map/ppermute | solution.py:593
  2.6 9.6 %collective-permute-start.3 = (bf16[2,32,2048]{2,1,0:T(8,128)(2,1)S(1)}, bf16[2,32,2048]{2,1,0:T(8,128)(2,1)S(1)}, u32[]{:S(2)}, u32[]{:S(2)}) collective-permute-start(bf16[2,32,2048]{2,1,0:T(8,128)(2,1)S(1)} %get-tuple-element.35.after), channel_id=1, source_target_pairs={{0,24},{8,16},{16,8},{24,0},{1,25},{9,17},{17,9},{25,1},{2,26},{10... | collective-permute-start | bytes 786440 | tf_op jit(solution)/shard_map/ppermute | solution.py:593
  5.3 1.4 %copy-start = (f32[16,4]{0,1:T(4,128)S(1)}, f32[16,4]{0,1:T(4,128)}, u32[]{:S(2)}) copy-start(f32[16,4]{0,1:T(4,128)} %param.9) | copy-start | bytes 772
  9.0 6.7 %collective-permute-start.4 = (bf16[32,2304]{1,0:T(8,128)(2,1)S(1)}, bf16[32,2304]{1,0:T(8,128)(2,1)S(1)}, u32[]{:S(2)}, u32[]{:S(2)}) collective-permute-start(bf16[32,2304]{1,0:T(8,128)(2,1)S(1)} %get-tuple-element.44), channel_id=1, source_target_pairs={{0,16},{8,24},{16,0},{24,8},{1,17},{9,25},{17,1},{25,9},{2,18},{10... | collective-permute-start | bytes 442376 | tf_op jit(solution)/shard_map/ppermute | solution.py:593
  10.0 8.8 %collective-permute-start.5 = (bf16[32,2304]{1,0:T(8,128)(2,1)S(1)}, bf16[32,2304]{1,0:T(8,128)(2,1)S(1)}, u32[]{:S(2)}, u32[]{:S(2)}) collective-permute-start(bf16[32,2304]{1,0:T(8,128)(2,1)S(1)} %get-tuple-element.45), channel_id=1, source_target_pairs={{0,16},{8,24},{16,0},{24,8},{1,17},{9,25},{17,1},{25,9},{2,18},{10... | collective-permute-start | bytes 442376 | tf_op jit(solution)/shard_map/ppermute | solution.py:593
  11.0 17.5 %collective-permute-start.2 = (bf16[2,32,2048]{2,1,0:T(8,128)(2,1)}, bf16[2,32,2048]{2,1,0:T(8,128)(2,1)S(1)}, u32[]{:S(2)}, u32[]{:S(2)}) collective-permute-start(bf16[2,32,2048]{2,1,0:T(8,128)(2,1)} %get-tuple-element.40), channel_id=1, source_target_pairs={{0,16},{8,24},{16,0},{24,8},{1,17},{9,25},{17,1},{25,9},{2,18},{10... | collective-permute-start | bytes 786440 | tf_op jit(solution)/shard_map/ppermute | solution.py:593
  12.1 17.9 %collective-permute-start.6 = (bf16[2,32,2048]{2,1,0:T(8,128)(2,1)}, bf16[2,32,2048]{2,1,0:T(8,128)(2,1)S(1)}, u32[]{:S(2)}, u32[]{:S(2)}) collective-permute-start(bf16[2,32,2048]{2,1,0:T(8,128)(2,1)} %get-tuple-element.47), channel_id=1, source_target_pairs={{0,24},{8,16},{16,8},{24,0},{1,25},{9,17},{17,9},{25,1},{2,26},{10... | collective-permute-start | bytes 786440 | tf_op jit(solution)/shard_map/ppermute | solution.py:593
  20.1 14.0 %all-to-all-start = ((f32[32,8,128]{2,1,0:T(8,128)}), f32[32,8,128]{2,1,0:T(8,128)S(1)}, u32[]{:S(2)}, u32[]{:S(2)}) async-start(f32[32,8,128]{2,1,0:T(8,128)} %get-tuple-element.51), calls=%async_computation | async-start | bytes 262144 | tf_op jit(solution)/shard_map/all_to_all | solution.py:661
  28.0 4.2 %collective-permute-start.10 = (bf16[3,16,2048]{2,1,0:T(8,128)(2,1)S(1)}, bf16[3,16,2048]{2,1,0:T(8,128)(2,1)S(1)}, u32[]{:S(2)}, u32[]{:S(2)}) collective-permute-start(bf16[3,16,2048]{2,1,0:T(8,128)(2,1)S(1)} %get-tuple-element.53), channel_id=1, source_target_pairs={{0,8},{8,0},{16,24},{24,16},{1,9},{9,1},{17,25},{25,17},{2,10},{10... | collective-permute-start | bytes 589832 | tf_op jit(solution)/shard_map/ppermute | solution.py:593
  28.3 3.9 %collective-permute-start.11 = (bf16[3,16,2048]{2,1,0:T(8,128)(2,1)S(1)}, bf16[3,16,2048]{2,1,0:T(8,128)(2,1)S(1)}, u32[]{:S(2)}, u32[]{:S(2)}) collective-permute-start(bf16[3,16,2048]{2,1,0:T(8,128)(2,1)S(1)} %get-tuple-element.54), channel_id=1, source_target_pairs={{0,8},{8,0},{16,24},{24,16},{1,9},{9,1},{17,25},{25,17},{2,10},{10... | collective-permute-start | bytes 589832 | tf_op jit(solution)/shard_map/ppermute | solution.py:593
  31.5 1.7 %collective-permute-start.7 = (bf16[32,2048]{1,0:T(8,128)(2,1)S(1)}, bf16[32,2048]{1,0:T(8,128)(2,1)S(1)}, u32[]{:S(2)}, u32[]{:S(2)}) collective-permute-start(bf16[32,2048]{1,0:T(8,128)(2,1)S(1)} %get-tuple-element.48), channel_id=1, source_target_pairs={{0,8},{8,0},{16,24},{24,16},{1,9},{9,1},{17,25},{25,17},{2,10},{10... | collective-permute-start | bytes 393224 | tf_op jit(solution)/shard_map/ppermute | solution.py:593
  31.6 1.6 %collective-permute-start.8 = (bf16[32,2048]{1,0:T(8,128)(2,1)S(1)}, bf16[32,2048]{1,0:T(8,128)(2,1)S(1)}, u32[]{:S(2)}, u32[]{:S(2)}) collective-permute-start(bf16[32,2048]{1,0:T(8,128)(2,1)S(1)} %get-tuple-element.49), channel_id=1, source_target_pairs={{0,8},{8,0},{16,24},{24,16},{1,9},{9,1},{17,25},{25,17},{2,10},{10... | collective-permute-start | bytes 393224 | tf_op jit(solution)/shard_map/ppermute | solution.py:593
  32.1 1.3 %collective-permute-start.9 = (bf16[32,2048]{1,0:T(8,128)(2,1)S(1)}, bf16[32,2048]{1,0:T(8,128)(2,1)S(1)}, u32[]{:S(2)}, u32[]{:S(2)}) collective-permute-start(bf16[32,2048]{1,0:T(8,128)(2,1)S(1)} %get-tuple-element.50), channel_id=1, source_target_pairs={{0,8},{8,0},{16,24},{24,16},{1,9},{9,1},{17,25},{25,17},{2,10},{10... | collective-permute-start | bytes 393224 | tf_op jit(solution)/shard_map/ppermute | solution.py:593

commit v7 on v6

--- a/solution.py
+++ b/solution.py
@@ -560,19 +560,23 @@
         copy.wait()
 
 
-def output_kernel(*refs):
-    back, shares, outs, out_bias, total, sems = refs[:3], refs[3], refs[7:10], *refs[10:]
+def late_output_kernel(*refs):
+    back, outs, sems = refs[:3], refs[6:9], refs[9]
     copies = output_copies(1 - my_place()[0], back, outs, 1, sems, 0)
     for copy in copies:
         copy.start()
+    for copy in copies:
+        copy.wait()
+
+
+def bias_kernel(shares, after, out_bias, total, sem):
     parts = [shares[j] for j in range(shares.shape[0])]
     while len(parts) > 1:
         parts = [a + b for a, b in zip(parts[::2], parts[1::2])]
     total[...] = parts[0][: total.shape[0], : total.shape[1]]
-    copies.append(pltpu.make_async_copy(total, out_bias, sems.at[len(copies)]))
-    copies[-1].start()
-    for copy in copies:
-        copy.wait()
+    copy = pltpu.make_async_copy(total, out_bias, sem)
+    copy.start()
+    copy.wait()
 
 
 def by_chips(query_vectors, key_vectors, value_vectors, grad_output, time_bias, sizes):
@@ -694,15 +698,24 @@
         hbm_out=range(3),
         aliases={3 + j: j for j in range(3)},
     )
-    *grads, bias = call(
-        output_kernel,
-        "outputs",
-        [whole] * 3 + [shape(frames, heads, dtype=wide)],
-        *back, shares, *in_hbm(grads),
-        scratch=[pltpu.VMEM((frames, heads), wide), output_sems],
-        hbm=range(4, 7),
-        hbm_out=range(4),
-        aliases={4 + j: j for j in range(3)},
+    grads = call(
+        late_output_kernel,
+        "late_outputs",
+        [whole] * 3,
+        *back, *in_hbm(grads),
+        scratch=[output_sems],
+        hbm=range(3, 6),
+        hbm_out=range(3),
+        aliases={3 + j: j for j in range(3)},
+    )
+    (bias,) = call(
+        bias_kernel,
+        "bias",
+        [shape(frames, heads, dtype=wide)],
+        shares, *in_hbm(grads[:1]),
+        scratch=[pltpu.VMEM((frames, heads), wide), pltpu.SemaphoreType.DMA],
+        hbm=(1,),
+        hbm_out=(0,),
     )
     return (*[x.reshape(query_vectors.shape) for x in grads], bias.T)
 

time: 35.2 us -> 35.3 us (level)
  waiting for transfers between devices: 7.86 us -> 7.21 us
  Pallas kernels: 12.4 us -> 13 us
    all_to_all x1, waiting for transfers between devices: 0.65 us -> 0.01 us  [by_chips(): lax.all_to_all(shares, tuple((axis for axis, _ in sizes)), 0, 0, tiled=True)]
    pallas_call x10 -> x11, Pallas kernels: 12.4 us -> 13 us  [call(): pl.pallas_call(kernel, in_specs=[any_spec if j in hbm else vmem_spec for...]
  transfers between devices with their start and end apart: 13 -> 13, of which waited for: 5 -> 4; matrix products, arithmetic and copies ran while one was open for 0% -> 0% of each run, Pallas kernels for 29% -> 31%
where the time goes in v7:
time: 35.3 us; the launch traced here: 34.9 us
  starting transfers between devices  13.9 us (39%)
  Pallas kernels  13 us (37%)
  waiting for transfers between devices  7.21 us (20%)
  between operations  0.76 us (2%)
    pallas_call x11, Pallas kernels, call(): pl.pallas_call(kernel, in_specs=[any_spec if j in hbm else vmem_spec for...  13 us
    ppermute x12, starting transfers between devices, swap(): return lax.ppermute(x, 'tm', [(i, i ^ bits) for i in range(4)])  7.7 us
    ppermute x12, waiting for transfers between devices, swap(): return lax.ppermute(x, 'tm', [(i, i ^ bits) for i in range(4)])  7.21 us
    all_to_all x1, starting transfers between devices, by_chips(): lax.all_to_all(shares, tuple((axis for axis, _ in sizes)), 0, 0, tiled=True)  6.25 us
  transfers between devices with their start and end apart: 13, of which 4 were waited for; matrix products, arithmetic and copies ran while one was open for 0% of the time, Pallas kernels for 31%

profile of v7, /device:TPU:0, one launch (start us, length us, event | category | flops | bytes accessed | tf_op | source)
XLA Modules:
  0.0 34.9 jit_solution(13947774359450966688)
XLA Ops:
  0.6 1.4 %fetch_theirs.1 = (bf16[4,32,2048]{2,1,0:T(8,128)(2,1)S(1)}, bf16[4,32,2048]{2,1,0:T(8,128)(2,1)S(1)}, bf16[2,32,2048]{2,1,0:T(8,128)(2,1)S(1)}) custom-call(bf16[128,2048]{1,0:T(8,128)(2,1)} %bitcast.16, bf16[128,2048]{1,0:T(8,128)(2,1)} %bitcast.18, bf16[128,2048]{1,0:T(8,128)(2,1)} %bitcast.20, bf16[128,2048]{1,0:T(8,128)(2,1)} %bitcast.22), custom_call_target="tpu_custom_call" | custom-call | flops 1 | bytes 1 | tf_op jit(solution)/shard_map/fetch_theirs/pallas_call | solution.py:603
  2.0 0.5 %collective-permute-start = (bf16[4,32,2048]{2,1,0:T(8,128)(2,1)S(1)}, bf16[4,32,2048]{2,1,0:T(8,128)(2,1)S(1)}, u32[]{:S(2)}, u32[]{:S(2)}) collective-permute-start(bf16[4,32,2048]{2,1,0:T(8,128)(2,1)S(1)} %get-tuple-element.36), channel_id=1, source_target_pairs={{0,8},{8,0},{16,24},{24,16},{1,9},{9,1},{17,25},{25,17},{2,10},{10... | collective-permute-start | bytes 1572872 | tf_op jit(solution)/shard_map/ppermute | solution.py:597
  2.5 0.1 collective-permute-start.1
  2.6 2.6 %collective-permute-start.3 = (bf16[2,32,2048]{2,1,0:T(8,128)(2,1)S(1)}, bf16[2,32,2048]{2,1,0:T(8,128)(2,1)S(1)}, u32[]{:S(2)}, u32[]{:S(2)}) collective-permute-start(bf16[2,32,2048]{2,1,0:T(8,128)(2,1)S(1)} %get-tuple-element.34.after), channel_id=1, source_target_pairs={{0,24},{8,16},{16,8},{24,0},{1,25},{9,17},{17,9},{25,1},{2,26},{10... | collective-permute-start | bytes 786440 | tf_op jit(solution)/shard_map/ppermute | solution.py:597
  5.3 0.0 copy-start
  5.3 1.4 %fetch_mine.1 = (bf16[4,32,2048]{2,1,0:T(8,128)(2,1)S(1)}, bf16[4,32,2048]{2,1,0:T(8,128)(2,1)S(1)}) custom-call(bf16[128,2048]{1,0:T(8,128)(2,1)} %bitcast.17, bf16[128,2048]{1,0:T(8,128)(2,1)} %bitcast.19, bf16[128,2048]{1,0:T(8,128)(2,1)} %bitcast.21, bf16[128,2048]{1,0:T(8,128)(2,1)} %bitcast.23, bf16[2,32,2048]{2,1,0:T(8,128)(2,1)S(1)} %get-tuple-element.34.after), custom_call_target="tpu_custom_call" | custom-call | flops 1 | bytes 1 | tf_op jit(solution)/shard_map/fetch_mine/pallas_call | solution.py:603
  6.6 0.0 copy-done
  6.6 0.0 collective-permute-done.refs_3_.near
  6.7 0.0 collective-permute-done.1.refs_2_.near
  6.7 2.3 %local_scores.1 = (f32[32,128]{1,0:T(8,128)S(1)}, f32[32,128]{1,0:T(8,128)S(1)}, f32[8,128]{1,0:T(8,128)S(1)}, bf16[2,32,2048]{2,1,0:T(8,128)(2,1)}, bf16[32,230...) custom-call(f32[8,128]{1,0:T(8,128)S(1)} %pad.4.table, ...), custom_call_target="tpu_custom_call" | custom-call | flops 1 | bytes 1 | tf_op jit(solution)/shard_map/local_scores/pallas_call | solution.py:603
  9.0 1.0 %collective-permute-start.4 = (bf16[32,2304]{1,0:T(8,128)(2,1)S(1)}, bf16[32,2304]{1,0:T(8,128)(2,1)S(1)}, u32[]{:S(2)}, u32[]{:S(2)}) collective-permute-start(bf16[32,2304]{1,0:T(8,128)(2,1)S(1)} %get-tuple-element.43), channel_id=1, source_target_pairs={{0,16},{8,24},{16,0},{24,8},{1,17},{9,25},{17,1},{25,9},{2,18},{10... | collective-permute-start | bytes 442376 | tf_op jit(solution)/shard_map/ppermute | solution.py:597
  10.0 1.0 %collective-permute-start.5 = (bf16[32,2304]{1,0:T(8,128)(2,1)S(1)}, bf16[32,2304]{1,0:T(8,128)(2,1)S(1)}, u32[]{:S(2)}, u32[]{:S(2)}) collective-permute-start(bf16[32,2304]{1,0:T(8,128)(2,1)S(1)} %get-tuple-element.44), channel_id=1, source_target_pairs={{0,16},{8,24},{16,0},{24,8},{1,17},{9,25},{17,1},{25,9},{2,18},{10... | collective-permute-start | bytes 442376 | tf_op jit(solution)/shard_map/ppermute | solution.py:597
  11.0 1.0 %collective-permute-start.2 = (bf16[2,32,2048]{2,1,0:T(8,128)(2,1)}, bf16[2,32,2048]{2,1,0:T(8,128)(2,1)S(1)}, u32[]{:S(2)}, u32[]{:S(2)}) collective-permute-start(bf16[2,32,2048]{2,1,0:T(8,128)(2,1)} %get-tuple-element.39), channel_id=1, source_target_pairs={{0,16},{8,24},{16,0},{24,8},{1,17},{9,25},{17,1},{25,9},{2,18},{10... | collective-permute-start | bytes 786440 | tf_op jit(solution)/shard_map/ppermute | solution.py:597
  12.1 0.2 collective-permute-start.6
  12.3 0.0 collective-permute-done.3.refs_0_.refs_2_
  12.3 0.5 %first_dots.1.known = f32[32,128]{1,0:T(8,128)S(1)} custom-call(bf16[4,32,2048]{2,1,0:T(8,128)(2,1)S(1)} %get-tuple-element.37.refs_0_.mine, bf16[4,32,2048]{2,1,0:T(8,128)(2,1)S(1)} %collective-permute-done.1.refs_2_.near, bf16[2,32,2048]{2,1,0:T(8,128)(2,1)S(1)} %collective-permute-done.3.refs_0_.refs_2_), custom_call_target="tpu_custom_call" | custom-call | flops 1 | bytes 1 | tf_op jit(solution)/shard_map/first_dots/pallas_call | solution.py:603
  12.8 2.9 %collective-permute-done.4.refs_0_ = bf16[32,2304]{1,0:T(8,128)(2,1)S(1)} collective-permute-done((bf16[32,2304]{1,0:T(8,128)(2,1)S(1)}, bf16[32,2304]{1,0:T(8,128)(2,1)S(1)}, u32[]{:S(2)}, u32[]{:S(2)}) %collective-permute-start.4) | collective-permute-done | bytes 147488 | tf_op jit(solution)/shard_map/ppermute | solution.py:597
  15.7 3.2 %collective-permute-done.5.refs_1_ = bf16[32,2304]{1,0:T(8,128)(2,1)S(1)} collective-permute-done((bf16[32,2304]{1,0:T(8,128)(2,1)S(1)}, bf16[32,2304]{1,0:T(8,128)(2,1)S(1)}, u32[]{:S(2)}, u32[]{:S(2)}) %collective-permute-start.5) | collective-permute-done | bytes 147488 | tf_op jit(solution)/shard_map/ppermute | solution.py:597
  18.8 1.3 %scores.1 = (bf16[14,32,128]{2,1,0:T(8,128)(2,1)S(1)}, f32[32,8,128]{2,1,0:T(8,128)}, f32[32,128]{1,0:T(8,128)S(1)}) custom-call(f32[32,128]{1,0:T(8,128)S(1)} %first_dots.1.known, f32[8,128]{1,0:T(8,128)S(1)} %pad.4.table, f32[32,128]{1,0:T(8,128)S(1)} %get-tuple-element.41.small, f32[8,128]{1,0:T(8,128)S(1)} %get-tuple-element.42.bias, ...), custom_call_target="tpu_custom_call" | custom-call | flops 1 | bytes 1 | tf_op jit(solution)/shard_map/scores/pallas_call | solution.py:603
  20.1 6.2 %all-to-all-start = ((f32[32,8,128]{2,1,0:T(8,128)}), f32[32,8,128]{2,1,0:T(8,128)S(1)}, u32[]{:S(2)}, u32[]{:S(2)}) async-start(f32[32,8,128]{2,1,0:T(8,128)} %get-tuple-element.63), calls=%async_computation | async-start | bytes 262144 | tf_op jit(solution)/shard_map/all_to_all | solution.py:665
  26.3 1.6 %gradients.1 = (bf16[3,16,2048]{2,1,0:T(8,128)(2,1)S(1)}, bf16[3,16,2048]{2,1,0:T(8,128)(2,1)S(1)}, bf16[128,2048]{1,0:T(8,128)(2,1)}, bf16[128,2048]{1,0:T(8,128)(2,1)}, bf16[128,2048]{1,0:T(8,128)(2,1)}) custom-call(bf16[14,32,128]{2,1,0:T(8,128)(2,1)S(1)} %get-tuple-element.50.items_ref, bf16[4,32,2048]{2,1,0:T(8,128)(2,1)S(1)} %get-tuple-element.37.refs_0_.mine, ...), custom_call_target="tpu_custom_call" | custom-call | flops 1 | bytes 1 | tf_op jit(solution)/shard_map/gradients/pallas_call | solution.py:603
  28.0 0.3 collective-permute-start.10
  28.3 0.3 collective-permute-start.11
  28.6 0.0 collective-permute-done.2.refs_0_
  28.6 0.5 %last_dots.1.known = f32[32,128]{1,0:T(8,128)S(1)} custom-call(bf16[4,32,2048]{2,1,0:T(8,128)(2,1)S(1)} %get-tuple-element.35.refs_1_.mine, bf16[4,32,2048]{2,1,0:T(8,128)(2,1)S(1)} %collective-permute-done.refs_3_.near, bf16[2,32,2048]{2,1,0:T(8,128)(2,1)S(1)} %collective-permute-done.2.refs_0_), custom_call_target="tpu_custom_call" | custom-call | flops 1 | bytes 1 | tf_op jit(solution)/shard_map/last_dots/pallas_call | solution.py:603
  29.1 0.9 %collective-permute-done.6.refs_1_ = bf16[2,32,2048]{2,1,0:T(8,128)(2,1)S(1)} collective-permute-done((bf16[2,32,2048]{2,1,0:T(8,128)(2,1)}, bf16[2,32,2048]{2,1,0:T(8,128)(2,1)S(1)}, u32[]{:S(2)}, u32[]{:S(2)}) %collective-permute-start.6) | collective-permute-done | bytes 262176 | tf_op jit(solution)/shard_map/ppermute | solution.py:597
  30.0 1.5 %scores_and_gradients.1 = (bf16[3,32,2048]{2,1,0:T(8,128)(2,1)S(1)}, bf16[32,2048]{1,0:T(8,128)(2,1)S(1)}, bf16[32,2048]{1,0:T(8,128)(2,1)S(1)}, bf16[32,2048]{1,0:T(8,128)(2,1)S(1)}) custom-call(f32[32,128]{1,0:T(8,128)S(1)} %last_dots.1.known, f32[8,128]{1,0:T(8,128)S(1)} %pad.4.table, f32[32,128]{1,0:T(8,128)S(1)} %get-tuple-element.40.small, ...), custom_call_target="tpu_custom_call" | custom-call | flops 1 | bytes 1 | tf_op jit(solution)/shard_map/scores_and_gradients/pallas_call | solution.py:603
  31.5 0.1 collective-permute-start.7
  31.6 0.5 %collective-permute-start.8 = (bf16[32,2048]{1,0:T(8,128)(2,1)S(1)}, bf16[32,2048]{1,0:T(8,128)(2,1)S(1)}, u32[]{:S(2)}, u32[]{:S(2)}) collective-permute-start(bf16[32,2048]{1,0:T(8,128)(2,1)S(1)} %get-tuple-element.48), channel_id=1, source_target_pairs={{0,8},{8,0},{16,24},{24,16},{1,9},{9,1},{17,25},{25,17},{2,10},{10... | collective-permute-start | bytes 393224 | tf_op jit(solution)/shard_map/ppermute | solution.py:597
  32.1 0.1 collective-permute-start.9
  32.1 0.0 collective-permute-done.10.refs_0_
  32.1 0.0 collective-permute-done.11.refs_1_
  32.2 1.0 %early_outputs.1 = (bf16[128,2048]{1,0:T(8,128)(2,1)}, bf16[128,2048]{1,0:T(8,128)(2,1)}, bf16[128,2048]{1,0:T(8,128)(2,1)}) custom-call(bf16[3,16,2048]{2,1,0:T(8,128)(2,1)S(1)} %collective-permute-done.10.refs_0_, bf16[3,16,2048]{2,1,0:T(8,128)(2,1)S(1)} %collective-permute-done.11.refs_1_, ...), custom_call_target="tpu_custom_call", output_to_operand_aliasing={{0}: (3, {}), {1}: (4, {}), {2}: (5, {})} | custom-call | flops 1 | bytes 1 | tf_op jit(solution)/shard_map/early_outputs/pallas_call | solution.py:603
  33.1 0.0 collective-permute-done.7.refs_0_
  33.1 0.0 collective-permute-done.8.refs_1_
  33.2 0.3 collective-permute-done.9.refs_2_
  33.4 0.9 %late_outputs.1 = (bf16[128,2048]{1,0:T(8,128)(2,1)}, bf16[128,2048]{1,0:T(8,128)(2,1)}, bf16[128,2048]{1,0:T(8,128)(2,1)}) custom-call(bf16[32,2048]{1,0:T(8,128)(2,1)S(1)} %collective-permute-done.7.refs_0_, bf16[32,2048]{1,0:T(8,128)(2,1)S(1)} %collective-permute-done.8.refs_1_, ...), custom_call_target="tpu_custom_call", output_to_operand_aliasing={{0}: (3, {}), {1}: (4, {}), {2}: (5, {})} | custom-call | flops 1 | bytes 1 | tf_op jit(solution)/shard_map/late_outputs/pallas_call | solution.py:603
  34.3 0.0 all-to-all-done.shares
  34.3 0.6 %bias.1 = f32[4,16]{1,0:T(4,128)} custom-call(f32[32,8,128]{2,1,0:T(8,128)S(1)} %all-to-all-done.shares, bf16[128,2048]{1,0:T(8,128)(2,1)} %get-tuple-element.60.after), custom_call_target="tpu_custom_call" | custom-call | flops 1 | bytes 1 | tf_op jit(solution)/shard_map/bias/pallas_call | solution.py:603
  (1 shorter events, 0.0 us)
Async XLA Ops:
  2.0 4.6 %collective-permute-start = (bf16[4,32,2048]{2,1,0:T(8,128)(2,1)S(1)}, bf16[4,32,2048]{2,1,0:T(8,128)(2,1)S(1)}, u32[]{:S(2)}, u32[]{:S(2)}) collective-permute-start(bf16[4,32,2048]{2,1,0:T(8,128)(2,1)S(1)} %get-tuple-element.36), channel_id=1, source_target_pairs={{0,8},{8,0},{16,24},{24,16},{1,9},{9,1},{17,25},{25,17},{2,10},{10... | collective-permute-start | bytes 1572872 | tf_op jit(solution)/shard_map/ppermute | solution.py:597
  2.5 4.1 %collective-permute-start.1 = (bf16[4,32,2048]{2,1,0:T(8,128)(2,1)S(1)}, bf16[4,32,2048]{2,1,0:T(8,128)(2,1)S(1)}, u32[]{:S(2)}, u32[]{:S(2)}) collective-permute-start(bf16[4,32,2048]{2,1,0:T(8,128)(2,1)S(1)} %get-tuple-element.38.refs_4_), channel_id=1, source_target_pairs={{0,8},{8,0},{16,24},{24,16},{1,9},{9,1},{17,25},{25,17},{2,10},{10... | collective-permute-start | bytes 1572872 | tf_op jit(solution)/shard_map/ppermute | solution.py:597
  2.6 9.6 %collective-permute-start.3 = (bf16[2,32,2048]{2,1,0:T(8,128)(2,1)S(1)}, bf16[2,32,2048]{2,1,0:T(8,128)(2,1)S(1)}, u32[]{:S(2)}, u32[]{:S(2)}) collective-permute-start(bf16[2,32,2048]{2,1,0:T(8,128)(2,1)S(1)} %get-tuple-element.34.after), channel_id=1, source_target_pairs={{0,24},{8,16},{16,8},{24,0},{1,25},{9,17},{17,9},{25,1},{2,26},{10... | collective-permute-start | bytes 786440 | tf_op jit(solution)/shard_map/ppermute | solution.py:597
  5.3 1.4 %copy-start = (f32[16,4]{0,1:T(4,128)S(1)}, f32[16,4]{0,1:T(4,128)}, u32[]{:S(2)}) copy-start(f32[16,4]{0,1:T(4,128)} %param.9) | copy-start | bytes 772
  9.0 6.7 %collective-permute-start.4 = (bf16[32,2304]{1,0:T(8,128)(2,1)S(1)}, bf16[32,2304]{1,0:T(8,128)(2,1)S(1)}, u32[]{:S(2)}, u32[]{:S(2)}) collective-permute-start(bf16[32,2304]{1,0:T(8,128)(2,1)S(1)} %get-tuple-element.43), channel_id=1, source_target_pairs={{0,16},{8,24},{16,0},{24,8},{1,17},{9,25},{17,1},{25,9},{2,18},{10... | collective-permute-start | bytes 442376 | tf_op jit(solution)/shard_map/ppermute | solution.py:597
  10.0 8.8 %collective-permute-start.5 = (bf16[32,2304]{1,0:T(8,128)(2,1)S(1)}, bf16[32,2304]{1,0:T(8,128)(2,1)S(1)}, u32[]{:S(2)}, u32[]{:S(2)}) collective-permute-start(bf16[32,2304]{1,0:T(8,128)(2,1)S(1)} %get-tuple-element.44), channel_id=1, source_target_pairs={{0,16},{8,24},{16,0},{24,8},{1,17},{9,25},{17,1},{25,9},{2,18},{10... | collective-permute-start | bytes 442376 | tf_op jit(solution)/shard_map/ppermute | solution.py:597
  11.0 17.5 %collective-permute-start.2 = (bf16[2,32,2048]{2,1,0:T(8,128)(2,1)}, bf16[2,32,2048]{2,1,0:T(8,128)(2,1)S(1)}, u32[]{:S(2)}, u32[]{:S(2)}) collective-permute-start(bf16[2,32,2048]{2,1,0:T(8,128)(2,1)} %get-tuple-element.39), channel_id=1, source_target_pairs={{0,16},{8,24},{16,0},{24,8},{1,17},{9,25},{17,1},{25,9},{2,18},{10... | collective-permute-start | bytes 786440 | tf_op jit(solution)/shard_map/ppermute | solution.py:597
  12.1 17.9 %collective-permute-start.6 = (bf16[2,32,2048]{2,1,0:T(8,128)(2,1)}, bf16[2,32,2048]{2,1,0:T(8,128)(2,1)S(1)}, u32[]{:S(2)}, u32[]{:S(2)}) collective-permute-start(bf16[2,32,2048]{2,1,0:T(8,128)(2,1)} %get-tuple-element.46), channel_id=1, source_target_pairs={{0,24},{8,16},{16,8},{24,0},{1,25},{9,17},{17,9},{25,1},{2,26},{10... | collective-permute-start | bytes 786440 | tf_op jit(solution)/shard_map/ppermute | solution.py:597
  20.1 14.2 %all-to-all-start = ((f32[32,8,128]{2,1,0:T(8,128)}), f32[32,8,128]{2,1,0:T(8,128)S(1)}, u32[]{:S(2)}, u32[]{:S(2)}) async-start(f32[32,8,128]{2,1,0:T(8,128)} %get-tuple-element.63), calls=%async_computation | async-start | bytes 262144 | tf_op jit(solution)/shard_map/all_to_all | solution.py:665
  28.0 4.2 %collective-permute-start.10 = (bf16[3,16,2048]{2,1,0:T(8,128)(2,1)S(1)}, bf16[3,16,2048]{2,1,0:T(8,128)(2,1)S(1)}, u32[]{:S(2)}, u32[]{:S(2)}) collective-permute-start(bf16[3,16,2048]{2,1,0:T(8,128)(2,1)S(1)} %get-tuple-element.51), channel_id=1, source_target_pairs={{0,8},{8,0},{16,24},{24,16},{1,9},{9,1},{17,25},{25,17},{2,10},{10... | collective-permute-start | bytes 589832 | tf_op jit(solution)/shard_map/ppermute | solution.py:597
  28.3 3.9 %collective-permute-start.11 = (bf16[3,16,2048]{2,1,0:T(8,128)(2,1)S(1)}, bf16[3,16,2048]{2,1,0:T(8,128)(2,1)S(1)}, u32[]{:S(2)}, u32[]{:S(2)}) collective-permute-start(bf16[3,16,2048]{2,1,0:T(8,128)(2,1)S(1)} %get-tuple-element.52), channel_id=1, source_target_pairs={{0,8},{8,0},{16,24},{24,16},{1,9},{9,1},{17,25},{25,17},{2,10},{10... | collective-permute-start | bytes 589832 | tf_op jit(solution)/shard_map/ppermute | solution.py:597
  31.5 1.7 %collective-permute-start.7 = (bf16[32,2048]{1,0:T(8,128)(2,1)S(1)}, bf16[32,2048]{1,0:T(8,128)(2,1)S(1)}, u32[]{:S(2)}, u32[]{:S(2)}) collective-permute-start(bf16[32,2048]{1,0:T(8,128)(2,1)S(1)} %get-tuple-element.47), channel_id=1, source_target_pairs={{0,8},{8,0},{16,24},{24,16},{1,9},{9,1},{17,25},{25,17},{2,10},{10... | collective-permute-start | bytes 393224 | tf_op jit(solution)/shard_map/ppermute | solution.py:597
  31.6 1.6 %collective-permute-start.8 = (bf16[32,2048]{1,0:T(8,128)(2,1)S(1)}, bf16[32,2048]{1,0:T(8,128)(2,1)S(1)}, u32[]{:S(2)}, u32[]{:S(2)}) collective-permute-start(bf16[32,2048]{1,0:T(8,128)(2,1)S(1)} %get-tuple-element.48), channel_id=1, source_target_pairs={{0,8},{8,0},{16,24},{24,16},{1,9},{9,1},{17,25},{25,17},{2,10},{10... | collective-permute-start | bytes 393224 | tf_op jit(solution)/shard_map/ppermute | solution.py:597
  32.1 1.3 %collective-permute-start.9 = (bf16[32,2048]{1,0:T(8,128)(2,1)S(1)}, bf16[32,2048]{1,0:T(8,128)(2,1)S(1)}, u32[]{:S(2)}, u32[]{:S(2)}) collective-permute-start(bf16[32,2048]{1,0:T(8,128)(2,1)S(1)} %get-tuple-element.49), channel_id=1, source_target_pairs={{0,8},{8,0},{16,24},{24,16},{1,9},{9,1},{17,25},{25,17},{2,10},{10... | collective-permute-start | bytes 393224 | tf_op jit(solution)/shard_map/ppermute | solution.py:597

commit v8 on v6

--- a/solution.py
+++ b/solution.py
@@ -9,7 +9,8 @@
 from jax.sharding import PartitionSpec as P
 
 LANES = 128
-TILE = 16
+TILE = 32
+ALIGN = 16
 LITTLE = pl.CostEstimate(flops=1, bytes_accessed=1, transcendentals=0)
 CHUNKS = 2
 
@@ -485,7 +486,7 @@
 def output_copies(which, piece, outs, chunk, sems, at, offset=0):
     half = outs[0].shape[0] // 2
     start = which * half + chunk_start(chunk, half // CHUNKS) + offset
-    rows = pl.ds(pl.multiple_of(start, TILE), piece[0].shape[0])
+    rows = pl.ds(pl.multiple_of(start, ALIGN), piece[0].shape[0])
     return [
         pltpu.make_async_copy(part, out.at[rows], sems.at[at + j])
         for j, (part, out) in enumerate(zip(piece, outs))
@@ -515,9 +516,8 @@
         copy.start()
     start = 0
     for out in out_others:
-        for row in range(0, out.shape[1], TILE):
-            for j in range(3):
-                out[j, row : row + TILE, :] = given[j, start + row : start + row + TILE, :]
+        for j in range(3):
+            out[j] = given[j, start : start + out.shape[1], :]
         start += out.shape[1]
     for copy in copies:
         copy.wait()

time: 35.2 us -> 35.2 us (level)
  Pallas kernels: 12.4 us -> 11.5 us
  waiting for transfers between devices: 7.86 us -> 8.51 us
    pallas_call x10, Pallas kernels: 12.4 us -> 11.5 us  [call(): pl.pallas_call(kernel, in_specs=[any_spec if j in hbm else vmem_spec for...]
    ppermute x12, waiting for transfers between devices: 7.21 us -> 7.89 us  [swap(): return lax.ppermute(x, 'tm', [(i, i ^ bits) for i in range(4)])]
  transfers between devices with their start and end apart: 13 -> 13, of which waited for: 5 -> 5; matrix products, arithmetic and copies ran while one was open for 0% -> 0% of each run, Pallas kernels for 29% -> 26%
where the time goes in v8:
time: 35.2 us; the launch traced here: 35 us
  starting transfers between devices  14 us (40%)
  Pallas kernels  11.5 us (33%)
  waiting for transfers between devices  8.51 us (24%)
  between operations  0.92 us (3%)
    pallas_call x10, Pallas kernels, call(): pl.pallas_call(kernel, in_specs=[any_spec if j in hbm else vmem_spec for...  11.5 us
    ppermute x12, waiting for transfers between devices, swap(): return lax.ppermute(x, 'tm', [(i, i ^ bits) for i in range(4)])  7.89 us
    ppermute x12, starting transfers between devices, swap(): return lax.ppermute(x, 'tm', [(i, i ^ bits) for i in range(4)])  7.7 us
    all_to_all x1, starting transfers between devices, by_chips(): lax.all_to_all(shares, tuple((axis for axis, _ in sizes)), 0, 0, tiled=True)  6.33 us
  transfers between devices with their start and end apart: 13, of which 5 were waited for; matrix products, arithmetic and copies ran while one was open for 0% of the time, Pallas kernels for 26%

profile of v8, /device:TPU:0, one launch (start us, length us, event | category | flops | bytes accessed | tf_op | source)
XLA Modules:
  0.0 35.0 jit_solution(15122936849879491737)
XLA Ops:
  0.6 1.4 %fetch_theirs.1 = (bf16[4,32,2048]{2,1,0:T(8,128)(2,1)S(1)}, bf16[4,32,2048]{2,1,0:T(8,128)(2,1)S(1)}, bf16[2,32,2048]{2,1,0:T(8,128)(2,1)S(1)}) custom-call(bf16[128,2048]{1,0:T(8,128)(2,1)} %bitcast.15, bf16[128,2048]{1,0:T(8,128)(2,1)} %bitcast.17, bf16[128,2048]{1,0:T(8,128)(2,1)} %bitcast.19, bf16[128,2048]{1,0:T(8,128)(2,1)} %bitcast.21), custom_call_target="tpu_custom_call" | custom-call | flops 1 | bytes 1 | tf_op jit(solution)/shard_map/fetch_theirs/pallas_call | solution.py:599
  2.0 0.5 %collective-permute-start = (bf16[4,32,2048]{2,1,0:T(8,128)(2,1)S(1)}, bf16[4,32,2048]{2,1,0:T(8,128)(2,1)S(1)}, u32[]{:S(2)}, u32[]{:S(2)}) collective-permute-start(bf16[4,32,2048]{2,1,0:T(8,128)(2,1)S(1)} %get-tuple-element.37), channel_id=1, source_target_pairs={{0,8},{8,0},{16,24},{24,16},{1,9},{9,1},{17,25},{25,17},{2,10},{10... | collective-permute-start | bytes 1572872 | tf_op jit(solution)/shard_map/ppermute | solution.py:593
  2.5 0.1 collective-permute-start.1
  2.6 2.6 %collective-permute-start.3 = (bf16[2,32,2048]{2,1,0:T(8,128)(2,1)S(1)}, bf16[2,32,2048]{2,1,0:T(8,128)(2,1)S(1)}, u32[]{:S(2)}, u32[]{:S(2)}) collective-permute-start(bf16[2,32,2048]{2,1,0:T(8,128)(2,1)S(1)} %get-tuple-element.35.after), channel_id=1, source_target_pairs={{0,24},{8,16},{16,8},{24,0},{1,25},{9,17},{17,9},{25,1},{2,26},{10... | collective-permute-start | bytes 786440 | tf_op jit(solution)/shard_map/ppermute | solution.py:593
  5.3 0.0 copy-start
  5.3 1.4 %fetch_mine.1 = (bf16[4,32,2048]{2,1,0:T(8,128)(2,1)S(1)}, bf16[4,32,2048]{2,1,0:T(8,128)(2,1)S(1)}) custom-call(bf16[128,2048]{1,0:T(8,128)(2,1)} %bitcast.16, bf16[128,2048]{1,0:T(8,128)(2,1)} %bitcast.18, bf16[128,2048]{1,0:T(8,128)(2,1)} %bitcast.20, bf16[128,2048]{1,0:T(8,128)(2,1)} %bitcast.22, bf16[2,32,2048]{2,1,0:T(8,128)(2,1)S(1)} %get-tuple-element.35.after), custom_call_target="tpu_custom_call" | custom-call | flops 1 | bytes 1 | tf_op jit(solution)/shard_map/fetch_mine/pallas_call | solution.py:599
  6.6 0.0 copy-done
  6.6 0.0 collective-permute-done.refs_3_.near
  6.7 0.0 collective-permute-done.1.refs_2_.near
  6.7 2.1 %local_scores.1 = (f32[32,128]{1,0:T(8,128)S(1)}, f32[32,128]{1,0:T(8,128)S(1)}, f32[8,128]{1,0:T(8,128)S(1)}, bf16[2,32,2048]{2,1,0:T(8,128)(2,1)}, bf16[32,230...) custom-call(f32[8,128]{1,0:T(8,128)S(1)} %pad.4.table, ...), custom_call_target="tpu_custom_call" | custom-call | flops 1 | bytes 1 | tf_op jit(solution)/shard_map/local_scores/pallas_call | solution.py:599
  8.7 1.0 %collective-permute-start.4 = (bf16[32,2304]{1,0:T(8,128)(2,1)S(1)}, bf16[32,2304]{1,0:T(8,128)(2,1)S(1)}, u32[]{:S(2)}, u32[]{:S(2)}) collective-permute-start(bf16[32,2304]{1,0:T(8,128)(2,1)S(1)} %get-tuple-element.44), channel_id=1, source_target_pairs={{0,16},{8,24},{16,0},{24,8},{1,17},{9,25},{17,1},{25,9},{2,18},{10... | collective-permute-start | bytes 442376 | tf_op jit(solution)/shard_map/ppermute | solution.py:593
  9.8 1.0 %collective-permute-start.5 = (bf16[32,2304]{1,0:T(8,128)(2,1)S(1)}, bf16[32,2304]{1,0:T(8,128)(2,1)S(1)}, u32[]{:S(2)}, u32[]{:S(2)}) collective-permute-start(bf16[32,2304]{1,0:T(8,128)(2,1)S(1)} %get-tuple-element.45), channel_id=1, source_target_pairs={{0,16},{8,24},{16,0},{24,8},{1,17},{9,25},{17,1},{25,9},{2,18},{10... | collective-permute-start | bytes 442376 | tf_op jit(solution)/shard_map/ppermute | solution.py:593
  10.7 1.0 %collective-permute-start.2 = (bf16[2,32,2048]{2,1,0:T(8,128)(2,1)}, bf16[2,32,2048]{2,1,0:T(8,128)(2,1)S(1)}, u32[]{:S(2)}, u32[]{:S(2)}) collective-permute-start(bf16[2,32,2048]{2,1,0:T(8,128)(2,1)} %get-tuple-element.40), channel_id=1, source_target_pairs={{0,16},{8,24},{16,0},{24,8},{1,17},{9,25},{17,1},{25,9},{2,18},{10... | collective-permute-start | bytes 786440 | tf_op jit(solution)/shard_map/ppermute | solution.py:593
  11.8 0.2 collective-permute-start.6
  12.0 0.0 collective-permute-done.3.refs_0_.refs_2_
  12.0 0.4 %first_dots.1.known = f32[32,128]{1,0:T(8,128)S(1)} custom-call(bf16[4,32,2048]{2,1,0:T(8,128)(2,1)S(1)} %get-tuple-element.38.refs_0_.mine, bf16[4,32,2048]{2,1,0:T(8,128)(2,1)S(1)} %collective-permute-done.1.refs_2_.near, bf16[2,32,2048]{2,1,0:T(8,128)(2,1)S(1)} %collective-permute-done.3.refs_0_.refs_2_), custom_call_target="tpu_custom_call" | custom-call | flops 1 | bytes 1 | tf_op jit(solution)/shard_map/first_dots/pallas_call | solution.py:599
  12.4 3.2 %collective-permute-done.4.refs_0_ = bf16[32,2304]{1,0:T(8,128)(2,1)S(1)} collective-permute-done((bf16[32,2304]{1,0:T(8,128)(2,1)S(1)}, bf16[32,2304]{1,0:T(8,128)(2,1)S(1)}, u32[]{:S(2)}, u32[]{:S(2)}) %collective-permute-start.4) | collective-permute-done | bytes 147488 | tf_op jit(solution)/shard_map/ppermute | solution.py:593
  15.6 3.2 %collective-permute-done.5.refs_1_ = bf16[32,2304]{1,0:T(8,128)(2,1)S(1)} collective-permute-done((bf16[32,2304]{1,0:T(8,128)(2,1)S(1)}, bf16[32,2304]{1,0:T(8,128)(2,1)S(1)}, u32[]{:S(2)}, u32[]{:S(2)}) %collective-permute-start.5) | collective-permute-done | bytes 147488 | tf_op jit(solution)/shard_map/ppermute | solution.py:593
  18.7 1.1 %scores.1 = (bf16[14,32,128]{2,1,0:T(8,128)(2,1)S(1)}, f32[32,8,128]{2,1,0:T(8,128)}, f32[32,128]{1,0:T(8,128)S(1)}) custom-call(f32[32,128]{1,0:T(8,128)S(1)} %first_dots.1.known, f32[8,128]{1,0:T(8,128)S(1)} %pad.4.table, f32[32,128]{1,0:T(8,128)S(1)} %get-tuple-element.42.small, f32[8,128]{1,0:T(8,128)S(1)} %get-tuple-element.43.bias, ...), custom_call_target="tpu_custom_call" | custom-call | flops 1 | bytes 1 | tf_op jit(solution)/shard_map/scores/pallas_call | solution.py:599
  19.9 6.3 %all-to-all-start = ((f32[32,8,128]{2,1,0:T(8,128)}), f32[32,8,128]{2,1,0:T(8,128)S(1)}, u32[]{:S(2)}, u32[]{:S(2)}) async-start(f32[32,8,128]{2,1,0:T(8,128)} %get-tuple-element.51), calls=%async_computation | async-start | bytes 262144 | tf_op jit(solution)/shard_map/all_to_all | solution.py:661
  26.2 1.5 %gradients.1 = (bf16[3,16,2048]{2,1,0:T(8,128)(2,1)S(1)}, bf16[3,16,2048]{2,1,0:T(8,128)(2,1)S(1)}, bf16[128,2048]{1,0:T(8,128)(2,1)}, bf16[128,2048]{1,0:T(8,128)(2,1)}, bf16[128,2048]{1,0:T(8,128)(2,1)}) custom-call(bf16[14,32,128]{2,1,0:T(8,128)(2,1)S(1)} %get-tuple-element.52.items_ref, bf16[4,32,2048]{2,1,0:T(8,128)(2,1)S(1)} %get-tuple-element.38.refs_0_.mine, ...), custom_call_target="tpu_custom_call" | custom-call | flops 1 | bytes 1 | tf_op jit(solution)/shard_map/gradients/pallas_call | solution.py:599
  27.7 0.3 collective-permute-start.10
  28.0 0.3 collective-permute-start.11
  28.3 0.0 collective-permute-done.2.refs_0_
  28.3 0.4 %last_dots.1.known = f32[32,128]{1,0:T(8,128)S(1)} custom-call(bf16[4,32,2048]{2,1,0:T(8,128)(2,1)S(1)} %get-tuple-element.36.refs_1_.mine, bf16[4,32,2048]{2,1,0:T(8,128)(2,1)S(1)} %collective-permute-done.refs_3_.near, bf16[2,32,2048]{2,1,0:T(8,128)(2,1)S(1)} %collective-permute-done.2.refs_0_), custom_call_target="tpu_custom_call" | custom-call | flops 1 | bytes 1 | tf_op jit(solution)/shard_map/last_dots/pallas_call | solution.py:599
  28.7 1.3 %collective-permute-done.6.refs_1_ = bf16[2,32,2048]{2,1,0:T(8,128)(2,1)S(1)} collective-permute-done((bf16[2,32,2048]{2,1,0:T(8,128)(2,1)}, bf16[2,32,2048]{2,1,0:T(8,128)(2,1)S(1)}, u32[]{:S(2)}, u32[]{:S(2)}) %collective-permute-start.6) | collective-permute-done | bytes 262176 | tf_op jit(solution)/shard_map/ppermute | solution.py:593
  30.0 1.4 %scores_and_gradients.1 = (bf16[3,32,2048]{2,1,0:T(8,128)(2,1)S(1)}, bf16[32,2048]{1,0:T(8,128)(2,1)S(1)}, bf16[32,2048]{1,0:T(8,128)(2,1)S(1)}, bf16[32,2048]{1,0:T(8,128)(2,1)S(1)}) custom-call(f32[32,128]{1,0:T(8,128)S(1)} %last_dots.1.known, f32[8,128]{1,0:T(8,128)S(1)} %pad.4.table, f32[32,128]{1,0:T(8,128)S(1)} %get-tuple-element.41.small, ...), custom_call_target="tpu_custom_call" | custom-call | flops 1 | bytes 1 | tf_op jit(solution)/shard_map/scores_and_gradients/pallas_call | solution.py:599
  31.4 0.1 collective-permute-start.7
  31.5 0.5 %collective-permute-start.8 = (bf16[32,2048]{1,0:T(8,128)(2,1)S(1)}, bf16[32,2048]{1,0:T(8,128)(2,1)S(1)}, u32[]{:S(2)}, u32[]{:S(2)}) collective-permute-start(bf16[32,2048]{1,0:T(8,128)(2,1)S(1)} %get-tuple-element.49), channel_id=1, source_target_pairs={{0,8},{8,0},{16,24},{24,16},{1,9},{9,1},{17,25},{25,17},{2,10},{10... | collective-permute-start | bytes 393224 | tf_op jit(solution)/shard_map/ppermute | solution.py:593
  32.0 0.1 collective-permute-start.9
  32.0 0.0 collective-permute-done.10.refs_0_
  32.0 0.0 collective-permute-done.11.refs_1_
  32.0 1.0 %early_outputs.1 = (bf16[128,2048]{1,0:T(8,128)(2,1)}, bf16[128,2048]{1,0:T(8,128)(2,1)}, bf16[128,2048]{1,0:T(8,128)(2,1)}) custom-call(bf16[3,16,2048]{2,1,0:T(8,128)(2,1)S(1)} %collective-permute-done.10.refs_0_, bf16[3,16,2048]{2,1,0:T(8,128)(2,1)S(1)} %collective-permute-done.11.refs_1_, ...), custom_call_target="tpu_custom_call", output_to_operand_aliasing={{0}: (3, {}), {1}: (4, {}), {2}: (5, {})} | custom-call | flops 1 | bytes 1 | tf_op jit(solution)/shard_map/early_outputs/pallas_call | solution.py:599
  33.0 0.0 collective-permute-done.7.refs_0_
  33.0 0.0 collective-permute-done.8.refs_1_
  33.1 0.3 collective-permute-done.9.refs_2_
  33.3 0.6 %all-to-all-done.refs_3_ = f32[32,8,128]{2,1,0:T(8,128)S(1)} async-done(((f32[32,8,128]{2,1,0:T(8,128)}), f32[32,8,128]{2,1,0:T(8,128)S(1)}, u32[]{:S(2)}, u32[]{:S(2)}) %all-to-all-start) | async-done | bytes 131104 | tf_op jit(solution)/shard_map/all_to_all | solution.py:661
  33.9 0.9 %outputs.1 = (bf16[128,2048]{1,0:T(8,128)(2,1)}, bf16[128,2048]{1,0:T(8,128)(2,1)}, bf16[128,2048]{1,0:T(8,128)(2,1)}, f32[4,16]{1,0:T(4,128)}) custom-call(bf16[32,2048]{1,0:T(8,128)(2,1)S(1)} %collective-permute-done.7.refs_0_, bf16[32,2048]{1,0:T(8,128)(2,1)S(1)} %collective-permute-done.8.refs_1_, ...), custom_call_target="tpu_custom_call", output_to_operand_aliasing={{0}: (4, {}), {1}: (5, {}), {2}: (6, {})} | custom-call | flops 1 | bytes 1 | tf_op jit(solution)/shard_map/outputs/pallas_call | solution.py:599
  (1 shorter events, 0.0 us)
Async XLA Ops:
  2.0 4.6 %collective-permute-start = (bf16[4,32,2048]{2,1,0:T(8,128)(2,1)S(1)}, bf16[4,32,2048]{2,1,0:T(8,128)(2,1)S(1)}, u32[]{:S(2)}, u32[]{:S(2)}) collective-permute-start(bf16[4,32,2048]{2,1,0:T(8,128)(2,1)S(1)} %get-tuple-element.37), channel_id=1, source_target_pairs={{0,8},{8,0},{16,24},{24,16},{1,9},{9,1},{17,25},{25,17},{2,10},{10... | collective-permute-start | bytes 1572872 | tf_op jit(solution)/shard_map/ppermute | solution.py:593
  2.5 4.1 %collective-permute-start.1 = (bf16[4,32,2048]{2,1,0:T(8,128)(2,1)S(1)}, bf16[4,32,2048]{2,1,0:T(8,128)(2,1)S(1)}, u32[]{:S(2)}, u32[]{:S(2)}) collective-permute-start(bf16[4,32,2048]{2,1,0:T(8,128)(2,1)S(1)} %get-tuple-element.39.refs_4_), channel_id=1, source_target_pairs={{0,8},{8,0},{16,24},{24,16},{1,9},{9,1},{17,25},{25,17},{2,10},{10... | collective-permute-start | bytes 1572872 | tf_op jit(solution)/shard_map/ppermute | solution.py:593
  2.6 9.4 %collective-permute-start.3 = (bf16[2,32,2048]{2,1,0:T(8,128)(2,1)S(1)}, bf16[2,32,2048]{2,1,0:T(8,128)(2,1)S(1)}, u32[]{:S(2)}, u32[]{:S(2)}) collective-permute-start(bf16[2,32,2048]{2,1,0:T(8,128)(2,1)S(1)} %get-tuple-element.35.after), channel_id=1, source_target_pairs={{0,24},{8,16},{16,8},{24,0},{1,25},{9,17},{17,9},{25,1},{2,26},{10... | collective-permute-start | bytes 786440 | tf_op jit(solution)/shard_map/ppermute | solution.py:593
  5.3 1.4 %copy-start = (f32[16,4]{0,1:T(4,128)S(1)}, f32[16,4]{0,1:T(4,128)}, u32[]{:S(2)}) copy-start(f32[16,4]{0,1:T(4,128)} %param.9) | copy-start | bytes 772
  8.7 6.8 %collective-permute-start.4 = (bf16[32,2304]{1,0:T(8,128)(2,1)S(1)}, bf16[32,2304]{1,0:T(8,128)(2,1)S(1)}, u32[]{:S(2)}, u32[]{:S(2)}) collective-permute-start(bf16[32,2304]{1,0:T(8,128)(2,1)S(1)} %get-tuple-element.44), channel_id=1, source_target_pairs={{0,16},{8,24},{16,0},{24,8},{1,17},{9,25},{17,1},{25,9},{2,18},{10... | collective-permute-start | bytes 442376 | tf_op jit(solution)/shard_map/ppermute | solution.py:593
  9.8 9.0 %collective-permute-start.5 = (bf16[32,2304]{1,0:T(8,128)(2,1)S(1)}, bf16[32,2304]{1,0:T(8,128)(2,1)S(1)}, u32[]{:S(2)}, u32[]{:S(2)}) collective-permute-start(bf16[32,2304]{1,0:T(8,128)(2,1)S(1)} %get-tuple-element.45), channel_id=1, source_target_pairs={{0,16},{8,24},{16,0},{24,8},{1,17},{9,25},{17,1},{25,9},{2,18},{10... | collective-permute-start | bytes 442376 | tf_op jit(solution)/shard_map/ppermute | solution.py:593
  10.7 17.6 %collective-permute-start.2 = (bf16[2,32,2048]{2,1,0:T(8,128)(2,1)}, bf16[2,32,2048]{2,1,0:T(8,128)(2,1)S(1)}, u32[]{:S(2)}, u32[]{:S(2)}) collective-permute-start(bf16[2,32,2048]{2,1,0:T(8,128)(2,1)} %get-tuple-element.40), channel_id=1, source_target_pairs={{0,16},{8,24},{16,0},{24,8},{1,17},{9,25},{17,1},{25,9},{2,18},{10... | collective-permute-start | bytes 786440 | tf_op jit(solution)/shard_map/ppermute | solution.py:593
  11.8 18.2 %collective-permute-start.6 = (bf16[2,32,2048]{2,1,0:T(8,128)(2,1)}, bf16[2,32,2048]{2,1,0:T(8,128)(2,1)S(1)}, u32[]{:S(2)}, u32[]{:S(2)}) collective-permute-start(bf16[2,32,2048]{2,1,0:T(8,128)(2,1)} %get-tuple-element.47), channel_id=1, source_target_pairs={{0,24},{8,16},{16,8},{24,0},{1,25},{9,17},{17,9},{25,1},{2,26},{10... | collective-permute-start | bytes 786440 | tf_op jit(solution)/shard_map/ppermute | solution.py:593
  19.9 14.1 %all-to-all-start = ((f32[32,8,128]{2,1,0:T(8,128)}), f32[32,8,128]{2,1,0:T(8,128)S(1)}, u32[]{:S(2)}, u32[]{:S(2)}) async-start(f32[32,8,128]{2,1,0:T(8,128)} %get-tuple-element.51), calls=%async_computation | async-start | bytes 262144 | tf_op jit(solution)/shard_map/all_to_all | solution.py:661
  27.7 4.3 %collective-permute-start.10 = (bf16[3,16,2048]{2,1,0:T(8,128)(2,1)S(1)}, bf16[3,16,2048]{2,1,0:T(8,128)(2,1)S(1)}, u32[]{:S(2)}, u32[]{:S(2)}) collective-permute-start(bf16[3,16,2048]{2,1,0:T(8,128)(2,1)S(1)} %get-tuple-element.53), channel_id=1, source_target_pairs={{0,8},{8,0},{16,24},{24,16},{1,9},{9,1},{17,25},{25,17},{2,10},{10... | collective-permute-start | bytes 589832 | tf_op jit(solution)/shard_map/ppermute | solution.py:593
  28.0 4.0 %collective-permute-start.11 = (bf16[3,16,2048]{2,1,0:T(8,128)(2,1)S(1)}, bf16[3,16,2048]{2,1,0:T(8,128)(2,1)S(1)}, u32[]{:S(2)}, u32[]{:S(2)}) collective-permute-start(bf16[3,16,2048]{2,1,0:T(8,128)(2,1)S(1)} %get-tuple-element.54), channel_id=1, source_target_pairs={{0,8},{8,0},{16,24},{24,16},{1,9},{9,1},{17,25},{25,17},{2,10},{10... | collective-permute-start | bytes 589832 | tf_op jit(solution)/shard_map/ppermute | solution.py:593
  31.4 1.7 %collective-permute-start.7 = (bf16[32,2048]{1,0:T(8,128)(2,1)S(1)}, bf16[32,2048]{1,0:T(8,128)(2,1)S(1)}, u32[]{:S(2)}, u32[]{:S(2)}) collective-permute-start(bf16[32,2048]{1,0:T(8,128)(2,1)S(1)} %get-tuple-element.48), channel_id=1, source_target_pairs={{0,8},{8,0},{16,24},{24,16},{1,9},{9,1},{17,25},{25,17},{2,10},{10... | collective-permute-start | bytes 393224 | tf_op jit(solution)/shard_map/ppermute | solution.py:593
  31.5 1.6 %collective-permute-start.8 = (bf16[32,2048]{1,0:T(8,128)(2,1)S(1)}, bf16[32,2048]{1,0:T(8,128)(2,1)S(1)}, u32[]{:S(2)}, u32[]{:S(2)}) collective-permute-start(bf16[32,2048]{1,0:T(8,128)(2,1)S(1)} %get-tuple-element.49), channel_id=1, source_target_pairs={{0,8},{8,0},{16,24},{24,16},{1,9},{9,1},{17,25},{25,17},{2,10},{10... | collective-permute-start | bytes 393224 | tf_op jit(solution)/shard_map/ppermute | solution.py:593
  32.0 1.3 %collective-permute-start.9 = (bf16[32,2048]{1,0:T(8,128)(2,1)S(1)}, bf16[32,2048]{1,0:T(8,128)(2,1)S(1)}, u32[]{:S(2)}, u32[]{:S(2)}) collective-permute-start(bf16[32,2048]{1,0:T(8,128)(2,1)S(1)} %get-tuple-element.50), channel_id=1, source_target_pairs={{0,8},{8,0},{16,24},{24,16},{1,9},{9,1},{17,25},{25,17},{2,10},{10... | collective-permute-start | bytes 393224 | tf_op jit(solution)/shard_map/ppermute | solution.py:593

commit v9 on v8

--- a/solution.py
+++ b/solution.py
@@ -13,6 +13,7 @@
 ALIGN = 16
 LITTLE = pl.CostEstimate(flops=1, bytes_accessed=1, transcendentals=0)
 CHUNKS = 2
+FORWARD_MORE = 6
 
 
 def score_table(bias_rows, frames):
@@ -213,17 +214,24 @@
     return jnp.where(my_place()[1] == 0, chunk, CHUNKS - 1 - chunk) * size
 
 
-def copy_chunks(sources, core, outs, sems):
-    size = outs[0].shape[1]
+def chunk_copies(sources, core, outs, sems, at=0):
     copies = []
     for c, out in enumerate(outs):
-        start = pl.multiple_of(core * CHUNKS * size + chunk_start(c, size), TILE)
+        if out is None:
+            continue
+        size = out.shape[1]
+        start = pl.multiple_of(core * CHUNKS * size + chunk_start(c, size), ALIGN)
         for j, ref in enumerate(sources):
             copies.append(
                 pltpu.make_async_copy(
-                    ref.at[pl.ds(start, size)], out.at[j], sems.at[len(copies)]
+                    ref.at[pl.ds(start, size)], out.at[j], sems.at[at + len(copies)]
                 )
             )
+    return copies
+
+
+def copy_chunks(sources, core, outs, sems):
+    copies = chunk_copies(sources, core, outs, sems)
     for copy in copies:
         copy.start()
     for copy in copies:
@@ -243,10 +251,35 @@
     pl.when(chip == 1)(lambda: take((0, 3)))
 
 
-def fetch_theirs_kernel(q, k, v, o, *refs):
-    nears, other, sems = refs[:CHUNKS], refs[CHUNKS], refs[CHUNKS + 1]
-    copy_chunks((q, k, v, o), 1 - my_place()[0], nears, sems)
-    take_far(planes(nears[CHUNKS - 1]), planes(other))
+def fetch_other_kernel(q, k, v, o, other, got, sems):
+    core, chip = my_place()
+
+    def fetch(arrays):
+        copy_chunks(arrays, 1 - core, (None,) * (CHUNKS - 1) + (got,), sems)
+        for j in range(2):
+            other[j, :, : got.shape[2]] = got[j]
+            other[j, :, got.shape[2] :] = jnp.zeros((other.shape[1], LANES), jnp.bfloat16)
+
+    pl.when(chip == 0)(lambda: fetch((k, v)))
+    pl.when(chip == 1)(lambda: fetch((q, o)))
+
+
+def forward_kernel(came, out):
+    size, width = came.shape[1], out.shape[1]
+    for j in range(2):
+        out[j * size : (j + 1) * size, :] = came[j, :, :width]
+    out[2 * size :, :] = jnp.zeros((out.shape[0] - 2 * size, width), jnp.bfloat16)
+
+
+def fetch_theirs_kernel(q, k, v, o, after, *refs):
+    *nears, sems = refs
+    core = 1 - my_place()[0]
+    copies = chunk_copies((q, k), core, nears[:CHUNKS], sems)
+    copies += chunk_copies((v, o), core, nears[CHUNKS:], sems, len(copies))
+    for copy in copies:
+        copy.start()
+    for copy in copies:
+        copy.wait()
 
 
 def fetch_mine_kernel(q, k, v, o, after, *refs):
@@ -277,8 +310,10 @@
 
 
 def local_kernel(heads, scale, table, *refs):
-    mines, nears, theirs, refs = refs[:2], refs[2:4], refs[4], refs[5:]
-    smalls, out_bias, other, sames = refs[:2], refs[2], refs[3], (refs[4:6], planes(refs[6]))
+    mines, refs = refs[:2], refs[2:]
+    nears = [planes(refs[0]) + planes(refs[2]), planes(refs[1]) + planes(refs[3])]
+    theirs, refs = planes(refs[4]) + planes(refs[5]), refs[6:]
+    smalls, out_bias, other, sames = refs[:2], refs[2], refs[3], [planes(x) for x in refs[4:]]
     core, chip = my_place()
     size, width = mines[0].shape[1:]
     offset = [table[d : d + 1, :] for d in range(4)]
@@ -301,11 +336,11 @@
         over_tiles(size, tile)
 
     for mine, near, small in zip(mines, nears, smalls):
-        own, neighbour = shifted(planes(mine), 0), shifted(planes(near), 0)
+        own, neighbour = shifted(planes(mine), 0), shifted(near, 0)
         pl.when(core == 0)(functools.partial(run, own, neighbour, small))
         pl.when(core == 1)(functools.partial(run, neighbour, own, small))
 
-    take_far(planes(theirs), planes(other))
+    take_far(theirs, planes(other))
     for c, out in enumerate(sames):
         take_far(planes(mines[1 - c]), out)
         for row in range(0, size, TILE):
@@ -335,10 +370,10 @@
     )
 
 
-def piece_kernel(heads, same, mine, near, *refs):
+def piece_kernel(heads, same, mine, near_first, near_second, *refs):
     far, out = refs[:-1], refs[-1]
-    piece = far if len(far) == 2 else planes(far[0])
-    own, other = planes(mine), planes(near)
+    piece = pair_of(far)
+    own, other = planes(mine), planes(near_first) + planes(near_second)
     if same:
         own, other = own + piece, other + (None, None)
     else:
@@ -440,28 +475,33 @@
     return tuple(ref.at[j] for j in range(ref.shape[0]))
 
 
-def frames_of(mine, near, far):
-    *same, other = far
+def frames_of(mine, near, same, other):
+    near_first, near_second = near
     return (
         shifted(planes(mine) + pair_of(same), 0),
-        shifted(planes(near) + planes(other), 0),
-    )
-
-
-def pair_of(same):
-    return tuple(same) if len(same) == 2 else planes(same[0])
+        shifted(planes(near_first) + planes(near_second) + pair_of(other), 0),
+    )
+
+
+def pair_of(piece):
+    (ref,) = piece
+    if len(ref.shape) == 3:
+        return planes(ref)
+    return tuple(ref.at[j * TILE * (ref.shape[0] // 2 // TILE) :] for j in range(2))
 
 
 def far_small(far, rows, width, heads, chunk):
     at = slice(width + chunk * LANES, width + (chunk + 1) * LANES)
-    return unpacked_small(*(ref[rows, at] for ref in pair_of(far[:-1])), heads)
-
-
-def score_kernel(heads, scale, known, table, small, bias, mine, near, *refs):
-    far, (out_items, out_shares, out_small), lines_ref = refs[:3], refs[3:6], refs[6]
+    return unpacked_small(*(ref[rows, at] for ref in far), heads)
+
+
+def score_kernel(heads, scale, known, table, small, bias, mine, *refs):
+    near, same, other = refs[:2], refs[2:3], refs[3:4]
+    far = pair_of(same)
+    (out_items, out_shares, out_small), lines_ref = refs[4:7], refs[7]
     size, width = mine.shape[1:]
     lines_ref[...] = bias[...]
-    own, neighbour = frames_of(mine, near, far)
+    own, neighbour = frames_of(mine, near, same, other)
 
     def work(chip, a, b):
         def tile(row):
@@ -493,9 +533,10 @@
     ]
 
 
-def gradient_kernel(heads, scale, items_ref, mine, near, *refs):
-    far, out_others, outs, kept, given, sems = refs[:3], refs[3:5], refs[5:8], *refs[8:]
-    own, neighbour = frames_of(mine, near, far)
+def gradient_kernel(heads, scale, items_ref, mine, *refs):
+    near, same, other, refs = refs[:2], refs[2:3], refs[3:4], refs[4:]
+    out_others, outs, kept, given, sems = refs[:2], refs[2:5], *refs[5:]
+    own, neighbour = frames_of(mine, near, same, other)
     own_out, other_out = shifted(planes(kept), 0), shifted(planes(given), 0)
 
     def work(chip, a, b):
@@ -523,9 +564,9 @@
         copy.wait()
 
 
-def whole_kernel(heads, scale, known, table, small, small_far, mine, near, *refs):
-    far, out_own, out_others = refs[:2], refs[2], refs[3:6]
-    own, neighbour = frames_of(mine, near, far)
+def whole_kernel(heads, scale, known, table, small, small_far, mine, *refs):
+    near, same, other, out_own, out_others = refs[:2], refs[2:3], refs[3:4], refs[4], refs[5:]
+    own, neighbour = frames_of(mine, near, same, other)
     own_out, other_out = shifted(planes(out_own), 0), shifted(out_others, 0)
 
     def work(chip, a, b):
@@ -614,38 +655,44 @@
     copies = [pltpu.SemaphoreType.DMA((4 * CHUNKS,))]
     table = jnp.pad(time_bias.T, ((0, 8 - frames), (0, LANES - heads)))
 
-    *theirs, other = call(
-        fetch_theirs_kernel, "fetch_theirs", [chunk_shape] * CHUNKS + [far_shape], *own,
-        scratch=copies, hbm=range(4),
+    pair = shape(2, size, width)
+    (other,) = call(
+        fetch_other_kernel, "fetch_other", [shape(2, size, width + LANES)], *own,
+        scratch=[pltpu.VMEM((2, size, width), jnp.bfloat16)] + copies, hbm=range(4),
+    )
+    came = swap(other, 2)
+    theirs = call(
+        fetch_theirs_kernel, "fetch_theirs", [pair] * (2 * CHUNKS), *own, other,
+        scratch=copies, hbm=range(5),
     )
     nears = [swap(x, 1) for x in theirs]
-    others = [swap(other, 3)]
     mines = call(
-        fetch_mine_kernel, "fetch_mine", [chunk_shape] * CHUNKS, *own, other,
+        fetch_mine_kernel, "fetch_mine", [chunk_shape] * CHUNKS, *own, theirs[0],
         scratch=copies, hbm=range(5),
     )
-
-    *smalls, bias, other, same_first, same_second, same = call(
+    (forward,) = call(forward_kernel, "forward", [shape(2 * size + FORWARD_MORE, width)], came)
+    others = [[swap(forward, 1)]]
+
+    *smalls, bias, other, same_first, same = call(
         functools.partial(local_kernel, heads, scale),
         "local_scores",
         [shape(size, LANES, dtype=wide)] * CHUNKS
         + [lines, far_shape]
-        + [shape(size, width + CHUNKS * LANES)] * 2
-        + [far_shape],
-        table, *mines, *nears, theirs[0],
-    )
-    sames = [[swap(same_first, 2), swap(same_second, 2)], [swap(same, 2)]]
-    others.append(swap(other, 3))
+        + [shape(2, size, width + CHUNKS * LANES), far_shape],
+        table, *mines, *nears, theirs[0], theirs[CHUNKS],
+    )
+    sames = [[swap(same_first, 2)], [swap(same, 2)]]
+    others.append([swap(other, 3)])
 
     whole = pltpu.HBM((rows, width), jnp.bfloat16)
     stack, piece = shape(3, size, width), shape(size, width)
     output_sems = pltpu.SemaphoreType.DMA((13,))
-    first = (mines[0], nears[0], *sames[0], others[0])
+    first = (mines[0], nears[0], nears[CHUNKS], *sames[0], *others[0])
     (known,) = call(
         functools.partial(piece_kernel, heads, False),
         "first_dots",
         [shape(size, LANES, dtype=wide)],
-        mines[0], nears[0], others[0],
+        mines[0], nears[0], nears[CHUNKS], *others[0],
     )
     items, shares, small_far = call(
         functools.partial(score_kernel, heads, scale),
@@ -674,13 +721,14 @@
         functools.partial(piece_kernel, heads, True),
         "last_dots",
         [shape(size, LANES, dtype=wide)],
-        mines[1], nears[1], *sames[1],
+        mines[1], nears[1], nears[CHUNKS + 1], *sames[1],
     )
     kept, *back = call(
         functools.partial(whole_kernel, heads, scale),
         "scores_and_gradients",
         [stack] + [piece] * 3,
-        known_last, table, smalls[1], small_far, mines[1], nears[1], *sames[1], others[1],
+        known_last, table, smalls[1], small_far, mines[1], nears[1], nears[CHUNKS + 1],
+        *sames[1], *others[1],
     )
     back = [swap(x, 1) for x in back]
     in_hbm = lambda arrays: [pltpu.with_memory_space_constraint(x, pltpu.HBM) for x in arrays]

time: 35.2 us -> 35.9 us (1.020)
  Pallas kernels: 11.5 us -> 12.6 us
  starting transfers between devices: 14 us -> 13.4 us
    all_to_all x1, starting transfers between devices: 6.33 us -> 4.89 us  [by_chips(): lax.all_to_all(shares, tuple((axis for axis, _ in sizes)), 0, 0, tiled=True)]
    pallas_call x10 -> x12, Pallas kernels: 11.5 us -> 12.6 us  [call(): pl.pallas_call(kernel, in_specs=[any_spec if j in hbm else vmem_spec for...]
    ppermute x12 -> x14, waiting for transfers between devices: 7.89 us -> 8.73 us  [swap(): return lax.ppermute(x, 'tm', [(i, i ^ bits) for i in range(4)])]
    ppermute x12 -> x14, starting transfers between devices: 7.7 us -> 8.47 us  [swap(): return lax.ppermute(x, 'tm', [(i, i ^ bits) for i in range(4)])]
    all_to_all x1, waiting for transfers between devices: 0.62 us -> 0.01 us  [by_chips(): lax.all_to_all(shares, tuple((axis for axis, _ in sizes)), 0, 0, tiled=True)]
  transfers between devices with their start and end apart: 13 -> 15, of which waited for: 5 -> 4; matrix products, arithmetic and copies ran while one was open for 0% -> 0% of each run, Pallas kernels for 26% -> 30%
where the time goes in v9:
time: 35.9 us; the launch traced here: 35.6 us
  starting transfers between devices  13.4 us (37%)
  Pallas kernels  12.6 us (35%)
  waiting for transfers between devices  8.73 us (24%)
  between operations  0.96 us (3%)
    pallas_call x12, Pallas kernels, call(): pl.pallas_call(kernel, in_specs=[any_spec if j in hbm else vmem_spec for...  12.6 us
    ppermute x14, waiting for transfers between devices, swap(): return lax.ppermute(x, 'tm', [(i, i ^ bits) for i in range(4)])  8.73 us
    ppermute x14, starting transfers between devices, swap(): return lax.ppermute(x, 'tm', [(i, i ^ bits) for i in range(4)])  8.47 us
    all_to_all x1, starting transfers between devices, by_chips(): lax.all_to_all(shares, tuple((axis for axis, _ in sizes)), 0, 0, tiled=True)  4.89 us
  transfers between devices with their start and end apart: 15, of which 4 were waited for; matrix products, arithmetic and copies ran while one was open for 0% of the time, Pallas kernels for 30%

profile of v9, /device:TPU:0, one launch (start us, length us, event | category | flops | bytes accessed | tf_op | source)
XLA Modules:
  0.0 35.6 jit_solution(15015183651370135127)
XLA Ops:
  0.6 1.1 %fetch_other.1.after = bf16[2,32,2176]{2,1,0:T(8,128)(2,1)S(1)} custom-call(bf16[128,2048]{1,0:T(8,128)(2,1)} %bitcast.15, bf16[128,2048]{1,0:T(8,128)(2,1)} %bitcast.18, bf16[128,2048]{1,0:T(8,128)(2,1)} %bitcast.21, bf16[128,2048]{1,0:T(8,128)(2,1)} %bitcast.24), custom_call_target="tpu_custom_call" | custom-call | flops 1 | bytes 1 | tf_op jit(solution)/shard_map/fetch_other/pallas_call | solution.py:640
  1.7 3.0 %collective-permute-start.5 = (bf16[2,32,2176]{2,1,0:T(8,128)(2,1)S(1)}, bf16[2,32,2176]{2,1,0:T(8,128)(2,1)S(1)}, u32[]{:S(2)}, u32[]{:S(2)}) collective-permute-start(bf16[2,32,2176]{2,1,0:T(8,128)(2,1)S(1)} %fetch_other.1.after), channel_id=1, source_target_pairs={{0,16},{8,24},{16,0},{24,8},{1,17},{9,25},{17,1},{25,9},{2,18},{10... | collective-permute-start | bytes 835592 | tf_op jit(solution)/shard_map/ppermute | solution.py:634
  4.8 1.3 %fetch_theirs.1 = (bf16[2,32,2048]{2,1,0:T(8,128)(2,1)S(1)}, bf16[2,32,2048]{2,1,0:T(8,128)(2,1)S(1)}, bf16[2,32,2048]{2,1,0:T(8,128)(2,1)S(1)}, bf16[2,32,2048]{2,1,0:T(8,128)(2,1)S(1)}) custom-call(bf16[128,2048]{1,0:T(8,128)(2,1)} %bitcast.16, bf16[128,2048]{1,0:T(8,128)(2,1)} %bitcast.19, bf16[128,2048]{1,0:T(8,128)(2,1)} %bitcast.22, ...), custom_call_target="tpu_custom_call" | custom-call | flops 1 | bytes 1 | tf_op jit(solution)/shard_map/fetch_theirs/pallas_call | solution.py:640
  6.1 0.1 collective-permute-start
  6.2 0.5 %collective-permute-start.1 = (bf16[2,32,2048]{2,1,0:T(8,128)(2,1)S(1)}, bf16[2,32,2048]{2,1,0:T(8,128)(2,1)S(1)}, u32[]{:S(2)}, u32[]{:S(2)}) collective-permute-start(bf16[2,32,2048]{2,1,0:T(8,128)(2,1)S(1)} %get-tuple-element.38), channel_id=1, source_target_pairs={{0,8},{8,0},{16,24},{24,16},{1,9},{9,1},{17,25},{25,17},{2,10},{10... | collective-permute-start | bytes 786440 | tf_op jit(solution)/shard_map/ppermute | solution.py:634
  6.7 0.1 collective-permute-start.3
  6.8 0.4 %collective-permute-start.2 = (bf16[2,32,2048]{2,1,0:T(8,128)(2,1)S(1)}, bf16[2,32,2048]{2,1,0:T(8,128)(2,1)S(1)}, u32[]{:S(2)}, u32[]{:S(2)}) collective-permute-start(bf16[2,32,2048]{2,1,0:T(8,128)(2,1)S(1)} %get-tuple-element.35.after.refs_6_), channel_id=1, source_target_pairs={{0,8},{8,0},{16,24},{24,16},{1,9},{9,1},{17,25},{25,17},{2,10},{10... | collective-permute-start | bytes 786440 | tf_op jit(solution)/shard_map/ppermute | solution.py:634
  7.2 0.0 copy-start
  7.2 1.4 %fetch_mine.1 = (bf16[4,32,2048]{2,1,0:T(8,128)(2,1)S(1)}, bf16[4,32,2048]{2,1,0:T(8,128)(2,1)S(1)}) custom-call(bf16[128,2048]{1,0:T(8,128)(2,1)} %bitcast.17, bf16[128,2048]{1,0:T(8,128)(2,1)} %bitcast.20, bf16[128,2048]{1,0:T(8,128)(2,1)} %bitcast.23, bf16[128,2048]{1,0:T(8,128)(2,1)} %bitcast.26, bf16[2,32,2048]{2,1,0:T(8,128)(2,1)S(1)} %get-tuple-element.35.after.refs_6_), custom_call_target="tpu_custom_call" | custom-call | flops 1 | bytes 1 | tf_op jit(solution)/shard_map/fetch_mine/pallas_call | solution.py:640
  8.6 0.0 copy-done
  8.6 0.0 collective-permute-done.refs_3_.near_first.refs_0_
  8.6 0.0 collective-permute-done.1.refs_5_.near_second.refs_1_
  8.6 0.0 collective-permute-done.3.refs_4_.near_second.refs_1_
  8.6 0.2 collective-permute-done.2.refs_2_.near_first.refs_0_
  8.8 2.0 %local_scores.1 = (f32[32,128]{1,0:T(8,128)S(1)}, f32[32,128]{1,0:T(8,128)S(1)}, f32[8,128]{1,0:T(8,128)S(1)}, bf16[2,32,2048]{2,1,0:T(8,128)(2,1)}, bf16[2,32,2...) custom-call(f32[8,128]{1,0:T(8,128)S(1)} %pad.4.table, bf16[4,32,2048]{2,1,0:T(8,128)(2,1)S(1)} %get-tuple-element.39.refs_0_.mine, ...), custom_call_target="tpu_custom_call" | custom-call | flops 1 | bytes 1 | tf_op jit(solution)/shard_map/local_scores/pallas_call | solution.py:640
  10.9 0.0 collective-permute-start.7
  10.9 0.5 %collective-permute-done.5.came = bf16[2,32,2176]{2,1,0:T(8,128)(2,1)S(1)} collective-permute-done((bf16[2,32,2176]{2,1,0:T(8,128)(2,1)S(1)}, bf16[2,32,2176]{2,1,0:T(8,128)(2,1)S(1)}, u32[]{:S(2)}, u32[]{:S(2)}) %collective-permute-start.5) | collective-permute-done | bytes 278560 | tf_op jit(solution)/shard_map/ppermute | solution.py:634
  11.4 0.1 collective-permute-start.6
  11.5 1.8 %collective-permute-start.4 = (bf16[2,32,2048]{2,1,0:T(8,128)(2,1)}, bf16[2,32,2048]{2,1,0:T(8,128)(2,1)S(1)}, u32[]{:S(2)}, u32[]{:S(2)}) collective-permute-start(bf16[2,32,2048]{2,1,0:T(8,128)(2,1)} %get-tuple-element.41), channel_id=1, source_target_pairs={{0,16},{8,24},{16,0},{24,8},{1,17},{9,25},{17,1},{25,9},{2,18},{10... | collective-permute-start | bytes 786440 | tf_op jit(solution)/shard_map/ppermute | solution.py:634
  13.3 0.1 collective-permute-start.8
  13.4 0.0 collective-permute-done.6.refs_0_.refs_3_
  13.4 0.4 %first_dots.1.known = f32[32,128]{1,0:T(8,128)S(1)} custom-call(bf16[4,32,2048]{2,1,0:T(8,128)(2,1)S(1)} %get-tuple-element.39.refs_0_.mine, bf16[2,32,2048]{2,1,0:T(8,128)(2,1)S(1)} %collective-permute-done.2.refs_2_.near_first.refs_0_, bf16[2,32,2048]{2,1,0:T(8,128)(2,1)S(1)} %collective-permute-done.3.refs_4_.near_second.refs_1_, ...), custom_call_target="tpu_custom_call" | custom-call | flops 1 | bytes 1 | tf_op jit(solution)/shard_map/first_dots/pallas_call | solution.py:640
  13.8 6.9 %collective-permute-done.7.refs_2_ = bf16[2,32,2304]{2,1,0:T(8,128)(2,1)S(1)} collective-permute-done((bf16[2,32,2304]{2,1,0:T(8,128)(2,1)S(1)}, bf16[2,32,2304]{2,1,0:T(8,128)(2,1)S(1)}, u32[]{:S(2)}, u32[]{:S(2)}) %collective-permute-start.7) | collective-permute-done | bytes 294944 | tf_op jit(solution)/shard_map/ppermute | solution.py:634
  20.7 1.1 %scores.1 = (bf16[14,32,128]{2,1,0:T(8,128)(2,1)S(1)}, f32[32,8,128]{2,1,0:T(8,128)}, f32[32,128]{1,0:T(8,128)S(1)}) custom-call(f32[32,128]{1,0:T(8,128)S(1)} %first_dots.1.known, f32[8,128]{1,0:T(8,128)S(1)} %pad.4.table, f32[32,128]{1,0:T(8,128)S(1)} %get-tuple-element.43.small, f32[8,128]{1,0:T(8,128)S(1)} %get-tuple-element.44.bias, ...), custom_call_target="tpu_custom_call" | custom-call | flops 1 | bytes 1 | tf_op jit(solution)/shard_map/scores/pallas_call | solution.py:640
  21.9 4.9 %all-to-all-start = ((f32[32,8,128]{2,1,0:T(8,128)}), f32[32,8,128]{2,1,0:T(8,128)S(1)}, u32[]{:S(2)}, u32[]{:S(2)}) async-start(f32[32,8,128]{2,1,0:T(8,128)} %get-tuple-element.51), calls=%async_computation | async-start | bytes 262144 | tf_op jit(solution)/shard_map/all_to_all | solution.py:708
  26.8 1.5 %gradients.1 = (bf16[3,16,2048]{2,1,0:T(8,128)(2,1)S(1)}, bf16[3,16,2048]{2,1,0:T(8,128)(2,1)S(1)}, bf16[128,2048]{1,0:T(8,128)(2,1)}, bf16[128,2048]{1,0:T(8,128)(2,1)}, bf16[128,2048]{1,0:T(8,128)(2,1)}) custom-call(bf16[14,32,128]{2,1,0:T(8,128)(2,1)S(1)} %get-tuple-element.52.items_ref, bf16[4,32,2048]{2,1,0:T(8,128)(2,1)S(1)} %get-tuple-element.39.refs_0_.mine, ...), custom_call_target="tpu_custom_call" | custom-call | flops 1 | bytes 1 | tf_op jit(solution)/shard_map/gradients/pallas_call | solution.py:640
  28.3 0.3 collective-permute-start.12
  28.6 0.3 collective-permute-start.13
  28.9 0.0 collective-permute-done.4.refs_0_.refs_2_
  28.9 0.4 %last_dots.1.known = f32[32,128]{1,0:T(8,128)S(1)} custom-call(bf16[4,32,2048]{2,1,0:T(8,128)(2,1)S(1)} %get-tuple-element.36.refs_1_.mine, bf16[2,32,2048]{2,1,0:T(8,128)(2,1)S(1)} %collective-permute-done.refs_3_.near_first.refs_0_, bf16[2,32,2048]{2,1,0:T(8,128)(2,1)S(1)} %collective-permute-done.1.refs_5_.near_second.refs_1_, ...), custom_call_target="tpu_custom_call" | custom-call | flops 1 | bytes 1 | tf_op jit(solution)/shard_map/last_dots/pallas_call | solution.py:640
  29.3 1.1 %collective-permute-done.8.refs_3_ = bf16[2,32,2048]{2,1,0:T(8,128)(2,1)S(1)} collective-permute-done((bf16[2,32,2048]{2,1,0:T(8,128)(2,1)}, bf16[2,32,2048]{2,1,0:T(8,128)(2,1)S(1)}, u32[]{:S(2)}, u32[]{:S(2)}) %collective-permute-start.8) | collective-permute-done | bytes 262176 | tf_op jit(solution)/shard_map/ppermute | solution.py:634
  30.4 1.4 %scores_and_gradients.1 = (bf16[3,32,2048]{2,1,0:T(8,128)(2,1)S(1)}, bf16[32,2048]{1,0:T(8,128)(2,1)S(1)}, bf16[32,2048]{1,0:T(8,128)(2,1)S(1)}, bf16[32,2048]{1,0:T(8,128)(2,1)S(1)}) custom-call(f32[32,128]{1,0:T(8,128)S(1)} %last_dots.1.known, f32[8,128]{1,0:T(8,128)S(1)} %pad.4.table, f32[32,128]{1,0:T(8,128)S(1)} %get-tuple-element.42.small, ...), custom_call_target="tpu_custom_call" | custom-call | flops 1 | bytes 1 | tf_op jit(solution)/shard_map/scores_and_gradients/pallas_call | solution.py:640
  31.7 1.3 %collective-permute-start.9 = (bf16[32,2048]{1,0:T(8,128)(2,1)S(1)}, bf16[32,2048]{1,0:T(8,128)(2,1)S(1)}, u32[]{:S(2)}, u32[]{:S(2)}) collective-permute-start(bf16[32,2048]{1,0:T(8,128)(2,1)S(1)} %get-tuple-element.48), channel_id=1, source_target_pairs={{0,8},{8,0},{16,24},{24,16},{1,9},{9,1},{17,25},{25,17},{2,10},{10... | collective-permute-start | bytes 393224 | tf_op jit(solution)/shard_map/ppermute | solution.py:634
  33.0 0.1 collective-permute-start.10
  33.1 0.4 %collective-permute-start.11 = (bf16[32,2048]{1,0:T(8,128)(2,1)S(1)}, bf16[32,2048]{1,0:T(8,128)(2,1)S(1)}, u32[]{:S(2)}, u32[]{:S(2)}) collective-permute-start(bf16[32,2048]{1,0:T(8,128)(2,1)S(1)} %get-tuple-element.50), channel_id=1, source_target_pairs={{0,8},{8,0},{16,24},{24,16},{1,9},{9,1},{17,25},{25,17},{2,10},{10... | collective-permute-start | bytes 393224 | tf_op jit(solution)/shard_map/ppermute | solution.py:634
  33.5 0.0 collective-permute-done.12.refs_0_
  33.5 0.0 collective-permute-done.13.refs_1_
  33.5 1.0 %early_outputs.1 = (bf16[128,2048]{1,0:T(8,128)(2,1)}, bf16[128,2048]{1,0:T(8,128)(2,1)}, bf16[128,2048]{1,0:T(8,128)(2,1)}) custom-call(bf16[3,16,2048]{2,1,0:T(8,128)(2,1)S(1)} %collective-permute-done.12.refs_0_, bf16[3,16,2048]{2,1,0:T(8,128)(2,1)S(1)} %collective-permute-done.13.refs_1_, ...), custom_call_target="tpu_custom_call", output_to_operand_aliasing={{0}: (3, {}), {1}: (4, {}), {2}: (5, {})} | custom-call | flops 1 | bytes 1 | tf_op jit(solution)/shard_map/early_outputs/pallas_call | solution.py:640
  34.5 0.0 collective-permute-done.9.refs_0_
  34.5 0.0 collective-permute-done.10.refs_1_
  34.6 0.0 collective-permute-done.11.refs_2_
  34.6 0.0 all-to-all-done.refs_3_
  34.6 0.9 %outputs.1 = (bf16[128,2048]{1,0:T(8,128)(2,1)}, bf16[128,2048]{1,0:T(8,128)(2,1)}, bf16[128,2048]{1,0:T(8,128)(2,1)}, f32[4,16]{1,0:T(4,128)}) custom-call(bf16[32,2048]{1,0:T(8,128)(2,1)S(1)} %collective-permute-done.9.refs_0_, bf16[32,2048]{1,0:T(8,128)(2,1)S(1)} %collective-permute-done.10.refs_1_, ...), custom_call_target="tpu_custom_call", output_to_operand_aliasing={{0}: (4, {}), {1}: (5, {}), {2}: (6, {})} | custom-call | flops 1 | bytes 1 | tf_op jit(solution)/shard_map/outputs/pallas_call | solution.py:640
  (2 shorter events, 0.0 us)
Async XLA Ops:
  1.7 9.7 %collective-permute-start.5 = (bf16[2,32,2176]{2,1,0:T(8,128)(2,1)S(1)}, bf16[2,32,2176]{2,1,0:T(8,128)(2,1)S(1)}, u32[]{:S(2)}, u32[]{:S(2)}) collective-permute-start(bf16[2,32,2176]{2,1,0:T(8,128)(2,1)S(1)} %fetch_other.1.after), channel_id=1, source_target_pairs={{0,16},{8,24},{16,0},{24,8},{1,17},{9,25},{17,1},{25,9},{2,18},{10... | collective-permute-start | bytes 835592 | tf_op jit(solution)/shard_map/ppermute | solution.py:634
  6.1 2.5 %collective-permute-start = (bf16[2,32,2048]{2,1,0:T(8,128)(2,1)S(1)}, bf16[2,32,2048]{2,1,0:T(8,128)(2,1)S(1)}, u32[]{:S(2)}, u32[]{:S(2)}) collective-permute-start(bf16[2,32,2048]{2,1,0:T(8,128)(2,1)S(1)} %get-tuple-element.37), channel_id=1, source_target_pairs={{0,8},{8,0},{16,24},{24,16},{1,9},{9,1},{17,25},{25,17},{2,10},{10... | collective-permute-start | bytes 786440 | tf_op jit(solution)/shard_map/ppermute | solution.py:634
  6.2 2.4 %collective-permute-start.1 = (bf16[2,32,2048]{2,1,0:T(8,128)(2,1)S(1)}, bf16[2,32,2048]{2,1,0:T(8,128)(2,1)S(1)}, u32[]{:S(2)}, u32[]{:S(2)}) collective-permute-start(bf16[2,32,2048]{2,1,0:T(8,128)(2,1)S(1)} %get-tuple-element.38), channel_id=1, source_target_pairs={{0,8},{8,0},{16,24},{24,16},{1,9},{9,1},{17,25},{25,17},{2,10},{10... | collective-permute-start | bytes 786440 | tf_op jit(solution)/shard_map/ppermute | solution.py:634
  6.7 1.9 %collective-permute-start.3 = (bf16[2,32,2048]{2,1,0:T(8,128)(2,1)S(1)}, bf16[2,32,2048]{2,1,0:T(8,128)(2,1)S(1)}, u32[]{:S(2)}, u32[]{:S(2)}) collective-permute-start(bf16[2,32,2048]{2,1,0:T(8,128)(2,1)S(1)} %get-tuple-element.40.refs_7_), channel_id=1, source_target_pairs={{0,8},{8,0},{16,24},{24,16},{1,9},{9,1},{17,25},{25,17},{2,10},{10... | collective-permute-start | bytes 786440 | tf_op jit(solution)/shard_map/ppermute | solution.py:634
  6.8 2.1 %collective-permute-start.2 = (bf16[2,32,2048]{2,1,0:T(8,128)(2,1)S(1)}, bf16[2,32,2048]{2,1,0:T(8,128)(2,1)S(1)}, u32[]{:S(2)}, u32[]{:S(2)}) collective-permute-start(bf16[2,32,2048]{2,1,0:T(8,128)(2,1)S(1)} %get-tuple-element.35.after.refs_6_), channel_id=1, source_target_pairs={{0,8},{8,0},{16,24},{24,16},{1,9},{9,1},{17,25},{25,17},{2,10},{10... | collective-permute-start | bytes 786440 | tf_op jit(solution)/shard_map/ppermute | solution.py:634
  7.2 1.4 %copy-start = (f32[16,4]{0,1:T(4,128)S(1)}, f32[16,4]{0,1:T(4,128)}, u32[]{:S(2)}) copy-start(f32[16,4]{0,1:T(4,128)} %param.9) | copy-start | bytes 772
  10.9 9.9 %collective-permute-start.7 = (bf16[2,32,2304]{2,1,0:T(8,128)(2,1)S(1)}, bf16[2,32,2304]{2,1,0:T(8,128)(2,1)S(1)}, u32[]{:S(2)}, u32[]{:S(2)}) collective-permute-start(bf16[2,32,2304]{2,1,0:T(8,128)(2,1)S(1)} %get-tuple-element.45), channel_id=1, source_target_pairs={{0,16},{8,24},{16,0},{24,8},{1,17},{9,25},{17,1},{25,9},{2,18},{10... | collective-permute-start | bytes 884744 | tf_op jit(solution)/shard_map/ppermute | solution.py:634
  11.4 2.0 %collective-permute-start.6 = (bf16[70,2048]{1,0:T(8,128)(2,1)S(1)}, bf16[70,2048]{1,0:T(8,128)(2,1)S(1)}, u32[]{:S(2)}, u32[]{:S(2)}) collective-permute-start(bf16[70,2048]{1,0:T(8,128)(2,1)S(1)} %forward.1), channel_id=1, source_target_pairs={{0,8},{8,0},{16,24},{24,16},{1,9},{9,1},{17,25},{25,17},{2,10},{10... | collective-permute-start | bytes 860168 | tf_op jit(solution)/shard_map/ppermute | solution.py:634
  11.5 17.4 %collective-permute-start.4 = (bf16[2,32,2048]{2,1,0:T(8,128)(2,1)}, bf16[2,32,2048]{2,1,0:T(8,128)(2,1)S(1)}, u32[]{:S(2)}, u32[]{:S(2)}) collective-permute-start(bf16[2,32,2048]{2,1,0:T(8,128)(2,1)} %get-tuple-element.41), channel_id=1, source_target_pairs={{0,16},{8,24},{16,0},{24,8},{1,17},{9,25},{17,1},{25,9},{2,18},{10... | collective-permute-start | bytes 786440 | tf_op jit(solution)/shard_map/ppermute | solution.py:634
  13.3 17.0 %collective-permute-start.8 = (bf16[2,32,2048]{2,1,0:T(8,128)(2,1)}, bf16[2,32,2048]{2,1,0:T(8,128)(2,1)S(1)}, u32[]{:S(2)}, u32[]{:S(2)}) collective-permute-start(bf16[2,32,2048]{2,1,0:T(8,128)(2,1)} %get-tuple-element.47), channel_id=1, source_target_pairs={{0,24},{8,16},{16,8},{24,0},{1,25},{9,17},{17,9},{25,1},{2,26},{10... | collective-permute-start | bytes 786440 | tf_op jit(solution)/shard_map/ppermute | solution.py:634
  21.9 12.7 %all-to-all-start = ((f32[32,8,128]{2,1,0:T(8,128)}), f32[32,8,128]{2,1,0:T(8,128)S(1)}, u32[]{:S(2)}, u32[]{:S(2)}) async-start(f32[32,8,128]{2,1,0:T(8,128)} %get-tuple-element.51), calls=%async_computation | async-start | bytes 262144 | tf_op jit(solution)/shard_map/all_to_all | solution.py:708
  28.3 5.2 %collective-permute-start.12 = (bf16[3,16,2048]{2,1,0:T(8,128)(2,1)S(1)}, bf16[3,16,2048]{2,1,0:T(8,128)(2,1)S(1)}, u32[]{:S(2)}, u32[]{:S(2)}) collective-permute-start(bf16[3,16,2048]{2,1,0:T(8,128)(2,1)S(1)} %get-tuple-element.53), channel_id=1, source_target_pairs={{0,8},{8,0},{16,24},{24,16},{1,9},{9,1},{17,25},{25,17},{2,10},{10... | collective-permute-start | bytes 589832 | tf_op jit(solution)/shard_map/ppermute | solution.py:634
  28.6 4.9 %collective-permute-start.13 = (bf16[3,16,2048]{2,1,0:T(8,128)(2,1)S(1)}, bf16[3,16,2048]{2,1,0:T(8,128)(2,1)S(1)}, u32[]{:S(2)}, u32[]{:S(2)}) collective-permute-start(bf16[3,16,2048]{2,1,0:T(8,128)(2,1)S(1)} %get-tuple-element.54), channel_id=1, source_target_pairs={{0,8},{8,0},{16,24},{24,16},{1,9},{9,1},{17,25},{25,17},{2,10},{10... | collective-permute-start | bytes 589832 | tf_op jit(solution)/shard_map/ppermute | solution.py:634
  31.7 2.8 %collective-permute-start.9 = (bf16[32,2048]{1,0:T(8,128)(2,1)S(1)}, bf16[32,2048]{1,0:T(8,128)(2,1)S(1)}, u32[]{:S(2)}, u32[]{:S(2)}) collective-permute-start(bf16[32,2048]{1,0:T(8,128)(2,1)S(1)} %get-tuple-element.48), channel_id=1, source_target_pairs={{0,8},{8,0},{16,24},{24,16},{1,9},{9,1},{17,25},{25,17},{2,10},{10... | collective-permute-start | bytes 393224 | tf_op jit(solution)/shard_map/ppermute | solution.py:634
  33.0 1.5 %collective-permute-start.10 = (bf16[32,2048]{1,0:T(8,128)(2,1)S(1)}, bf16[32,2048]{1,0:T(8,128)(2,1)S(1)}, u32[]{:S(2)}, u32[]{:S(2)}) collective-permute-start(bf16[32,2048]{1,0:T(8,128)(2,1)S(1)} %get-tuple-element.49), channel_id=1, source_target_pairs={{0,8},{8,0},{16,24},{24,16},{1,9},{9,1},{17,25},{25,17},{2,10},{10... | collective-permute-start | bytes 393224 | tf_op jit(solution)/shard_map/ppermute | solution.py:634
  33.1 1.5 %collective-permute-start.11 = (bf16[32,2048]{1,0:T(8,128)(2,1)S(1)}, bf16[32,2048]{1,0:T(8,128)(2,1)S(1)}, u32[]{:S(2)}, u32[]{:S(2)}) collective-permute-start(bf16[32,2048]{1,0:T(8,128)(2,1)S(1)} %get-tuple-element.50), channel_id=1, source_target_pairs={{0,8},{8,0},{16,24},{24,16},{1,9},{9,1},{17,25},{25,17},{2,10},{10... | collective-permute-start | bytes 393224 | tf_op jit(solution)/shard_map/ppermute | solution.py:634

commit v10 on v8

--- a/solution.py
+++ b/solution.py
@@ -658,7 +658,7 @@
         known, table, smalls[0], bias, *first,
         scratch=[pltpu.VMEM((8, LANES), wide)],
     )
-    shares = lax.all_to_all(shares, tuple(axis for axis, _ in sizes), 0, 0, tiled=True)
+    shares = lax.all_to_all(shares, tuple(axis for axis, _ in sizes[::-1]), 0, 0, tiled=True)
     *back, grad_queries, grad_keys, grad_values = call(
         functools.partial(gradient_kernel, heads, scale),
         "gradients",

time: 35.2 us -> 35.7 us (1.014)
  waiting for transfers between devices: 8.51 us -> 9 us
    all_to_all x1, waiting for transfers between devices: 0.62 us -> 0.99 us  [by_chips(): lax.all_to_all(shares, tuple((axis for axis, _ in sizes[::-1])), 0, 0, ti...]
where the time goes in v10:
time: 35.7 us; the launch traced here: 35.5 us
  starting transfers between devices  14 us (39%)
  Pallas kernels  11.5 us (32%)
  waiting for transfers between devices  9 us (25%)
  between operations  0.92 us (3%)
    pallas_call x10, Pallas kernels, call(): pl.pallas_call(kernel, in_specs=[any_spec if j in hbm else vmem_spec for...  11.5 us
    ppermute x12, waiting for transfers between devices, swap(): return lax.ppermute(x, 'tm', [(i, i ^ bits) for i in range(4)])  8.02 us
    ppermute x12, starting transfers between devices, swap(): return lax.ppermute(x, 'tm', [(i, i ^ bits) for i in range(4)])  7.7 us
    all_to_all x1, starting transfers between devices, by_chips(): lax.all_to_all(shares, tuple((axis for axis, _ in sizes[::-1])), 0, 0, ti...  6.33 us
    all_to_all x1, waiting for transfers between devices, by_chips(): lax.all_to_all(shares, tuple((axis for axis, _ in sizes[::-1])), 0, 0, ti...  0.99 us
  transfers between devices with their start and end apart: 13, of which 5 were waited for; matrix products, arithmetic and copies ran while one was open for 0% of the time, Pallas kernels for 26%

profile of v10, /device:TPU:0, one launch (start us, length us, event | category | flops | bytes accessed | tf_op | source)
XLA Modules:
  0.0 35.5 jit_solution(14296347341204829023)
XLA Ops:
  0.6 1.4 %fetch_theirs.1 = (bf16[4,32,2048]{2,1,0:T(8,128)(2,1)S(1)}, bf16[4,32,2048]{2,1,0:T(8,128)(2,1)S(1)}, bf16[2,32,2048]{2,1,0:T(8,128)(2,1)S(1)}) custom-call(bf16[128,2048]{1,0:T(8,128)(2,1)} %bitcast.15, bf16[128,2048]{1,0:T(8,128)(2,1)} %bitcast.17, bf16[128,2048]{1,0:T(8,128)(2,1)} %bitcast.19, bf16[128,2048]{1,0:T(8,128)(2,1)} %bitcast.21), custom_call_target="tpu_custom_call" | custom-call | flops 1 | bytes 1 | tf_op jit(solution)/shard_map/fetch_theirs/pallas_call | solution.py:599
  2.0 0.5 %collective-permute-start = (bf16[4,32,2048]{2,1,0:T(8,128)(2,1)S(1)}, bf16[4,32,2048]{2,1,0:T(8,128)(2,1)S(1)}, u32[]{:S(2)}, u32[]{:S(2)}) collective-permute-start(bf16[4,32,2048]{2,1,0:T(8,128)(2,1)S(1)} %get-tuple-element.37), channel_id=1, source_target_pairs={{0,8},{8,0},{16,24},{24,16},{1,9},{9,1},{17,25},{25,17},{2,10},{10... | collective-permute-start | bytes 1572872 | tf_op jit(solution)/shard_map/ppermute | solution.py:593
  2.5 0.1 collective-permute-start.1
  2.6 2.6 %collective-permute-start.3 = (bf16[2,32,2048]{2,1,0:T(8,128)(2,1)S(1)}, bf16[2,32,2048]{2,1,0:T(8,128)(2,1)S(1)}, u32[]{:S(2)}, u32[]{:S(2)}) collective-permute-start(bf16[2,32,2048]{2,1,0:T(8,128)(2,1)S(1)} %get-tuple-element.35.after), channel_id=1, source_target_pairs={{0,24},{8,16},{16,8},{24,0},{1,25},{9,17},{17,9},{25,1},{2,26},{10... | collective-permute-start | bytes 786440 | tf_op jit(solution)/shard_map/ppermute | solution.py:593
  5.3 0.0 copy-start
  5.3 1.4 %fetch_mine.1 = (bf16[4,32,2048]{2,1,0:T(8,128)(2,1)S(1)}, bf16[4,32,2048]{2,1,0:T(8,128)(2,1)S(1)}) custom-call(bf16[128,2048]{1,0:T(8,128)(2,1)} %bitcast.16, bf16[128,2048]{1,0:T(8,128)(2,1)} %bitcast.18, bf16[128,2048]{1,0:T(8,128)(2,1)} %bitcast.20, bf16[128,2048]{1,0:T(8,128)(2,1)} %bitcast.22, bf16[2,32,2048]{2,1,0:T(8,128)(2,1)S(1)} %get-tuple-element.35.after), custom_call_target="tpu_custom_call" | custom-call | flops 1 | bytes 1 | tf_op jit(solution)/shard_map/fetch_mine/pallas_call | solution.py:599
  6.6 0.0 copy-done
  6.6 0.0 collective-permute-done.refs_3_.near
  6.7 0.0 collective-permute-done.1.refs_2_.near
  6.7 2.1 %local_scores.1 = (f32[32,128]{1,0:T(8,128)S(1)}, f32[32,128]{1,0:T(8,128)S(1)}, f32[8,128]{1,0:T(8,128)S(1)}, bf16[2,32,2048]{2,1,0:T(8,128)(2,1)}, bf16[32,230...) custom-call(f32[8,128]{1,0:T(8,128)S(1)} %pad.4.table, ...), custom_call_target="tpu_custom_call" | custom-call | flops 1 | bytes 1 | tf_op jit(solution)/shard_map/local_scores/pallas_call | solution.py:599
  8.7 1.0 %collective-permute-start.4 = (bf16[32,2304]{1,0:T(8,128)(2,1)S(1)}, bf16[32,2304]{1,0:T(8,128)(2,1)S(1)}, u32[]{:S(2)}, u32[]{:S(2)}) collective-permute-start(bf16[32,2304]{1,0:T(8,128)(2,1)S(1)} %get-tuple-element.44), channel_id=1, source_target_pairs={{0,16},{8,24},{16,0},{24,8},{1,17},{9,25},{17,1},{25,9},{2,18},{10... | collective-permute-start | bytes 442376 | tf_op jit(solution)/shard_map/ppermute | solution.py:593
  9.8 1.0 %collective-permute-start.5 = (bf16[32,2304]{1,0:T(8,128)(2,1)S(1)}, bf16[32,2304]{1,0:T(8,128)(2,1)S(1)}, u32[]{:S(2)}, u32[]{:S(2)}) collective-permute-start(bf16[32,2304]{1,0:T(8,128)(2,1)S(1)} %get-tuple-element.45), channel_id=1, source_target_pairs={{0,16},{8,24},{16,0},{24,8},{1,17},{9,25},{17,1},{25,9},{2,18},{10... | collective-permute-start | bytes 442376 | tf_op jit(solution)/shard_map/ppermute | solution.py:593
  10.7 1.0 %collective-permute-start.2 = (bf16[2,32,2048]{2,1,0:T(8,128)(2,1)}, bf16[2,32,2048]{2,1,0:T(8,128)(2,1)S(1)}, u32[]{:S(2)}, u32[]{:S(2)}) collective-permute-start(bf16[2,32,2048]{2,1,0:T(8,128)(2,1)} %get-tuple-element.40), channel_id=1, source_target_pairs={{0,16},{8,24},{16,0},{24,8},{1,17},{9,25},{17,1},{25,9},{2,18},{10... | collective-permute-start | bytes 786440 | tf_op jit(solution)/shard_map/ppermute | solution.py:593
  11.8 0.2 collective-permute-start.6
  12.0 0.0 collective-permute-done.3.refs_0_.refs_2_
  12.0 0.4 %first_dots.1.known = f32[32,128]{1,0:T(8,128)S(1)} custom-call(bf16[4,32,2048]{2,1,0:T(8,128)(2,1)S(1)} %get-tuple-element.38.refs_0_.mine, bf16[4,32,2048]{2,1,0:T(8,128)(2,1)S(1)} %collective-permute-done.1.refs_2_.near, bf16[2,32,2048]{2,1,0:T(8,128)(2,1)S(1)} %collective-permute-done.3.refs_0_.refs_2_), custom_call_target="tpu_custom_call" | custom-call | flops 1 | bytes 1 | tf_op jit(solution)/shard_map/first_dots/pallas_call | solution.py:599
  12.4 3.2 %collective-permute-done.4.refs_0_ = bf16[32,2304]{1,0:T(8,128)(2,1)S(1)} collective-permute-done((bf16[32,2304]{1,0:T(8,128)(2,1)S(1)}, bf16[32,2304]{1,0:T(8,128)(2,1)S(1)}, u32[]{:S(2)}, u32[]{:S(2)}) %collective-permute-start.4) | collective-permute-done | bytes 147488 | tf_op jit(solution)/shard_map/ppermute | solution.py:593
  15.6 3.2 %collective-permute-done.5.refs_1_ = bf16[32,2304]{1,0:T(8,128)(2,1)S(1)} collective-permute-done((bf16[32,2304]{1,0:T(8,128)(2,1)S(1)}, bf16[32,2304]{1,0:T(8,128)(2,1)S(1)}, u32[]{:S(2)}, u32[]{:S(2)}) %collective-permute-start.5) | collective-permute-done | bytes 147488 | tf_op jit(solution)/shard_map/ppermute | solution.py:593
  18.7 1.1 %scores.1 = (bf16[14,32,128]{2,1,0:T(8,128)(2,1)S(1)}, f32[32,8,128]{2,1,0:T(8,128)}, f32[32,128]{1,0:T(8,128)S(1)}) custom-call(f32[32,128]{1,0:T(8,128)S(1)} %first_dots.1.known, f32[8,128]{1,0:T(8,128)S(1)} %pad.4.table, f32[32,128]{1,0:T(8,128)S(1)} %get-tuple-element.42.small, f32[8,128]{1,0:T(8,128)S(1)} %get-tuple-element.43.bias, ...), custom_call_target="tpu_custom_call" | custom-call | flops 1 | bytes 1 | tf_op jit(solution)/shard_map/scores/pallas_call | solution.py:599
  19.9 6.3 %all-to-all-start = ((f32[32,8,128]{2,1,0:T(8,128)}), f32[32,8,128]{2,1,0:T(8,128)S(1)}, u32[]{:S(2)}, u32[]{:S(2)}) async-start(f32[32,8,128]{2,1,0:T(8,128)} %get-tuple-element.51), calls=%async_computation | async-start | bytes 262144 | tf_op jit(solution)/shard_map/all_to_all | solution.py:661
  26.2 1.5 %gradients.1 = (bf16[3,16,2048]{2,1,0:T(8,128)(2,1)S(1)}, bf16[3,16,2048]{2,1,0:T(8,128)(2,1)S(1)}, bf16[128,2048]{1,0:T(8,128)(2,1)}, bf16[128,2048]{1,0:T(8,128)(2,1)}, bf16[128,2048]{1,0:T(8,128)(2,1)}) custom-call(bf16[14,32,128]{2,1,0:T(8,128)(2,1)S(1)} %get-tuple-element.52.items_ref, bf16[4,32,2048]{2,1,0:T(8,128)(2,1)S(1)} %get-tuple-element.38.refs_0_.mine, ...), custom_call_target="tpu_custom_call" | custom-call | flops 1 | bytes 1 | tf_op jit(solution)/shard_map/gradients/pallas_call | solution.py:599
  27.7 0.3 collective-permute-start.10
  28.0 0.3 collective-permute-start.11
  28.3 0.0 collective-permute-done.2.refs_0_
  28.3 0.4 %last_dots.1.known = f32[32,128]{1,0:T(8,128)S(1)} custom-call(bf16[4,32,2048]{2,1,0:T(8,128)(2,1)S(1)} %get-tuple-element.36.refs_1_.mine, bf16[4,32,2048]{2,1,0:T(8,128)(2,1)S(1)} %collective-permute-done.refs_3_.near, bf16[2,32,2048]{2,1,0:T(8,128)(2,1)S(1)} %collective-permute-done.2.refs_0_), custom_call_target="tpu_custom_call" | custom-call | flops 1 | bytes 1 | tf_op jit(solution)/shard_map/last_dots/pallas_call | solution.py:599
  28.7 1.4 %collective-permute-done.6.refs_1_ = bf16[2,32,2048]{2,1,0:T(8,128)(2,1)S(1)} collective-permute-done((bf16[2,32,2048]{2,1,0:T(8,128)(2,1)}, bf16[2,32,2048]{2,1,0:T(8,128)(2,1)S(1)}, u32[]{:S(2)}, u32[]{:S(2)}) %collective-permute-start.6) | collective-permute-done | bytes 262176 | tf_op jit(solution)/shard_map/ppermute | solution.py:593
  30.1 1.4 %scores_and_gradients.1 = (bf16[3,32,2048]{2,1,0:T(8,128)(2,1)S(1)}, bf16[32,2048]{1,0:T(8,128)(2,1)S(1)}, bf16[32,2048]{1,0:T(8,128)(2,1)S(1)}, bf16[32,2048]{1,0:T(8,128)(2,1)S(1)}) custom-call(f32[32,128]{1,0:T(8,128)S(1)} %last_dots.1.known, f32[8,128]{1,0:T(8,128)S(1)} %pad.4.table, f32[32,128]{1,0:T(8,128)S(1)} %get-tuple-element.41.small, ...), custom_call_target="tpu_custom_call" | custom-call | flops 1 | bytes 1 | tf_op jit(solution)/shard_map/scores_and_gradients/pallas_call | solution.py:599
  31.5 0.1 collective-permute-start.7
  31.6 0.5 %collective-permute-start.8 = (bf16[32,2048]{1,0:T(8,128)(2,1)S(1)}, bf16[32,2048]{1,0:T(8,128)(2,1)S(1)}, u32[]{:S(2)}, u32[]{:S(2)}) collective-permute-start(bf16[32,2048]{1,0:T(8,128)(2,1)S(1)} %get-tuple-element.49), channel_id=1, source_target_pairs={{0,8},{8,0},{16,24},{24,16},{1,9},{9,1},{17,25},{25,17},{2,10},{10... | collective-permute-start | bytes 393224 | tf_op jit(solution)/shard_map/ppermute | solution.py:593
  32.1 0.1 collective-permute-start.9
  32.2 0.0 collective-permute-done.10.refs_0_
  32.2 0.0 collective-permute-done.11.refs_1_
  32.2 1.0 %early_outputs.1 = (bf16[128,2048]{1,0:T(8,128)(2,1)}, bf16[128,2048]{1,0:T(8,128)(2,1)}, bf16[128,2048]{1,0:T(8,128)(2,1)}) custom-call(bf16[3,16,2048]{2,1,0:T(8,128)(2,1)S(1)} %collective-permute-done.10.refs_0_, bf16[3,16,2048]{2,1,0:T(8,128)(2,1)S(1)} %collective-permute-done.11.refs_1_, ...), custom_call_target="tpu_custom_call", output_to_operand_aliasing={{0}: (3, {}), {1}: (4, {}), {2}: (5, {})} | custom-call | flops 1 | bytes 1 | tf_op jit(solution)/shard_map/early_outputs/pallas_call | solution.py:599
  33.2 0.0 collective-permute-done.7.refs_0_
  33.2 0.0 collective-permute-done.8.refs_1_
  33.2 0.3 collective-permute-done.9.refs_2_
  33.4 1.0 %all-to-all-done.refs_3_ = f32[32,8,128]{2,1,0:T(8,128)S(1)} async-done(((f32[32,8,128]{2,1,0:T(8,128)}), f32[32,8,128]{2,1,0:T(8,128)S(1)}, u32[]{:S(2)}, u32[]{:S(2)}) %all-to-all-start) | async-done | bytes 131104 | tf_op jit(solution)/shard_map/all_to_all | solution.py:661
  34.4 0.9 %outputs.1 = (bf16[128,2048]{1,0:T(8,128)(2,1)}, bf16[128,2048]{1,0:T(8,128)(2,1)}, bf16[128,2048]{1,0:T(8,128)(2,1)}, f32[4,16]{1,0:T(4,128)}) custom-call(bf16[32,2048]{1,0:T(8,128)(2,1)S(1)} %collective-permute-done.7.refs_0_, bf16[32,2048]{1,0:T(8,128)(2,1)S(1)} %collective-permute-done.8.refs_1_, ...), custom_call_target="tpu_custom_call", output_to_operand_aliasing={{0}: (4, {}), {1}: (5, {}), {2}: (6, {})} | custom-call | flops 1 | bytes 1 | tf_op jit(solution)/shard_map/outputs/pallas_call | solution.py:599
  (1 shorter events, 0.0 us)
Async XLA Ops:
  2.0 4.6 %collective-permute-start = (bf16[4,32,2048]{2,1,0:T(8,128)(2,1)S(1)}, bf16[4,32,2048]{2,1,0:T(8,128)(2,1)S(1)}, u32[]{:S(2)}, u32[]{:S(2)}) collective-permute-start(bf16[4,32,2048]{2,1,0:T(8,128)(2,1)S(1)} %get-tuple-element.37), channel_id=1, source_target_pairs={{0,8},{8,0},{16,24},{24,16},{1,9},{9,1},{17,25},{25,17},{2,10},{10... | collective-permute-start | bytes 1572872 | tf_op jit(solution)/shard_map/ppermute | solution.py:593
  2.5 4.1 %collective-permute-start.1 = (bf16[4,32,2048]{2,1,0:T(8,128)(2,1)S(1)}, bf16[4,32,2048]{2,1,0:T(8,128)(2,1)S(1)}, u32[]{:S(2)}, u32[]{:S(2)}) collective-permute-start(bf16[4,32,2048]{2,1,0:T(8,128)(2,1)S(1)} %get-tuple-element.39.refs_4_), channel_id=1, source_target_pairs={{0,8},{8,0},{16,24},{24,16},{1,9},{9,1},{17,25},{25,17},{2,10},{10... | collective-permute-start | bytes 1572872 | tf_op jit(solution)/shard_map/ppermute | solution.py:593
  2.6 9.4 %collective-permute-start.3 = (bf16[2,32,2048]{2,1,0:T(8,128)(2,1)S(1)}, bf16[2,32,2048]{2,1,0:T(8,128)(2,1)S(1)}, u32[]{:S(2)}, u32[]{:S(2)}) collective-permute-start(bf16[2,32,2048]{2,1,0:T(8,128)(2,1)S(1)} %get-tuple-element.35.after), channel_id=1, source_target_pairs={{0,24},{8,16},{16,8},{24,0},{1,25},{9,17},{17,9},{25,1},{2,26},{10... | collective-permute-start | bytes 786440 | tf_op jit(solution)/shard_map/ppermute | solution.py:593
  5.3 1.4 %copy-start = (f32[16,4]{0,1:T(4,128)S(1)}, f32[16,4]{0,1:T(4,128)}, u32[]{:S(2)}) copy-start(f32[16,4]{0,1:T(4,128)} %param.9) | copy-start | bytes 772
  8.7 6.8 %collective-permute-start.4 = (bf16[32,2304]{1,0:T(8,128)(2,1)S(1)}, bf16[32,2304]{1,0:T(8,128)(2,1)S(1)}, u32[]{:S(2)}, u32[]{:S(2)}) collective-permute-start(bf16[32,2304]{1,0:T(8,128)(2,1)S(1)} %get-tuple-element.44), channel_id=1, source_target_pairs={{0,16},{8,24},{16,0},{24,8},{1,17},{9,25},{17,1},{25,9},{2,18},{10... | collective-permute-start | bytes 442376 | tf_op jit(solution)/shard_map/ppermute | solution.py:593
  9.8 9.0 %collective-permute-start.5 = (bf16[32,2304]{1,0:T(8,128)(2,1)S(1)}, bf16[32,2304]{1,0:T(8,128)(2,1)S(1)}, u32[]{:S(2)}, u32[]{:S(2)}) collective-permute-start(bf16[32,2304]{1,0:T(8,128)(2,1)S(1)} %get-tuple-element.45), channel_id=1, source_target_pairs={{0,16},{8,24},{16,0},{24,8},{1,17},{9,25},{17,1},{25,9},{2,18},{10... | collective-permute-start | bytes 442376 | tf_op jit(solution)/shard_map/ppermute | solution.py:593
  10.7 17.6 %collective-permute-start.2 = (bf16[2,32,2048]{2,1,0:T(8,128)(2,1)}, bf16[2,32,2048]{2,1,0:T(8,128)(2,1)S(1)}, u32[]{:S(2)}, u32[]{:S(2)}) collective-permute-start(bf16[2,32,2048]{2,1,0:T(8,128)(2,1)} %get-tuple-element.40), channel_id=1, source_target_pairs={{0,16},{8,24},{16,0},{24,8},{1,17},{9,25},{17,1},{25,9},{2,18},{10... | collective-permute-start | bytes 786440 | tf_op jit(solution)/shard_map/ppermute | solution.py:593
  11.8 18.3 %collective-permute-start.6 = (bf16[2,32,2048]{2,1,0:T(8,128)(2,1)}, bf16[2,32,2048]{2,1,0:T(8,128)(2,1)S(1)}, u32[]{:S(2)}, u32[]{:S(2)}) collective-permute-start(bf16[2,32,2048]{2,1,0:T(8,128)(2,1)} %get-tuple-element.47), channel_id=1, source_target_pairs={{0,24},{8,16},{16,8},{24,0},{1,25},{9,17},{17,9},{25,1},{2,26},{10... | collective-permute-start | bytes 786440 | tf_op jit(solution)/shard_map/ppermute | solution.py:593
  19.9 14.6 %all-to-all-start = ((f32[32,8,128]{2,1,0:T(8,128)}), f32[32,8,128]{2,1,0:T(8,128)S(1)}, u32[]{:S(2)}, u32[]{:S(2)}) async-start(f32[32,8,128]{2,1,0:T(8,128)} %get-tuple-element.51), calls=%async_computation | async-start | bytes 262144 | tf_op jit(solution)/shard_map/all_to_all | solution.py:661
  27.7 4.4 %collective-permute-start.10 = (bf16[3,16,2048]{2,1,0:T(8,128)(2,1)S(1)}, bf16[3,16,2048]{2,1,0:T(8,128)(2,1)S(1)}, u32[]{:S(2)}, u32[]{:S(2)}) collective-permute-start(bf16[3,16,2048]{2,1,0:T(8,128)(2,1)S(1)} %get-tuple-element.53), channel_id=1, source_target_pairs={{0,8},{8,0},{16,24},{24,16},{1,9},{9,1},{17,25},{25,17},{2,10},{10... | collective-permute-start | bytes 589832 | tf_op jit(solution)/shard_map/ppermute | solution.py:593
  28.0 4.1 %collective-permute-start.11 = (bf16[3,16,2048]{2,1,0:T(8,128)(2,1)S(1)}, bf16[3,16,2048]{2,1,0:T(8,128)(2,1)S(1)}, u32[]{:S(2)}, u32[]{:S(2)}) collective-permute-start(bf16[3,16,2048]{2,1,0:T(8,128)(2,1)S(1)} %get-tuple-element.54), channel_id=1, source_target_pairs={{0,8},{8,0},{16,24},{24,16},{1,9},{9,1},{17,25},{25,17},{2,10},{10... | collective-permute-start | bytes 589832 | tf_op jit(solution)/shard_map/ppermute | solution.py:593
  31.5 1.7 %collective-permute-start.7 = (bf16[32,2048]{1,0:T(8,128)(2,1)S(1)}, bf16[32,2048]{1,0:T(8,128)(2,1)S(1)}, u32[]{:S(2)}, u32[]{:S(2)}) collective-permute-start(bf16[32,2048]{1,0:T(8,128)(2,1)S(1)} %get-tuple-element.48), channel_id=1, source_target_pairs={{0,8},{8,0},{16,24},{24,16},{1,9},{9,1},{17,25},{25,17},{2,10},{10... | collective-permute-start | bytes 393224 | tf_op jit(solution)/shard_map/ppermute | solution.py:593
  31.6 1.6 %collective-permute-start.8 = (bf16[32,2048]{1,0:T(8,128)(2,1)S(1)}, bf16[32,2048]{1,0:T(8,128)(2,1)S(1)}, u32[]{:S(2)}, u32[]{:S(2)}) collective-permute-start(bf16[32,2048]{1,0:T(8,128)(2,1)S(1)} %get-tuple-element.49), channel_id=1, source_target_pairs={{0,8},{8,0},{16,24},{24,16},{1,9},{9,1},{17,25},{25,17},{2,10},{10... | collective-permute-start | bytes 393224 | tf_op jit(solution)/shard_map/ppermute | solution.py:593
  32.1 1.3 %collective-permute-start.9 = (bf16[32,2048]{1,0:T(8,128)(2,1)S(1)}, bf16[32,2048]{1,0:T(8,128)(2,1)S(1)}, u32[]{:S(2)}, u32[]{:S(2)}) collective-permute-start(bf16[32,2048]{1,0:T(8,128)(2,1)S(1)} %get-tuple-element.50), channel_id=1, source_target_pairs={{0,8},{8,0},{16,24},{24,16},{1,9},{9,1},{17,25},{25,17},{2,10},{10... | collective-permute-start | bytes 393224 | tf_op jit(solution)/shard_map/ppermute | solution.py:593

commit v11 on v8

--- a/solution.py
+++ b/solution.py
@@ -277,8 +277,7 @@
 
 
 def local_kernel(heads, scale, table, *refs):
-    mines, nears, theirs, refs = refs[:2], refs[2:4], refs[4], refs[5:]
-    smalls, out_bias, other, sames = refs[:2], refs[2], refs[3], (refs[4:6], planes(refs[6]))
+    mines, nears, smalls, out_bias, same = refs[:2], refs[2:4], refs[4:6], refs[6], refs[7:]
     core, chip = my_place()
     size, width = mines[0].shape[1:]
     offset = [table[d : d + 1, :] for d in range(4)]
@@ -305,14 +304,18 @@
         pl.when(core == 0)(functools.partial(run, own, neighbour, small))
         pl.when(core == 1)(functools.partial(run, neighbour, own, small))
 
-    take_far(planes(theirs), planes(other))
-    for c, out in enumerate(sames):
-        take_far(planes(mines[1 - c]), out)
+    take_far(planes(mines[1]), same)
+    for c in range(CHUNKS):
         for row in range(0, size, TILE):
             rows = slice(row, row + TILE)
             parts = packed_small(smalls[1 - c][rows, :], heads)
-            for ref, part in zip(sames[0], parts):
+            for ref, part in zip(same, parts):
                 ref[rows, width + c * LANES : width + (c + 1) * LANES] = part
+
+
+def pack_kernel(after, mine, theirs, same, other):
+    take_far(planes(mine), planes(same))
+    take_far(planes(theirs), planes(other))
 
 
 EARLY, LATE = 14, 10
@@ -625,17 +628,15 @@
         scratch=copies, hbm=range(5),
     )
 
-    *smalls, bias, other, same_first, same_second, same = call(
+    *smalls, bias, same_first, same_second = call(
         functools.partial(local_kernel, heads, scale),
         "local_scores",
         [shape(size, LANES, dtype=wide)] * CHUNKS
-        + [lines, far_shape]
-        + [shape(size, width + CHUNKS * LANES)] * 2
-        + [far_shape],
-        table, *mines, *nears, theirs[0],
-    )
-    sames = [[swap(same_first, 2), swap(same_second, 2)], [swap(same, 2)]]
-    others.append(swap(other, 3))
+        + [lines]
+        + [shape(size, width + CHUNKS * LANES)] * 2,
+        table, *mines, *nears,
+    )
+    sames = [[swap(same_first, 2), swap(same_second, 2)]]
 
     whole = pltpu.HBM((rows, width), jnp.bfloat16)
     stack, piece = shape(3, size, width), shape(size, width)
@@ -647,6 +648,9 @@
         [shape(size, LANES, dtype=wide)],
         mines[0], nears[0], others[0],
     )
+    same, other = call(pack_kernel, "pack", [far_shape] * 2, known, mines[0], theirs[0])
+    sames.append([swap(same, 2)])
+    others.append(swap(other, 3))
     items, shares, small_far = call(
         functools.partial(score_kernel, heads, scale),
         "scores",

time: 35.2 us -> 35.2 us (level)
  starting transfers between devices: 14 us -> 14.6 us
  waiting for transfers between devices: 8.51 us -> 7.94 us
    ppermute x12, starting transfers between devices: 7.7 us -> 8.5 us  [swap(): return lax.ppermute(x, 'tm', [(i, i ^ bits) for i in range(4)])]
    ppermute x12, waiting for transfers between devices: 7.89 us -> 7.31 us  [swap(): return lax.ppermute(x, 'tm', [(i, i ^ bits) for i in range(4)])]
    pallas_call x10 -> x11, Pallas kernels: 11.5 us -> 11.5 us  [call(): pl.pallas_call(kernel, in_specs=[any_spec if j in hbm else vmem_spec for...]
  transfers between devices with their start and end apart: 13 -> 13, of which waited for: 5 -> 6; matrix products, arithmetic and copies ran while one was open for 0% -> 0% of each run, Pallas kernels for 26% -> 26%
where the time goes in v11:
time: 35.2 us; the launch traced here: 35 us
  starting transfers between devices  14.6 us (41%)
  Pallas kernels  11.5 us (33%)
  waiting for transfers between devices  7.94 us (23%)
  between operations  0.93 us (3%)
    pallas_call x11, Pallas kernels, call(): pl.pallas_call(kernel, in_specs=[any_spec if j in hbm else vmem_spec for...  11.5 us
    ppermute x12, starting transfers between devices, swap(): return lax.ppermute(x, 'tm', [(i, i ^ bits) for i in range(4)])  8.5 us
    ppermute x12, waiting for transfers between devices, swap(): return lax.ppermute(x, 'tm', [(i, i ^ bits) for i in range(4)])  7.31 us
    all_to_all x1, starting transfers between devices, by_chips(): lax.all_to_all(shares, tuple((axis for axis, _ in sizes)), 0, 0, tiled=True)  6.07 us
  transfers between devices with their start and end apart: 13, of which 6 were waited for; matrix products, arithmetic and copies ran while one was open for 0% of the time, Pallas kernels for 26%

profile of v11, /device:TPU:0, one launch (start us, length us, event | category | flops | bytes accessed | tf_op | source)
XLA Modules:
  0.0 35.0 jit_solution(12413735408585992828)
XLA Ops:
  0.6 1.4 %fetch_theirs.1 = (bf16[4,32,2048]{2,1,0:T(8,128)(2,1)S(1)}, bf16[4,32,2048]{2,1,0:T(8,128)(2,1)S(1)}, bf16[2,32,2048]{2,1,0:T(8,128)(2,1)S(1)}) custom-call(bf16[128,2048]{1,0:T(8,128)(2,1)} %bitcast.15, bf16[128,2048]{1,0:T(8,128)(2,1)} %bitcast.17, bf16[128,2048]{1,0:T(8,128)(2,1)} %bitcast.19, bf16[128,2048]{1,0:T(8,128)(2,1)} %bitcast.21), custom_call_target="tpu_custom_call" | custom-call | flops 1 | bytes 1 | tf_op jit(solution)/shard_map/fetch_theirs/pallas_call | solution.py:602
  2.0 0.5 %collective-permute-start = (bf16[4,32,2048]{2,1,0:T(8,128)(2,1)S(1)}, bf16[4,32,2048]{2,1,0:T(8,128)(2,1)S(1)}, u32[]{:S(2)}, u32[]{:S(2)}) collective-permute-start(bf16[4,32,2048]{2,1,0:T(8,128)(2,1)S(1)} %get-tuple-element.37), channel_id=1, source_target_pairs={{0,8},{8,0},{16,24},{24,16},{1,9},{9,1},{17,25},{25,17},{2,10},{10... | collective-permute-start | bytes 1572872 | tf_op jit(solution)/shard_map/ppermute | solution.py:596
  2.5 0.1 collective-permute-start.1
  2.6 2.6 %collective-permute-start.2 = (bf16[2,32,2048]{2,1,0:T(8,128)(2,1)S(1)}, bf16[2,32,2048]{2,1,0:T(8,128)(2,1)S(1)}, u32[]{:S(2)}, u32[]{:S(2)}) collective-permute-start(bf16[2,32,2048]{2,1,0:T(8,128)(2,1)S(1)} %get-tuple-element.35.after), channel_id=1, source_target_pairs={{0,24},{8,16},{16,8},{24,0},{1,25},{9,17},{17,9},{25,1},{2,26},{10... | collective-permute-start | bytes 786440 | tf_op jit(solution)/shard_map/ppermute | solution.py:596
  5.3 0.0 copy-start
  5.3 1.4 %fetch_mine.1 = (bf16[4,32,2048]{2,1,0:T(8,128)(2,1)S(1)}, bf16[4,32,2048]{2,1,0:T(8,128)(2,1)S(1)}) custom-call(bf16[128,2048]{1,0:T(8,128)(2,1)} %bitcast.16, bf16[128,2048]{1,0:T(8,128)(2,1)} %bitcast.18, bf16[128,2048]{1,0:T(8,128)(2,1)} %bitcast.20, bf16[128,2048]{1,0:T(8,128)(2,1)} %bitcast.22, bf16[2,32,2048]{2,1,0:T(8,128)(2,1)S(1)} %get-tuple-element.35.after), custom_call_target="tpu_custom_call" | custom-call | flops 1 | bytes 1 | tf_op jit(solution)/shard_map/fetch_mine/pallas_call | solution.py:602
  6.6 0.0 copy-done
  6.6 0.0 collective-permute-done.near.refs_3_
  6.7 0.0 collective-permute-done.1.near.refs_2_
  6.7 1.2 %local_scores.1 = (f32[32,128]{1,0:T(8,128)S(1)}, f32[32,128]{1,0:T(8,128)S(1)}, f32[8,128]{1,0:T(8,128)S(1)}, bf16[32,2304]{1,0:T(8,128)(2,1)S(1)}, bf16[32,2304]{1,0:T(8,128)(2,1)S(1)}) custom-call(f32[8,128]{1,0:T(8,128)S(1)} %pad.4.table, bf16[4,32,2048]{2,1,0:T(8,128)(2,1)S(1)} %get-tuple-element.38.mine.refs_0_, ...), custom_call_target="tpu_custom_call" | custom-call | flops 1 | bytes 1 | tf_op jit(solution)/shard_map/local_scores/pallas_call | solution.py:602
  7.9 1.1 %collective-permute-start.4 = (bf16[32,2304]{1,0:T(8,128)(2,1)S(1)}, bf16[32,2304]{1,0:T(8,128)(2,1)S(1)}, u32[]{:S(2)}, u32[]{:S(2)}) collective-permute-start(bf16[32,2304]{1,0:T(8,128)(2,1)S(1)} %get-tuple-element.44), channel_id=1, source_target_pairs={{0,16},{8,24},{16,0},{24,8},{1,17},{9,25},{17,1},{25,9},{2,18},{10... | collective-permute-start | bytes 442376 | tf_op jit(solution)/shard_map/ppermute | solution.py:596
  9.0 1.0 %collective-permute-start.5 = (bf16[32,2304]{1,0:T(8,128)(2,1)S(1)}, bf16[32,2304]{1,0:T(8,128)(2,1)S(1)}, u32[]{:S(2)}, u32[]{:S(2)}) collective-permute-start(bf16[32,2304]{1,0:T(8,128)(2,1)S(1)} %get-tuple-element.45), channel_id=1, source_target_pairs={{0,16},{8,24},{16,0},{24,8},{1,17},{9,25},{17,1},{25,9},{2,18},{10... | collective-permute-start | bytes 442376 | tf_op jit(solution)/shard_map/ppermute | solution.py:596
  10.0 2.0 %collective-permute-done.2.refs_0_.refs_2_ = bf16[2,32,2048]{2,1,0:T(8,128)(2,1)S(1)} collective-permute-done((bf16[2,32,2048]{2,1,0:T(8,128)(2,1)S(1)}, bf16[2,32,2048]{2,1,0:T(8,128)(2,1)S(1)}, u32[]{:S(2)}, u32[]{:S(2)}) %collective-permute-start.2) | collective-permute-done | bytes 262176 | tf_op jit(solution)/shard_map/ppermute | solution.py:596
  12.0 0.4 %first_dots.1.after.known = f32[32,128]{1,0:T(8,128)S(1)} custom-call(bf16[4,32,2048]{2,1,0:T(8,128)(2,1)S(1)} %get-tuple-element.38.mine.refs_0_, bf16[4,32,2048]{2,1,0:T(8,128)(2,1)S(1)} %collective-permute-done.1.near.refs_2_, bf16[2,32,2048]{2,1,0:T(8,128)(2,1)S(1)} %collective-permute-done.2.refs_0_.refs_2_), custom_call_target="tpu_custom_call" | custom-call | flops 1 | bytes 1 | tf_op jit(solution)/shard_map/first_dots/pallas_call | solution.py:602
  12.4 0.9 %pack.1 = (bf16[2,32,2048]{2,1,0:T(8,128)(2,1)}, bf16[2,32,2048]{2,1,0:T(8,128)(2,1)}) custom-call(f32[32,128]{1,0:T(8,128)S(1)} %first_dots.1.after.known, bf16[4,32,2048]{2,1,0:T(8,128)(2,1)S(1)} %get-tuple-element.38.mine.refs_0_, bf16[4,32,2048]{2,1,0:T(8,128)(2,1)S(1)} %get-tuple-element.39.theirs), custom_call_target="tpu_custom_call" | custom-call | flops 1 | bytes 1 | tf_op jit(solution)/shard_map/pack/pallas_call | solution.py:602
  13.2 2.0 %collective-permute-start.3 = (bf16[2,32,2048]{2,1,0:T(8,128)(2,1)}, bf16[2,32,2048]{2,1,0:T(8,128)(2,1)S(1)}, u32[]{:S(2)}, u32[]{:S(2)}) collective-permute-start(bf16[2,32,2048]{2,1,0:T(8,128)(2,1)} %get-tuple-element.40), channel_id=1, source_target_pairs={{0,16},{8,24},{16,0},{24,8},{1,17},{9,25},{17,1},{25,9},{2,18},{10... | collective-permute-start | bytes 786440 | tf_op jit(solution)/shard_map/ppermute | solution.py:596
  15.2 0.0 collective-permute-start.6
  15.2 0.6 %collective-permute-done.4.refs_0_ = bf16[32,2304]{1,0:T(8,128)(2,1)S(1)} collective-permute-done((bf16[32,2304]{1,0:T(8,128)(2,1)S(1)}, bf16[32,2304]{1,0:T(8,128)(2,1)S(1)}, u32[]{:S(2)}, u32[]{:S(2)}) %collective-permute-start.4) | collective-permute-done | bytes 147488 | tf_op jit(solution)/shard_map/ppermute | solution.py:596
  15.8 3.2 %collective-permute-done.5.refs_1_ = bf16[32,2304]{1,0:T(8,128)(2,1)S(1)} collective-permute-done((bf16[32,2304]{1,0:T(8,128)(2,1)S(1)}, bf16[32,2304]{1,0:T(8,128)(2,1)S(1)}, u32[]{:S(2)}, u32[]{:S(2)}) %collective-permute-start.5) | collective-permute-done | bytes 147488 | tf_op jit(solution)/shard_map/ppermute | solution.py:596
  19.0 1.1 %scores.1 = (bf16[14,32,128]{2,1,0:T(8,128)(2,1)S(1)}, f32[32,8,128]{2,1,0:T(8,128)}, f32[32,128]{1,0:T(8,128)S(1)}) custom-call(f32[32,128]{1,0:T(8,128)S(1)} %first_dots.1.after.known, f32[8,128]{1,0:T(8,128)S(1)} %pad.4.table, f32[32,128]{1,0:T(8,128)S(1)} %get-tuple-element.42.small, f32[8,128]{1,0:T(8,128)S(1)} %get-tuple-element.43.bias, ...), custom_call_target="tpu_custom_call" | custom-call | flops 1 | bytes 1 | tf_op jit(solution)/shard_map/scores/pallas_call | solution.py:602
  20.1 6.1 %all-to-all-start = ((f32[32,8,128]{2,1,0:T(8,128)}), f32[32,8,128]{2,1,0:T(8,128)S(1)}, u32[]{:S(2)}, u32[]{:S(2)}) async-start(f32[32,8,128]{2,1,0:T(8,128)} %get-tuple-element.51), calls=%async_computation | async-start | bytes 262144 | tf_op jit(solution)/shard_map/all_to_all | solution.py:665
  26.2 1.5 %gradients.1 = (bf16[3,16,2048]{2,1,0:T(8,128)(2,1)S(1)}, bf16[3,16,2048]{2,1,0:T(8,128)(2,1)S(1)}, bf16[128,2048]{1,0:T(8,128)(2,1)}, bf16[128,2048]{1,0:T(8,128)(2,1)}, bf16[128,2048]{1,0:T(8,128)(2,1)}) custom-call(bf16[14,32,128]{2,1,0:T(8,128)(2,1)S(1)} %get-tuple-element.52.items_ref, bf16[4,32,2048]{2,1,0:T(8,128)(2,1)S(1)} %get-tuple-element.38.mine.refs_0_, ...), custom_call_target="tpu_custom_call" | custom-call | flops 1 | bytes 1 | tf_op jit(solution)/shard_map/gradients/pallas_call | solution.py:602
  27.7 0.3 collective-permute-start.10
  28.1 0.3 collective-permute-start.11
  28.3 0.0 collective-permute-done.3.refs_0_
  28.3 0.4 %last_dots.1.known = f32[32,128]{1,0:T(8,128)S(1)} custom-call(bf16[4,32,2048]{2,1,0:T(8,128)(2,1)S(1)} %get-tuple-element.36.mine.refs_1_, bf16[4,32,2048]{2,1,0:T(8,128)(2,1)S(1)} %collective-permute-done.near.refs_3_, bf16[2,32,2048]{2,1,0:T(8,128)(2,1)S(1)} %collective-permute-done.3.refs_0_), custom_call_target="tpu_custom_call" | custom-call | flops 1 | bytes 1 | tf_op jit(solution)/shard_map/last_dots/pallas_call | solution.py:602
  28.7 1.3 %collective-permute-done.6.refs_1_ = bf16[2,32,2048]{2,1,0:T(8,128)(2,1)S(1)} collective-permute-done((bf16[2,32,2048]{2,1,0:T(8,128)(2,1)}, bf16[2,32,2048]{2,1,0:T(8,128)(2,1)S(1)}, u32[]{:S(2)}, u32[]{:S(2)}) %collective-permute-start.6) | collective-permute-done | bytes 262176 | tf_op jit(solution)/shard_map/ppermute | solution.py:596
  30.0 1.4 %scores_and_gradients.1 = (bf16[3,32,2048]{2,1,0:T(8,128)(2,1)S(1)}, bf16[32,2048]{1,0:T(8,128)(2,1)S(1)}, bf16[32,2048]{1,0:T(8,128)(2,1)S(1)}, bf16[32,2048]{1,0:T(8,128)(2,1)S(1)}) custom-call(f32[32,128]{1,0:T(8,128)S(1)} %last_dots.1.known, f32[8,128]{1,0:T(8,128)S(1)} %pad.4.table, f32[32,128]{1,0:T(8,128)S(1)} %get-tuple-element.41.small, ...), custom_call_target="tpu_custom_call" | custom-call | flops 1 | bytes 1 | tf_op jit(solution)/shard_map/scores_and_gradients/pallas_call | solution.py:602
  31.4 0.1 collective-permute-start.7
  31.5 0.5 %collective-permute-start.8 = (bf16[32,2048]{1,0:T(8,128)(2,1)S(1)}, bf16[32,2048]{1,0:T(8,128)(2,1)S(1)}, u32[]{:S(2)}, u32[]{:S(2)}) collective-permute-start(bf16[32,2048]{1,0:T(8,128)(2,1)S(1)} %get-tuple-element.49), channel_id=1, source_target_pairs={{0,8},{8,0},{16,24},{24,16},{1,9},{9,1},{17,25},{25,17},{2,10},{10... | collective-permute-start | bytes 393224 | tf_op jit(solution)/shard_map/ppermute | solution.py:596
  32.0 0.1 collective-permute-start.9
  32.0 0.0 collective-permute-done.10.refs_0_
  32.0 0.0 collective-permute-done.11.refs_1_
  32.0 1.0 %early_outputs.1 = (bf16[128,2048]{1,0:T(8,128)(2,1)}, bf16[128,2048]{1,0:T(8,128)(2,1)}, bf16[128,2048]{1,0:T(8,128)(2,1)}) custom-call(bf16[3,16,2048]{2,1,0:T(8,128)(2,1)S(1)} %collective-permute-done.10.refs_0_, bf16[3,16,2048]{2,1,0:T(8,128)(2,1)S(1)} %collective-permute-done.11.refs_1_, ...), custom_call_target="tpu_custom_call", output_to_operand_aliasing={{0}: (3, {}), {1}: (4, {}), {2}: (5, {})} | custom-call | flops 1 | bytes 1 | tf_op jit(solution)/shard_map/early_outputs/pallas_call | solution.py:602
  33.0 0.0 collective-permute-done.7.refs_0_
  33.0 0.0 collective-permute-done.8.refs_1_
  33.1 0.3 collective-permute-done.9.refs_2_
  33.3 0.6 %all-to-all-done.refs_3_ = f32[32,8,128]{2,1,0:T(8,128)S(1)} async-done(((f32[32,8,128]{2,1,0:T(8,128)}), f32[32,8,128]{2,1,0:T(8,128)S(1)}, u32[]{:S(2)}, u32[]{:S(2)}) %all-to-all-start) | async-done | bytes 131104 | tf_op jit(solution)/shard_map/all_to_all | solution.py:665
  33.9 0.9 %outputs.1 = (bf16[128,2048]{1,0:T(8,128)(2,1)}, bf16[128,2048]{1,0:T(8,128)(2,1)}, bf16[128,2048]{1,0:T(8,128)(2,1)}, f32[4,16]{1,0:T(4,128)}) custom-call(bf16[32,2048]{1,0:T(8,128)(2,1)S(1)} %collective-permute-done.7.refs_0_, bf16[32,2048]{1,0:T(8,128)(2,1)S(1)} %collective-permute-done.8.refs_1_, ...), custom_call_target="tpu_custom_call", output_to_operand_aliasing={{0}: (4, {}), {1}: (5, {}), {2}: (6, {})} | custom-call | flops 1 | bytes 1 | tf_op jit(solution)/shard_map/outputs/pallas_call | solution.py:602
  (1 shorter events, 0.0 us)
Async XLA Ops:
  2.0 4.6 %collective-permute-start = (bf16[4,32,2048]{2,1,0:T(8,128)(2,1)S(1)}, bf16[4,32,2048]{2,1,0:T(8,128)(2,1)S(1)}, u32[]{:S(2)}, u32[]{:S(2)}) collective-permute-start(bf16[4,32,2048]{2,1,0:T(8,128)(2,1)S(1)} %get-tuple-element.37), channel_id=1, source_target_pairs={{0,8},{8,0},{16,24},{24,16},{1,9},{9,1},{17,25},{25,17},{2,10},{10... | collective-permute-start | bytes 1572872 | tf_op jit(solution)/shard_map/ppermute | solution.py:596
  2.5 4.1 %collective-permute-start.1 = (bf16[4,32,2048]{2,1,0:T(8,128)(2,1)S(1)}, bf16[4,32,2048]{2,1,0:T(8,128)(2,1)S(1)}, u32[]{:S(2)}, u32[]{:S(2)}) collective-permute-start(bf16[4,32,2048]{2,1,0:T(8,128)(2,1)S(1)} %get-tuple-element.39.theirs), channel_id=1, source_target_pairs={{0,8},{8,0},{16,24},{24,16},{1,9},{9,1},{17,25},{25,17},{2,10},{10... | collective-permute-start | bytes 1572872 | tf_op jit(solution)/shard_map/ppermute | solution.py:596
  2.6 9.3 %collective-permute-start.2 = (bf16[2,32,2048]{2,1,0:T(8,128)(2,1)S(1)}, bf16[2,32,2048]{2,1,0:T(8,128)(2,1)S(1)}, u32[]{:S(2)}, u32[]{:S(2)}) collective-permute-start(bf16[2,32,2048]{2,1,0:T(8,128)(2,1)S(1)} %get-tuple-element.35.after), channel_id=1, source_target_pairs={{0,24},{8,16},{16,8},{24,0},{1,25},{9,17},{17,9},{25,1},{2,26},{10... | collective-permute-start | bytes 786440 | tf_op jit(solution)/shard_map/ppermute | solution.py:596
  5.3 1.4 %copy-start = (f32[16,4]{0,1:T(4,128)S(1)}, f32[16,4]{0,1:T(4,128)}, u32[]{:S(2)}) copy-start(f32[16,4]{0,1:T(4,128)} %param.9) | copy-start | bytes 772
  7.9 7.9 %collective-permute-start.4 = (bf16[32,2304]{1,0:T(8,128)(2,1)S(1)}, bf16[32,2304]{1,0:T(8,128)(2,1)S(1)}, u32[]{:S(2)}, u32[]{:S(2)}) collective-permute-start(bf16[32,2304]{1,0:T(8,128)(2,1)S(1)} %get-tuple-element.44), channel_id=1, source_target_pairs={{0,16},{8,24},{16,0},{24,8},{1,17},{9,25},{17,1},{25,9},{2,18},{10... | collective-permute-start | bytes 442376 | tf_op jit(solution)/shard_map/ppermute | solution.py:596
  9.0 10.0 %collective-permute-start.5 = (bf16[32,2304]{1,0:T(8,128)(2,1)S(1)}, bf16[32,2304]{1,0:T(8,128)(2,1)S(1)}, u32[]{:S(2)}, u32[]{:S(2)}) collective-permute-start(bf16[32,2304]{1,0:T(8,128)(2,1)S(1)} %get-tuple-element.45), channel_id=1, source_target_pairs={{0,16},{8,24},{16,0},{24,8},{1,17},{9,25},{17,1},{25,9},{2,18},{10... | collective-permute-start | bytes 442376 | tf_op jit(solution)/shard_map/ppermute | solution.py:596
  13.2 15.1 %collective-permute-start.3 = (bf16[2,32,2048]{2,1,0:T(8,128)(2,1)}, bf16[2,32,2048]{2,1,0:T(8,128)(2,1)S(1)}, u32[]{:S(2)}, u32[]{:S(2)}) collective-permute-start(bf16[2,32,2048]{2,1,0:T(8,128)(2,1)} %get-tuple-element.40), channel_id=1, source_target_pairs={{0,16},{8,24},{16,0},{24,8},{1,17},{9,25},{17,1},{25,9},{2,18},{10... | collective-permute-start | bytes 786440 | tf_op jit(solution)/shard_map/ppermute | solution.py:596
  15.2 14.8 %collective-permute-start.6 = (bf16[2,32,2048]{2,1,0:T(8,128)(2,1)}, bf16[2,32,2048]{2,1,0:T(8,128)(2,1)S(1)}, u32[]{:S(2)}, u32[]{:S(2)}) collective-permute-start(bf16[2,32,2048]{2,1,0:T(8,128)(2,1)} %get-tuple-element.47), channel_id=1, source_target_pairs={{0,24},{8,16},{16,8},{24,0},{1,25},{9,17},{17,9},{25,1},{2,26},{10... | collective-permute-start | bytes 786440 | tf_op jit(solution)/shard_map/ppermute | solution.py:596
  20.1 13.8 %all-to-all-start = ((f32[32,8,128]{2,1,0:T(8,128)}), f32[32,8,128]{2,1,0:T(8,128)S(1)}, u32[]{:S(2)}, u32[]{:S(2)}) async-start(f32[32,8,128]{2,1,0:T(8,128)} %get-tuple-element.51), calls=%async_computation | async-start | bytes 262144 | tf_op jit(solution)/shard_map/all_to_all | solution.py:665
  27.7 4.3 %collective-permute-start.10 = (bf16[3,16,2048]{2,1,0:T(8,128)(2,1)S(1)}, bf16[3,16,2048]{2,1,0:T(8,128)(2,1)S(1)}, u32[]{:S(2)}, u32[]{:S(2)}) collective-permute-start(bf16[3,16,2048]{2,1,0:T(8,128)(2,1)S(1)} %get-tuple-element.53), channel_id=1, source_target_pairs={{0,8},{8,0},{16,24},{24,16},{1,9},{9,1},{17,25},{25,17},{2,10},{10... | collective-permute-start | bytes 589832 | tf_op jit(solution)/shard_map/ppermute | solution.py:596
  28.1 4.0 %collective-permute-start.11 = (bf16[3,16,2048]{2,1,0:T(8,128)(2,1)S(1)}, bf16[3,16,2048]{2,1,0:T(8,128)(2,1)S(1)}, u32[]{:S(2)}, u32[]{:S(2)}) collective-permute-start(bf16[3,16,2048]{2,1,0:T(8,128)(2,1)S(1)} %get-tuple-element.54), channel_id=1, source_target_pairs={{0,8},{8,0},{16,24},{24,16},{1,9},{9,1},{17,25},{25,17},{2,10},{10... | collective-permute-start | bytes 589832 | tf_op jit(solution)/shard_map/ppermute | solution.py:596
  31.4 1.7 %collective-permute-start.7 = (bf16[32,2048]{1,0:T(8,128)(2,1)S(1)}, bf16[32,2048]{1,0:T(8,128)(2,1)S(1)}, u32[]{:S(2)}, u32[]{:S(2)}) collective-permute-start(bf16[32,2048]{1,0:T(8,128)(2,1)S(1)} %get-tuple-element.48), channel_id=1, source_target_pairs={{0,8},{8,0},{16,24},{24,16},{1,9},{9,1},{17,25},{25,17},{2,10},{10... | collective-permute-start | bytes 393224 | tf_op jit(solution)/shard_map/ppermute | solution.py:596
  31.5 1.6 %collective-permute-start.8 = (bf16[32,2048]{1,0:T(8,128)(2,1)S(1)}, bf16[32,2048]{1,0:T(8,128)(2,1)S(1)}, u32[]{:S(2)}, u32[]{:S(2)}) collective-permute-start(bf16[32,2048]{1,0:T(8,128)(2,1)S(1)} %get-tuple-element.49), channel_id=1, source_target_pairs={{0,8},{8,0},{16,24},{24,16},{1,9},{9,1},{17,25},{25,17},{2,10},{10... | collective-permute-start | bytes 393224 | tf_op jit(solution)/shard_map/ppermute | solution.py:596
  32.0 1.3 %collective-permute-start.9 = (bf16[32,2048]{1,0:T(8,128)(2,1)S(1)}, bf16[32,2048]{1,0:T(8,128)(2,1)S(1)}, u32[]{:S(2)}, u32[]{:S(2)}) collective-permute-start(bf16[32,2048]{1,0:T(8,128)(2,1)S(1)} %get-tuple-element.50), channel_id=1, source_target_pairs={{0,8},{8,0},{16,24},{24,16},{1,9},{9,1},{17,25},{25,17},{2,10},{10... | collective-permute-start | bytes 393224 | tf_op jit(solution)/shard_map/ppermute | solution.py:596
